TPU v7x, 32 devices: a whole 2x2x4 slice. The times are simulated.
32 devices in a mesh: scene: 2 (over y), cell: 4 (over z), district: 4 (over x, core).
Axes of the slice: x: 2, y: 2, z: 4, core: 2. Of those that a mesh axis runs over, the one named last changes fastest.
Arguments:
- ray_geometry: float32 [6, 8192], P(None, ('scene', 'cell', 'district')), parts along dimension 1, may hold values from -5 to 5
- segment_length: float32 [8192, 4], P(('scene', 'cell', 'district')), parts along dimension 0, may hold values from 0.3 to 1
- jitter: float32 [8192, 128], P(('scene', 'cell', 'district')), parts along dimension 0, may hold values from 0 to 1
- appearance_codes: float32 [8192, 48], P(('scene', 'cell', 'district')), parts along dimension 0, may hold values from -5 to 5
- target: float32 [3, 8192], P(None, ('scene', 'cell', 'district')), parts along dimension 1, may hold values from 0 to 1
- crossing: int32 [8192, 4], P(('scene', 'cell', 'district')), parts along dimension 0, may hold values from 0 to 15, all different within a row; in each aligned block of 256 rows (0 to 255, 256 to 511, ...) at most 128 rows name the same one
- frequencies: float32 [3, 64], replicated, may hold values from -6 to 6
- cell_layers: bfloat16 [32, 2, 128, 128], P(('scene', 'cell', 'district')), parts along dimension 0, may hold values from -0.5 to 0.5
- district_prior: bfloat16 [8, 2, 128, 128], P(('scene', 'district')), parts along dimension 0, may hold values from -0.5 to 0.5
- head_weight: bfloat16 [32, 4, 128], P(('scene', 'cell', 'district')), parts along dimension 0, may hold values from -0.5 to 0.5
- appearance_weight: float32 [32, 3, 48], P(('scene', 'cell', 'district')), parts along dimension 0, may hold values from -0.875 to 0.875
Outputs:
- rendered: float32 [3, 8192], P(None, ('scene', 'cell', 'district')), parts along dimension 1
- grad_layers: float32 [32, 2, 128, 128], P(('scene', 'cell', 'district')), parts along dimension 0
- grad_prior: float32 [8, 2, 128, 128], P(('scene', 'district')), parts along dimension 0
- grad_head: float32 [32, 4, 128], P(('scene', 'cell', 'district')), parts along dimension 0
- grad_appearance: float32 [32, 3, 48], P(('scene', 'cell', 'district')), parts along dimension 0
- grad_codes: float32 [8192, 48], P(('scene', 'cell', 'district')), parts along dimension 0
There are 2 independent parts, one for each index of `scene`. A program takes and returns all parts, laid end to end along the dimension named above; an argument that names none is the same for every part. Nothing has to cross between parts.
Inputs may be any that keep to these rules, and one draw needn't show every extreme that they name: `crossing`: each ray names 4 different cells, in the order in which it crosses them. Among the 256 rays of one device no cell is named more than 128 times, and in every draw some device's rays name some cell exactly 128 times.
All inputs are finite; a program needn't handle non-finite values.
Results may differ from a plain program's by a relative error of at most 0.0098.
Values sent between devices are 32-bit elements; how exact they have to be, the bound alone decides.
No kernel may reach another device: no remote copies, remote signals or barrier semaphores. Data moves between devices by JAX's collectives and lax.ppermute only.
A program may use at most 192 MiB of HBM per device.

v0:
```python
import jax
import jax.numpy as jnp
from jax import lax
from jax.sharding import PartitionSpec as P

GEOMETRY = 8
HIGHEST_PRECISION = lax.Precision.HIGHEST


def build_front(ray_geometry, segment_length, jitter):
    ray_count, crossings = segment_length.shape
    samples = jitter.shape[1] // crossings
    near_depth = jnp.cumsum(segment_length, axis=1) - segment_length
    geometry = jnp.broadcast_to(ray_geometry.T[:, None, :], (ray_count, crossings, 6))
    front = jnp.concatenate(
        [
            geometry,
            near_depth[:, :, None],
            segment_length[:, :, None],
            jitter.reshape(ray_count, crossings, samples),
        ],
        axis=2,
    )
    return front.reshape(ray_count * crossings, front.shape[2])


def slot_positions(crossing, cell_total, capacity):
    target_cell = crossing.reshape(-1)
    total_rows = target_cell.shape[0]
    onehot = target_cell[:, None] == jnp.arange(cell_total, dtype=jnp.int32)[None, :]
    triangle = (
        lax.broadcasted_iota(jnp.int32, (total_rows, total_rows), 0)
        > lax.broadcasted_iota(jnp.int32, (total_rows, total_rows), 1)
    ).astype(jnp.bfloat16)
    earlier = jnp.dot(triangle, onehot.astype(jnp.bfloat16), preferred_element_type=jnp.float32)
    position = jnp.sum(jnp.where(onehot, earlier, 0.0), axis=1).astype(jnp.int32)
    return target_cell * capacity + position


def sample_spacing(payload, samples):
    near_depth = payload[:, 6:7]
    extent = payload[:, 7:8]
    offsets = jnp.arange(samples, dtype=jnp.float32)[None, :]
    depths = near_depth + extent * (offsets + payload[:, GEOMETRY : GEOMETRY + samples]) / samples
    ending = jnp.concatenate([depths[:, 1:], near_depth + extent], axis=1)
    return (depths, ending - depths)


def cell_forward(payload, frequencies, first_weight, second_weight, head_one, samples):
    depths, spacing = sample_spacing(payload, samples)
    phases = jnp.zeros((payload.shape[0], samples, frequencies.shape[1]), jnp.float32)
    for component in range(3):
        position = (
            payload[:, component : component + 1]
            + depths * payload[:, 3 + component : 4 + component]
        )
        phases = phases + position[:, :, None] * frequencies[component][None, None, :]
    encoded = jnp.concatenate([jnp.sin(phases), jnp.cos(phases)], axis=2)
    encoded = encoded.reshape(payload.shape[0] * samples, encoded.shape[2]).astype(jnp.bfloat16)
    first_act = jax.nn.relu(
        jnp.dot(encoded, first_weight, preferred_element_type=jnp.float32)
    ).astype(jnp.bfloat16)
    second_act = jax.nn.relu(
        jnp.dot(first_act, second_weight, preferred_element_type=jnp.float32)
    ).astype(jnp.bfloat16)
    raw_outputs = lax.dot_general(
        head_one, second_act, (((1,), (1,)), ((), ())), preferred_element_type=jnp.float32
    )
    return ((encoded, first_act, second_act, raw_outputs), spacing)


def shade(raw_outputs, payload, spacing, appearance_one, samples):
    slot_count = payload.shape[0]
    outputs = raw_outputs.reshape(4, slot_count, samples)
    code_part = payload[:, GEOMETRY + samples :]
    color_shift = jnp.dot(code_part, appearance_one.T, precision=HIGHEST_PRECISION)
    density = jax.nn.softplus(outputs[0])
    colors = jax.nn.sigmoid(outputs[1:] + color_shift.T[:, :, None])
    optical = density * spacing
    transmit = jnp.exp(-(jnp.cumsum(optical, axis=1) - optical))
    opacity = 1.0 - jnp.exp(-optical)
    blend_weight = transmit * opacity
    return (outputs, colors, optical, transmit, opacity, blend_weight, code_part)


def segment_partials(raw_outputs, payload, spacing, appearance_one, samples):
    shaded = shade(raw_outputs, payload, spacing, appearance_one, samples)
    colors, optical, blend_weight = (shaded[1], shaded[2], shaded[5])
    segment_color = jnp.sum(blend_weight[None] * colors, axis=2)
    segment_log = -jnp.sum(optical, axis=1)
    return jnp.concatenate([segment_color.T, segment_log[:, None]], axis=1)


def cell_backward(
    payload, saved_acts, spacing, cotangent, second_weight, head_one, appearance_one, samples
):
    encoded, first_act, second_act, raw_outputs = saved_acts
    outputs, colors, optical, transmit, opacity, blend_weight, code_part = shade(
        raw_outputs, payload, spacing, appearance_one, samples
    )
    color_grad = cotangent[:, :3].T
    log_grad = cotangent[:, 3]
    blend_grad = jnp.sum(color_grad[:, :, None] * colors, axis=0)
    colors_grad = color_grad[:, :, None] * blend_weight[None]
    transmit_grad = blend_grad * opacity
    optical_grad = blend_grad * transmit * (1.0 - opacity) - log_grad[:, None]
    before_grad = -transmit_grad * transmit
    later_sum = jnp.flip(jnp.cumsum(jnp.flip(before_grad, axis=1), axis=1), axis=1) - before_grad
    optical_grad = optical_grad + later_sum
    density_grad = optical_grad * spacing * jax.nn.sigmoid(outputs[0])
    logit_grad = colors_grad * colors * (1.0 - colors)
    slot_count = payload.shape[0]
    output_grad = (
        jnp.concatenate([density_grad[None], logit_grad], axis=0)
        .reshape(4, slot_count * samples)
        .astype(jnp.bfloat16)
    )
    head_grad = jnp.dot(output_grad, second_act, preferred_element_type=jnp.float32)
    shift_grad = jnp.sum(logit_grad, axis=2)
    second_grad = lax.dot_general(
        output_grad, head_one, (((0,), (0,)), ((), ())), preferred_element_type=jnp.float32
    )
    second_grad = jnp.where(second_act > 0, second_grad, 0.0).astype(jnp.bfloat16)
    second_weight_grad = lax.dot_general(
        first_act, second_grad, (((0,), (0,)), ((), ())), preferred_element_type=jnp.float32
    )
    first_grad = lax.dot_general(
        second_grad, second_weight, (((1,), (1,)), ((), ())), preferred_element_type=jnp.float32
    )
    first_grad = jnp.where(first_act > 0, first_grad, 0.0).astype(jnp.bfloat16)
    first_weight_grad = lax.dot_general(
        encoded, first_grad, (((0,), (0,)), ((), ())), preferred_element_type=jnp.float32
    )
    return (first_weight_grad, second_weight_grad, head_grad, shift_grad, code_part)


def composite(gathered, target):
    segment_color = gathered[:, :, :3]
    segment_log = gathered[:, :, 3]
    reach_weight = jnp.exp(jnp.cumsum(segment_log, axis=1) - segment_log)
    rendered = jnp.sum(reach_weight[:, :, None] * segment_color, axis=1).T
    residual = rendered - target
    color_grad = reach_weight[:, :, None] * residual.T[:, None, :]
    reach_grad = jnp.sum(residual.T[:, None, :] * segment_color, axis=2) * reach_weight
    log_grad = jnp.flip(jnp.cumsum(jnp.flip(reach_grad, axis=1), axis=1), axis=1) - reach_grad
    return (rendered, jnp.concatenate([color_grad, log_grad[:, :, None]], axis=2))


def local(
    ray_geometry,
    segment_length,
    jitter,
    appearance_codes,
    target,
    crossing,
    frequencies,
    cell_layers,
    district_prior,
    head_weight,
    appearance_weight,
):
    num_cell = lax.axis_size("cell")
    num_district = lax.axis_size("district")
    cell_total = num_cell * num_district
    ray_count, crossings = crossing.shape
    samples = jitter.shape[1] // crossings
    segments = ray_count * crossings
    capacity = 2 * segments // cell_total
    slot_total = cell_total * capacity
    code_width = appearance_codes.shape[1]
    front = build_front(ray_geometry, segment_length, jitter)
    codes_seg = jnp.broadcast_to(
        appearance_codes[:, None, :], (ray_count, crossings, code_width)
    ).reshape(segments, code_width)
    payload = jnp.concatenate([front, codes_seg], axis=1)
    appearance_one = appearance_weight[0]
    row_width = payload.shape[1]
    places = slot_positions(crossing, cell_total, capacity)
    outbox = (
        jnp.zeros((slot_total, row_width), jnp.float32)
        .at[places]
        .set(payload)
        .reshape(cell_total, capacity * row_width)
    )
    arrived = lax.all_to_all(outbox, ("cell", "district"), split_axis=0, concat_axis=0, tiled=True)
    arrived = arrived.reshape(slot_total, row_width)
    effective = (cell_layers[0].astype(jnp.float32) + district_prior[0].astype(jnp.float32)).astype(
        jnp.bfloat16
    )
    head_one = head_weight[0]
    block_rows = min(512, slot_total)
    blocked = arrived.reshape(slot_total // block_rows, block_rows, row_width)

    def forward_keep(slot_rows):
        saved_acts, spacing = cell_forward(
            slot_rows, frequencies, effective[0], effective[1], head_one, samples
        )
        return (
            segment_partials(saved_acts[3], slot_rows, spacing, appearance_one, samples),
            saved_acts,
        )

    partials, stored = lax.map(forward_keep, blocked)
    partials = partials.reshape(cell_total, capacity * 4)
    returned = lax.all_to_all(
        partials, ("cell", "district"), split_axis=0, concat_axis=0, tiled=True
    )
    returned = returned.reshape(slot_total, 4)
    rendered, cotangent = composite(returned[places].reshape(ray_count, crossings, 4), target)
    grad_box = (
        jnp.zeros((slot_total, 4), jnp.float32)
        .at[places]
        .set(cotangent.reshape(segments, 4))
        .reshape(cell_total, capacity * 4)
    )
    incoming = lax.all_to_all(
        grad_box, ("cell", "district"), split_axis=0, concat_axis=0, tiled=True
    )
    incoming = incoming.reshape(slot_total // block_rows, block_rows, 4)

    def finish(result):
        first_part, second_part, head_part, shift_grad, code_part = result
        appearance_part = jnp.dot(shift_grad, code_part, precision=HIGHEST_PRECISION)
        code_part_grad = jnp.dot(shift_grad.T, appearance_one, precision=HIGHEST_PRECISION)
        return (first_part, second_part, head_part, appearance_part, code_part_grad)

    def backward_keep(bundle):
        slot_rows, incoming_rows, saved_acts = bundle
        spacing = sample_spacing(slot_rows, samples)[1]
        return finish(
            cell_backward(
                slot_rows,
                saved_acts,
                spacing,
                incoming_rows,
                effective[1],
                head_one,
                appearance_one,
                samples,
            )
        )

    pieces = lax.map(backward_keep, (blocked, incoming, stored))
    first_w = jnp.sum(pieces[0], axis=0)
    second_w = jnp.sum(pieces[1], axis=0)
    head_grad = jnp.sum(pieces[2], axis=0)
    appearance_grad = jnp.sum(pieces[3], axis=0)
    code_box = pieces[4].reshape(cell_total, capacity * code_width)
    code_back = lax.all_to_all(
        code_box, ("cell", "district"), split_axis=0, concat_axis=0, tiled=True
    )
    code_back = code_back.reshape(slot_total, code_width)
    grad_codes = jnp.sum(code_back[places].reshape(ray_count, crossings, code_width), axis=1)
    grad_pair = jnp.stack([first_w, second_w], axis=0)
    grad_prior = lax.psum(grad_pair, "cell") / num_cell
    return (
        rendered,
        grad_pair[None],
        grad_prior[None],
        head_grad[None],
        appearance_grad[None],
        grad_codes,
    )


def solution(mesh):
    placed = (
        P(None, ("scene", "cell", "district")),
        P(("scene", "cell", "district"), None),
        P(("scene", "cell", "district"), None),
        P(("scene", "cell", "district"), None),
        P(None, ("scene", "cell", "district")),
        P(("scene", "cell", "district"), None),
        P(),
        P(("scene", "cell", "district"), None, None, None),
        P(("scene", "district"), None, None, None),
        P(("scene", "cell", "district"), None, None),
        P(("scene", "cell", "district"), None, None),
    )
    return jax.shard_map(
        local,
        mesh=mesh,
        in_specs=placed,
        out_specs=(
            P(None, ("scene", "cell", "district")),
            P(("scene", "cell", "district"), None, None, None),
            P(("scene", "district"), None, None, None),
            P(("scene", "cell", "district"), None, None),
            P(("scene", "cell", "district"), None, None),
            P(("scene", "cell", "district"), None),
        ),
        check_vma=False,
    )
```

profile of v0, /device:TPU:0, one launch (start us, length us, event | category | flops | bytes accessed | tf_op | source)
XLA Modules:
  0.0 494.3 jit_solution(12857817853743791660)
XLA Ops:
  22.3 7.5 %all-to-all-start = ((f32[16,1,11264]{2,1,0:T(1,128)}), f32[16,1,11264]{2,1,0:T(1,128)S(1)}, u32[]{:S(2)}, u32[]{:S(2)}) async-start(f32[16,1,11264]{2,1,0:T(1,128)} %all_to_all.32), calls=%async_computation | async-start | bytes 1441792 | tf_op jit(solution)/shard_map/all_to_all | solution.py:185
  29.9 17.5 %all-to-all-done = f32[16,1,11264]{2,1,0:T(1,128)S(1)} async-done(((f32[16,1,11264]{2,1,0:T(1,128)}), f32[16,1,11264]{2,1,0:T(1,128)S(1)}, u32[]{:S(2)}, u32[]{:S(2)}) %all-to-all-start) | async-done | bytes 720928 | tf_op jit(solution)/shard_map/all_to_all | solution.py:185
  50.6 207.9 %while.36 = (s32[]{:T(128)}, f32[4,512,4]{1,2,0:T(4,128)S(1)}, bf16[4,16384,128]{2,1,0:T(8,128)(2,1)}, bf16[4,16384,128]{2,1,0:T(8,128)(2,1)}, bf16[4,16384,128]...) while((s32[]{:T(128)}, f32[4,512,4]{1,2,0:T(4,128)S(1)}, ...), condition=%wide.region_7.8_spmd, body=%wide.region_3.7_spmd.sunk | while | flops 1125123072 | bytes 59342216 | solution.py:203
  51.5 33.3 %fusion.135 = (bf16[1,16384,64]{2,1,0:T(8,128)(2,1)}, bf16[1,16384,64]{2,1,0:T(8,128)(2,1)}, bf16[16384,64]{1,0:T(8,128)(2,1)S(1)}, bf16[16384,64]{1,0:T(8,128)(2,1)S(1)}) fusion(f32[64]{0:T(128)S(1)} %get-tuple-element.521, f32[16384]{0:T(1024)S(1)} %mul.495, f32[64]{0:T(128)S(1)} %get-tuple-element.527, f32[16384]{0:T(1024)S(1)} %mul.496, ...), kind=kLoop, calls=%fused_computation.45.clone.1 | loop fusion | flops 7340032 | bytes 8585984 | tf_op jit(solution)/shard_map/while/body/eval_jaxpr/concatenate | solution.py:58
  84.8 4.2 bitcast_dynamic-update-slice_fusion.6
  96.7 5.9 %maximum_dynamic-update-slice_fusion.2 = bf16[4,16384,128]{2,1,0:T(8,128)(2,1)} fusion(bf16[4,16384,128]{2,1,0:T(8,128)(2,1)} %get-tuple-element.580, s32[]{:T(128)} %get-tuple-element.578, bf16[1,16384,64]{2,1,0:T(8,128)(2,1)} %get-tuple-element.538, bf16[1,16384,64]{2,1,0:T(8,128)(2,1)} %get-tuple-element.539), kind=kLoop, calls=%fused_computation.14.clone.1 | loop fusion | flops 8388608 | bytes 12583424 | tf_op jit(solution)/shard_map/while/body/jit(dynamic_update_index_in_dim)/dynamic_update_slice | solution.py:203
  103.5 33.3 %fusion.135 = (bf16[1,16384,64]{2,1,0:T(8,128)(2,1)}, bf16[1,16384,64]{2,1,0:T(8,128)(2,1)}, bf16[16384,64]{1,0:T(8,128)(2,1)S(1)}, bf16[16384,64]{1,0:T(8,128)(2,1)S(1)}) fusion(f32[64]{0:T(128)S(1)} %get-tuple-element.521, f32[16384]{0:T(1024)S(1)} %mul.495, f32[64]{0:T(128)S(1)} %get-tuple-element.527, f32[16384]{0:T(1024)S(1)} %mul.496, ...), kind=kLoop, calls=%fused_computation.45.clone.1 | loop fusion | flops 7340032 | bytes 8585984 | tf_op jit(solution)/shard_map/while/body/eval_jaxpr/concatenate | solution.py:58
  136.8 4.3 bitcast_dynamic-update-slice_fusion.6
  148.6 6.0 %maximum_dynamic-update-slice_fusion.2 = bf16[4,16384,128]{2,1,0:T(8,128)(2,1)} fusion(bf16[4,16384,128]{2,1,0:T(8,128)(2,1)} %get-tuple-element.580, s32[]{:T(128)} %get-tuple-element.578, bf16[1,16384,64]{2,1,0:T(8,128)(2,1)} %get-tuple-element.538, bf16[1,16384,64]{2,1,0:T(8,128)(2,1)} %get-tuple-element.539), kind=kLoop, calls=%fused_computation.14.clone.1 | loop fusion | flops 8388608 | bytes 12583424 | tf_op jit(solution)/shard_map/while/body/jit(dynamic_update_index_in_dim)/dynamic_update_slice | solution.py:203
  155.5 33.3 %fusion.135 = (bf16[1,16384,64]{2,1,0:T(8,128)(2,1)}, bf16[1,16384,64]{2,1,0:T(8,128)(2,1)}, bf16[16384,64]{1,0:T(8,128)(2,1)S(1)}, bf16[16384,64]{1,0:T(8,128)(2,1)S(1)}) fusion(f32[64]{0:T(128)S(1)} %get-tuple-element.521, f32[16384]{0:T(1024)S(1)} %mul.495, f32[64]{0:T(128)S(1)} %get-tuple-element.527, f32[16384]{0:T(1024)S(1)} %mul.496, ...), kind=kLoop, calls=%fused_computation.45.clone.1 | loop fusion | flops 7340032 | bytes 8585984 | tf_op jit(solution)/shard_map/while/body/eval_jaxpr/concatenate | solution.py:58
  188.7 4.2 bitcast_dynamic-update-slice_fusion.6
  200.5 5.9 %maximum_dynamic-update-slice_fusion.2 = bf16[4,16384,128]{2,1,0:T(8,128)(2,1)} fusion(bf16[4,16384,128]{2,1,0:T(8,128)(2,1)} %get-tuple-element.580, s32[]{:T(128)} %get-tuple-element.578, bf16[1,16384,64]{2,1,0:T(8,128)(2,1)} %get-tuple-element.538, bf16[1,16384,64]{2,1,0:T(8,128)(2,1)} %get-tuple-element.539), kind=kLoop, calls=%fused_computation.14.clone.1 | loop fusion | flops 8388608 | bytes 12583424 | tf_op jit(solution)/shard_map/while/body/jit(dynamic_update_index_in_dim)/dynamic_update_slice | solution.py:203
  207.3 33.3 %fusion.135 = (bf16[1,16384,64]{2,1,0:T(8,128)(2,1)}, bf16[1,16384,64]{2,1,0:T(8,128)(2,1)}, bf16[16384,64]{1,0:T(8,128)(2,1)S(1)}, bf16[16384,64]{1,0:T(8,128)(2,1)S(1)}) fusion(f32[64]{0:T(128)S(1)} %get-tuple-element.521, f32[16384]{0:T(1024)S(1)} %mul.495, f32[64]{0:T(128)S(1)} %get-tuple-element.527, f32[16384]{0:T(1024)S(1)} %mul.496, ...), kind=kLoop, calls=%fused_computation.45.clone.1 | loop fusion | flops 7340032 | bytes 8585984 | tf_op jit(solution)/shard_map/while/body/eval_jaxpr/concatenate | solution.py:58
  240.6 4.2 bitcast_dynamic-update-slice_fusion.6
  252.4 6.0 %maximum_dynamic-update-slice_fusion.2 = bf16[4,16384,128]{2,1,0:T(8,128)(2,1)} fusion(bf16[4,16384,128]{2,1,0:T(8,128)(2,1)} %get-tuple-element.580, s32[]{:T(128)} %get-tuple-element.578, bf16[1,16384,64]{2,1,0:T(8,128)(2,1)} %get-tuple-element.538, bf16[1,16384,64]{2,1,0:T(8,128)(2,1)} %get-tuple-element.539), kind=kLoop, calls=%fused_computation.14.clone.1 | loop fusion | flops 8388608 | bytes 12583424 | tf_op jit(solution)/shard_map/while/body/jit(dynamic_update_index_in_dim)/dynamic_update_slice | solution.py:203
  260.3 5.1 %all-to-all-start.1 = ((f32[16,1,512]{2,1,0:T(1,128)}), f32[16,1,512]{2,1,0:T(1,128)S(1)}, u32[]{:S(2)}, u32[]{:S(2)}) async-start(f32[16,1,512]{2,1,0:T(1,128)} %all_to_all.33), calls=%async_computation.1 | async-start | bytes 65536 | tf_op jit(solution)/shard_map/all_to_all | solution.py:205
  265.6 6.5 %all-to-all-done.1 = f32[16,1,512]{2,1,0:T(1,128)S(1)} async-done(((f32[16,1,512]{2,1,0:T(1,128)}), f32[16,1,512]{2,1,0:T(1,128)S(1)}, u32[]{:S(2)}, u32[]{:S(2)}) %all-to-all-start.1) | async-done | bytes 32800 | tf_op jit(solution)/shard_map/all_to_all | solution.py:205
  289.6 6.5 %all-to-all-done.2 = f32[16,1,512]{2,1,0:T(1,128)S(1)} async-done(((f32[16,1,512]{2,1,0:T(1,128)}), f32[16,1,512]{2,1,0:T(1,128)S(1)}, u32[]{:S(2)}, u32[]{:S(2)}) %all-to-all-start.2) | async-done | bytes 32800 | tf_op jit(solution)/shard_map/all_to_all | solution.py:216
  298.2 135.9 %while.37 = (s32[]{:T(128)}, f32[4,128,128]{2,1,0:T(8,128)}, f32[4,128,128]{2,1,0:T(8,128)}, f32[4,4,128]{2,1,0:T(4,128)}, f32[4,3,48]{2,1,0:T(4,128)}, /*index=...) while((s32[]{:T(128)}, f32[4,128,128]{2,1,0:T(8,128)}, ...), condition=%wide.region_18.19_spmd, body=%wide.region_13.18_spmd.sunk | while | flops 1662925824 | bytes 59325544 | solution.py:243
  321.8 7.8 %fusion.155 = f32[4,128,128]{2,1,0:T(8,128)} fusion(f32[4,128,128]{2,1,0:T(8,128)} %get-tuple-element.624, s32[]{:T(128)} %get-tuple-element.623, bf16[16384,128]{1,0:T(8,128)(2,1)} %copy-done, bf16[4,16384,128]{2,1,0:T(8,128)(2,1)} %get-tuple-element.649, bf16[4,16384,128]{2,1,0:T(8,128)(2,1)} %get-tuple-element.648, ...), kind=kOutput, calls=%fused_computation.63.clone.1 | convolution fusion | flops 1080033280 | bytes 12682752 | tf_op jit(solution)/shard_map/while/body/eval_jaxpr/dot_general | solution.py:131
  355.7 7.8 %fusion.155 = f32[4,128,128]{2,1,0:T(8,128)} fusion(f32[4,128,128]{2,1,0:T(8,128)} %get-tuple-element.624, s32[]{:T(128)} %get-tuple-element.623, bf16[16384,128]{1,0:T(8,128)(2,1)} %copy-done, bf16[4,16384,128]{2,1,0:T(8,128)(2,1)} %get-tuple-element.649, bf16[4,16384,128]{2,1,0:T(8,128)(2,1)} %get-tuple-element.648, ...), kind=kOutput, calls=%fused_computation.63.clone.1 | convolution fusion | flops 1080033280 | bytes 12682752 | tf_op jit(solution)/shard_map/while/body/eval_jaxpr/dot_general | solution.py:131
  389.5 7.8 %fusion.155 = f32[4,128,128]{2,1,0:T(8,128)} fusion(f32[4,128,128]{2,1,0:T(8,128)} %get-tuple-element.624, s32[]{:T(128)} %get-tuple-element.623, bf16[16384,128]{1,0:T(8,128)(2,1)} %copy-done, bf16[4,16384,128]{2,1,0:T(8,128)(2,1)} %get-tuple-element.649, bf16[4,16384,128]{2,1,0:T(8,128)(2,1)} %get-tuple-element.648, ...), kind=kOutput, calls=%fused_computation.63.clone.1 | convolution fusion | flops 1080033280 | bytes 12682752 | tf_op jit(solution)/shard_map/while/body/eval_jaxpr/dot_general | solution.py:131
  423.4 7.8 %fusion.155 = f32[4,128,128]{2,1,0:T(8,128)} fusion(f32[4,128,128]{2,1,0:T(8,128)} %get-tuple-element.624, s32[]{:T(128)} %get-tuple-element.623, bf16[16384,128]{1,0:T(8,128)(2,1)} %copy-done, bf16[4,16384,128]{2,1,0:T(8,128)(2,1)} %get-tuple-element.649, bf16[4,16384,128]{2,1,0:T(8,128)(2,1)} %get-tuple-element.648, ...), kind=kOutput, calls=%fused_computation.63.clone.1 | convolution fusion | flops 1080033280 | bytes 12682752 | tf_op jit(solution)/shard_map/while/body/eval_jaxpr/dot_general | solution.py:131
  447.6 32.0 %all-reduce.2.cloned.1.call-done = f32[2,128,128]{2,1,0:T(8,128)} async-done(((f32[2,128,128]{2,1,0:T(8,128)}), f32[2,128,128]{2,1,0:T(8,128)}) %all-reduce.2.cloned.1.call-update) | async-done | bytes 131088 | tf_op jit(solution)/shard_map/psum | solution.py:255
  (469 shorter events, 196.5 us)
Async XLA Ops:
  7.2 22.7 %copy-start.18 = (f32[1,3,48]{2,0,1:T(1,128)S(1)}, f32[1,3,48]{2,0,1:T(1,128)}, u32[]{:S(2)}) copy-start(f32[1,3,48]{2,0,1:T(1,128)} %param.25) | copy-start | bytes 1732
  7.2 22.7 %copy-start.14 = (bf16[1,2,128,128]{3,2,1,0:T(8,128)(2,1)S(1)}, bf16[1,2,128,128]{3,2,1,0:T(8,128)(2,1)}, u32[]{:S(2)}) copy-start(bf16[1,2,128,128]{3,2,1,0:T(8,128)(2,1)} %param.22) | copy-start | bytes 196612
  7.2 22.7 %copy-start.13 = (bf16[1,2,128,128]{3,2,1,0:T(8,128)(2,1)S(1)}, bf16[1,2,128,128]{3,2,1,0:T(8,128)(2,1)}, u32[]{:S(2)}) copy-start(bf16[1,2,128,128]{3,2,1,0:T(8,128)(2,1)} %param.23) | copy-start | bytes 196612
  9.4 41.2 %copy-start.16 = (f32[3,64]{1,0:T(4,128)S(1)}, f32[3,64]{1,0:T(4,128)}, u32[]{:S(2)}) copy-start(f32[3,64]{1,0:T(4,128)} %param.21) | copy-start | bytes 2308
  22.3 25.2 %all-to-all-start = ((f32[16,1,11264]{2,1,0:T(1,128)}), f32[16,1,11264]{2,1,0:T(1,128)S(1)}, u32[]{:S(2)}, u32[]{:S(2)}) async-start(f32[16,1,11264]{2,1,0:T(1,128)} %all_to_all.32), calls=%async_computation | async-start | bytes 1441792 | tf_op jit(solution)/shard_map/all_to_all | solution.py:185
  50.6 214.8 %copy-start.17 = (f32[3,256]{1,0:T(4,128)S(1)}, f32[3,256]{1,0:T(4,128)}, u32[]{:S(2)}) copy-start(f32[3,256]{1,0:T(4,128)} %param.19) | copy-start | bytes 9220
  260.3 11.8 %all-to-all-start.1 = ((f32[16,1,512]{2,1,0:T(1,128)}), f32[16,1,512]{2,1,0:T(1,128)S(1)}, u32[]{:S(2)}, u32[]{:S(2)}) async-start(f32[16,1,512]{2,1,0:T(1,128)} %all_to_all.33), calls=%async_computation.1 | async-start | bytes 65536 | tf_op jit(solution)/shard_map/all_to_all | solution.py:205
  265.4 31.8 %copy-start.15 = (s32[1024]{0:T(1024)}, s32[1024]{0:T(1024)S(1)}, u32[]{:S(2)}) copy-start(s32[1024]{0:T(1024)S(1)} %broadcast_clamp_fusion) | copy-start | bytes 12292
  286.0 10.1 %all-to-all-start.2 = ((f32[16,1,512]{2,1,0:T(1,128)}), f32[16,1,512]{2,1,0:T(1,128)S(1)}, u32[]{:S(2)}, u32[]{:S(2)}) async-start(f32[16,1,512]{2,1,0:T(1,128)} %all_to_all.34), calls=%async_computation.2 | async-start | bytes 65536 | tf_op jit(solution)/shard_map/all_to_all | solution.py:216
  311.5 10.3 %copy-start.9 = (bf16[2,128,128]{2,1,0:T(8,128)(2,1)S(1)}, bf16[2,128,128]{2,1,0:T(8,128)(2,1)}, u32[]{:S(2)}) copy-start(bf16[2,128,128]{2,1,0:T(8,128)(2,1)} %copy-done.8) | copy-start | bytes 196612 | tf_op jit(solution)/shard_map/while
  321.8 8.1 %copy-start.4 = (f32[3,512]{1,0:T(4,128)S(1)}, f32[3,512]{1,0:T(4,128)}, u32[]{:S(2)}) copy-start(f32[3,512]{1,0:T(4,128)} %copy-done.3) | copy-start | bytes 18436 | tf_op jit(solution)/shard_map/while
  321.8 8.8 %copy-start.11 = (f32[3,48]{1,0:T(4,128)S(1)}, f32[3,48]{1,0:T(4,128)}, u32[]{:S(2)}) copy-start(f32[3,48]{1,0:T(4,128)} %copy-done.10) | copy-start | bytes 1732 | tf_op jit(solution)/shard_map/while
  345.4 10.3 %copy-start.9 = (bf16[2,128,128]{2,1,0:T(8,128)(2,1)S(1)}, bf16[2,128,128]{2,1,0:T(8,128)(2,1)}, u32[]{:S(2)}) copy-start(bf16[2,128,128]{2,1,0:T(8,128)(2,1)} %copy-done.8) | copy-start | bytes 196612 | tf_op jit(solution)/shard_map/while
  355.7 8.1 %copy-start.4 = (f32[3,512]{1,0:T(4,128)S(1)}, f32[3,512]{1,0:T(4,128)}, u32[]{:S(2)}) copy-start(f32[3,512]{1,0:T(4,128)} %copy-done.3) | copy-start | bytes 18436 | tf_op jit(solution)/shard_map/while
  355.7 8.8 %copy-start.11 = (f32[3,48]{1,0:T(4,128)S(1)}, f32[3,48]{1,0:T(4,128)}, u32[]{:S(2)}) copy-start(f32[3,48]{1,0:T(4,128)} %copy-done.10) | copy-start | bytes 1732 | tf_op jit(solution)/shard_map/while
  379.2 10.3 %copy-start.9 = (bf16[2,128,128]{2,1,0:T(8,128)(2,1)S(1)}, bf16[2,128,128]{2,1,0:T(8,128)(2,1)}, u32[]{:S(2)}) copy-start(bf16[2,128,128]{2,1,0:T(8,128)(2,1)} %copy-done.8) | copy-start | bytes 196612 | tf_op jit(solution)/shard_map/while
  389.5 8.1 %copy-start.4 = (f32[3,512]{1,0:T(4,128)S(1)}, f32[3,512]{1,0:T(4,128)}, u32[]{:S(2)}) copy-start(f32[3,512]{1,0:T(4,128)} %copy-done.3) | copy-start | bytes 18436 | tf_op jit(solution)/shard_map/while
  389.5 8.8 %copy-start.11 = (f32[3,48]{1,0:T(4,128)S(1)}, f32[3,48]{1,0:T(4,128)}, u32[]{:S(2)}) copy-start(f32[3,48]{1,0:T(4,128)} %copy-done.10) | copy-start | bytes 1732 | tf_op jit(solution)/shard_map/while
  413.1 10.3 %copy-start.9 = (bf16[2,128,128]{2,1,0:T(8,128)(2,1)S(1)}, bf16[2,128,128]{2,1,0:T(8,128)(2,1)}, u32[]{:S(2)}) copy-start(bf16[2,128,128]{2,1,0:T(8,128)(2,1)} %copy-done.8) | copy-start | bytes 196612 | tf_op jit(solution)/shard_map/while
  423.4 8.1 %copy-start.2 = (f32[3,512]{1,0:T(4,128)S(1)}, f32[3,512]{1,0:T(4,128)}, u32[]{:S(2)}) copy-start(f32[3,512]{1,0:T(4,128)} %copy-done.1) | copy-start | bytes 18436 | tf_op jit(solution)/shard_map/while
  423.4 8.1 %copy-start.4 = (f32[3,512]{1,0:T(4,128)S(1)}, f32[3,512]{1,0:T(4,128)}, u32[]{:S(2)}) copy-start(f32[3,512]{1,0:T(4,128)} %copy-done.3) | copy-start | bytes 18436 | tf_op jit(solution)/shard_map/while
  423.4 8.8 %copy-start.11 = (f32[3,48]{1,0:T(4,128)S(1)}, f32[3,48]{1,0:T(4,128)}, u32[]{:S(2)}) copy-start(f32[3,48]{1,0:T(4,128)} %copy-done.10) | copy-start | bytes 1732 | tf_op jit(solution)/shard_map/while
  437.2 44.1 %all-to-all-start.3 = ((f32[16,1,6144]{2,1,0:T(1,128)}), f32[16,1,6144]{2,1,0:T(1,128)S(1)}, u32[]{:S(2)}, u32[]{:S(2)}) async-start(f32[16,1,6144]{2,1,0:T(1,128)} %all_to_all.35), calls=%async_computation.3 | async-start | bytes 786432 | tf_op jit(solution)/shard_map/all_to_all | solution.py:249
  440.8 38.9 %all-reduce.2.cloned.1.call-start = ((), (), s32[]{:S(2)}) async-start(), calls=%async_computation.4 | async-start | bytes 262144 | tf_op jit(solution)/shard_map/psum | solution.py:255
  (36 other events, 90.8 us)
Sparse Core Ops, SparseCore 0:
  443.9 35.7 all-reduce.1
where the time goes:
time: 501 us; the launch traced here: 494 us
  other arithmetic  188 us (38%)
  matrix products  127 us (25%)
  local copies, waits for them, and re-layouts  80.1 us (16%)
  waiting for transfers between devices  62.6 us (12%)
  starting transfers between devices  19.8 us (4%)
  between operations  15.1 us (3%)
    concatenate x4, other arithmetic, cell_forward(): encoded = jnp.concatenate([jnp.sin(phases), jnp.cos(phases)], axis=2)  133 us
    psum x1, waiting for transfers between devices, local(): grad_prior = lax.psum(grad_pair, 'cell') / num_cell  32 us
    dot_general x4, matrix products, cell_backward(): lax.dot_general(encoded, first_grad, (((0,), (0,)), ((), ())), preferred_...  31.2 us
    dynamic_update_slice x8, other arithmetic, local(): partials, stored = lax.map(forward_keep, blocked)  23.9 us
    all_to_all x1, waiting for transfers between devices, local(): lax.all_to_all(outbox, ('cell', 'district'), split_axis=0, concat_axis=0,...  17.5 us
    dot_general x4, matrix products, cell_forward(): jnp.dot(encoded, first_weight, preferred_element_type=jnp.float32)  16.9 us
    dot_general x4, matrix products, cell_backward(): lax.dot_general(output_grad, head_one, (((0,), (0,)), ((), ())), preferre...  16.6 us
    dot_general x4, matrix products, cell_backward(): lax.dot_general(first_act, second_grad, (((0,), (0,)), ((), ())), preferr...  16.4 us
  transfers between devices with their start and end apart: 5, of which 4 were waited for; matrix products, arithmetic and copies ran while one was open for 2% of the time, Pallas kernels for 0%

commit v1 on v0

--- a/solution.py
+++ b/solution.py
@@ -1,6 +1,10 @@
+import functools
+
 import jax
 import jax.numpy as jnp
 from jax import lax
+from jax.experimental import pallas as pl
+from jax.experimental.pallas import tpu as pltpu
 from jax.sharding import PartitionSpec as P
 
 GEOMETRY = 8
@@ -146,7 +150,7 @@
     return (rendered, jnp.concatenate([color_grad, log_grad[:, :, None]], axis=2))
 
 
-def local(
+def routed(
     ray_geometry,
     segment_length,
     jitter,
@@ -263,6 +267,564 @@
     )
 
 
+TILE = 8
+UNROLL = 4
+ROWS = 264
+HEAD_ROW = 256
+APP_ROW = 260
+VMEM_LIMIT = 56 * 1024 * 1024
+COS = (
+    0.9999992251396179,
+    -19.738981246948242,
+    64.92865753173828,
+    -85.27162170410156,
+    58.79049301147461,
+    -21.07110595703125,
+)
+F32 = jnp.float32
+BF16 = jnp.bfloat16
+
+
+def iota(shape, axis):
+    return lax.broadcasted_iota(jnp.int32, shape, axis)
+
+
+def dot_nn(a, b):
+    return jnp.dot(a, b, preferred_element_type=F32)
+
+
+def dot_nt(a, b):
+    return lax.dot_general(a, b, (((1,), (1,)), ((), ())), preferred_element_type=F32)
+
+
+def split3(x):
+    high = x.astype(BF16)
+    rest = x - high.astype(F32)
+    mid = rest.astype(BF16)
+    low = (rest - mid.astype(F32)).astype(BF16)
+    return high, mid, low
+
+
+def pick_nn(x, select):
+    high, mid, low = split3(x)
+    return (dot_nn(low, select) + dot_nn(mid, select)) + dot_nn(high, select)
+
+
+def pick_nt(select, x):
+    high, mid, low = split3(x)
+    return (dot_nt(select, low) + dot_nt(select, mid)) + dot_nt(select, high)
+
+
+def exact_nn(a, b):
+    return jnp.dot(a, b, precision=HIGHEST_PRECISION, preferred_element_type=F32)
+
+
+def put_channel(ref, c, x):
+    for h in range(ref.shape[0]):
+        ref[h, pl.ds(c, x.shape[0], 8), :] = x[:, 128 * h : 128 * (h + 1)]
+
+
+def get_channel(ref, c):
+    tiles = ref.shape[1] // 8
+    return jnp.concatenate([ref[h, pl.ds(c, tiles, 8), :] for h in range(ref.shape[0])], axis=1)
+
+
+def get_tile(ref, t):
+    rows = pl.ds(pl.multiple_of(t * 8, 8), 8)
+    return jnp.concatenate([ref[h, rows, :] for h in range(ref.shape[0])], axis=1)
+
+
+def put_tile(ref, t, x):
+    rows = pl.ds(pl.multiple_of(t * 8, 8), 8)
+    for h in range(ref.shape[0]):
+        ref[h, rows, :] = x[:, 128 * h : 128 * (h + 1)]
+
+
+def pack_kernel(layers_ref, prior_ref, head_ref, app_ref, out_ref):
+    for layer in range(2):
+        both = layers_ref[0, layer].astype(F32) + prior_ref[0, layer].astype(F32)
+        out_ref[128 * layer : 128 * (layer + 1), :] = both.T
+    out_ref[HEAD_ROW:ROWS, :] = jnp.zeros((ROWS - HEAD_ROW, 128), F32)
+    out_ref[HEAD_ROW : HEAD_ROW + 4, :] = head_ref[0].astype(F32)
+    out_ref[APP_ROW : APP_ROW + 3, 0 : app_ref.shape[2]] = app_ref[0]
+
+
+def slot_mask(place_row):
+    return (iota((TILE, place_row.shape[1]), 0) == place_row.astype(jnp.int32)).astype(F32)
+
+
+def tile_onehot(tile_row, tiles):
+    return (iota((tiles, tile_row.shape[1]), 0) == tile_row.astype(jnp.int32)).astype(F32).astype(BF16)
+
+
+def cell_onehot(cells_ref, cells):
+    return [
+        (iota((cells, cells_ref.shape[1]), 0) == cells_ref[k : k + 1, :]).astype(F32)
+        for k in range(cells_ref.shape[0])
+    ]
+
+
+def lane_select(channels, lanes):
+    rows = channels * TILE
+    row, column = iota((rows, channels * lanes), 0), iota((rows, channels * lanes), 1)
+    same = (row // TILE == column // lanes) & (row % TILE == column % TILE)
+    return same.astype(F32).astype(BF16)
+
+
+def encode_kernel(
+    cells,
+    samples,
+    cells_ref,
+    geometry_ref,
+    length_ref,
+    jitter_ref,
+    frequency_ref,
+    encoded_ref,
+    meta_ref,
+    spacing_ref,
+    tile_cell_ref,
+    tile_start_ref,
+    position_ref,
+    factor_ref,
+):
+    tiles = spacing_ref.shape[0]
+    lanes = TILE * samples
+    crossings, rays = cells_ref.shape
+    segments = crossings * rays
+
+    @pl.when(pl.program_id(0) == 0)
+    def _():
+        onehot = jnp.concatenate(cell_onehot(cells_ref, cells), axis=1)
+        chunks = [onehot[:, 128 * c : 128 * (c + 1)] for c in range(segments // 128)]
+        before = (iota((128, 128), 0) < iota((128, 128), 1)).astype(F32).astype(BF16)
+        prefix = dot_nn(jnp.concatenate(chunks, axis=0).astype(BF16), before)
+        running = jnp.zeros((cells, 1), F32)
+        ranks = []
+        for c, chunk in enumerate(chunks):
+            earlier = prefix[cells * c : cells * (c + 1), :] + running
+            ranks.append(jnp.sum(chunk * earlier, axis=0, keepdims=True))
+            running = running + jnp.sum(chunk, axis=1, keepdims=True)
+        rank = jnp.concatenate(ranks, axis=1)
+        needed = jnp.broadcast_to(jnp.floor((running + (TILE - 1)) * (1.0 / TILE)), (cells, 128))
+        lower = (iota((cells, cells), 1) < iota((cells, cells), 0)).astype(F32).astype(BF16)
+        start = dot_nn(lower, needed.astype(BF16))
+        inside = jnp.floor(rank * (1.0 / TILE))
+        tile_row = jnp.sum(onehot * start[:, 0:1], axis=0, keepdims=True) + inside
+        place_row = rank - inside * TILE
+        meta_ref[...] = jnp.concatenate(
+            [tile_row, place_row, jnp.zeros((6, segments), F32)], axis=0
+        )
+        ends = start[:, 0:1] + needed[:, 0:1]
+        owner = jnp.sum(
+            (ends <= iota((cells, tile_cell_ref.shape[1]), 1).astype(F32)).astype(F32),
+            axis=0,
+            keepdims=True,
+        )
+        owner = jnp.minimum(owner, cells - 1.0).astype(jnp.int32)
+        tile_cell_ref[...] = jnp.broadcast_to(owner, tile_cell_ref.shape)
+        tile_start_ref[0:cells, :] = start.astype(jnp.int32)
+        tile_start_ref[cells : cells + 8, :] = jnp.broadcast_to(
+            ends[cells - 1 : cells, :], (8, 128)
+        ).astype(jnp.int32)
+
+        mask = slot_mask(place_row)
+        place = tile_onehot(tile_row, tiles)
+        lengths = length_ref[...].T
+        near = jnp.zeros((1, rays), F32)
+        nears, extents = [], []
+        for k in range(crossings):
+            nears.append(near)
+            extents.append(lengths[k : k + 1, :])
+            near = near + lengths[k : k + 1, :]
+        rows = [
+            jnp.concatenate([geometry_ref[c : c + 1, :]] * crossings, axis=1) for c in range(6)
+        ]
+        rows += [jnp.concatenate(nears, axis=1), jnp.concatenate(extents, axis=1)]
+        wide = pick_nt(place, jnp.concatenate([mask * row for row in rows], axis=0))
+        wide = pick_nn(wide, lane_select(8, lanes))
+        channel = [wide[:, lanes * c : lanes * (c + 1)] for c in range(8)]
+        turned = jitter_ref[...].T
+        offsets = jnp.concatenate(
+            [turned[samples * k : samples * (k + 1), :] for k in range(crossings)], axis=1
+        )
+        dealt = jnp.concatenate([mask * offsets[i : i + 1, :] for i in range(samples)], axis=0)
+        jitter = pick_nt(place, dealt)
+        step = (iota((tiles, lanes), 1) // TILE).astype(F32)
+        near, extent = channel[6], channel[7]
+        depths = near + extent * (step + jitter) / samples
+        following = pltpu.roll(depths, lanes - TILE, 1)
+        ending = jnp.where(iota((tiles, lanes), 1) >= lanes - TILE, near + extent, following)
+        spacing_ref[...] = ending - depths
+        for c in range(3):
+            put_channel(position_ref, c, channel[c] + depths * channel[3 + c])
+        put_channel(position_ref, 3, jnp.ones((tiles, lanes), F32))
+        for c in range(4, 8):
+            put_channel(position_ref, c, jnp.zeros((tiles, lanes), F32))
+        turns = frequency_ref[...] * 0.15915494309189535
+        turns = jnp.concatenate([turns, turns], axis=1)
+        features = turns.shape[1]
+        quarter = jnp.where(iota((1, features), 1) < features // 2, -0.25, 0.0)
+        block = jnp.concatenate([turns, quarter, jnp.zeros((4, features), F32)], axis=0)
+        high, mid, low = [part.astype(F32) for part in split3(block)]
+        stack = [high, high, high, mid, mid, low, jnp.zeros((features - 48, features), F32)]
+        factor_ref[...] = jnp.concatenate(stack, axis=0).T[:, 0:48].astype(BF16)
+
+    factor = factor_ref[...]
+    for u in range(UNROLL):
+        t = pl.program_id(0) * UNROLL + u
+        high, mid, low = split3(get_tile(position_ref, t))
+        high, mid, low = high.astype(F32), mid.astype(F32), low.astype(F32)
+        points = jnp.concatenate([high, mid, low, high, mid, high], axis=0).astype(BF16)
+        phase = dot_nn(factor, points)
+        phase = phase - jnp.round(phase)
+        square = phase * phase
+        value = jnp.full_like(square, COS[5])
+        for c in (4, 3, 2, 1, 0):
+            value = value * square + COS[c]
+        encoded_ref[u] = value.astype(BF16)
+
+
+def step_kernel(
+    cells,
+    samples,
+    num_cell,
+    tile_cell_ref,
+    tile_start_ref,
+    near_ref,
+    flip_ref,
+    core_near_ref,
+    core_flip_ref,
+    encoded_ref,
+    meta_ref,
+    cells_ref,
+    spacing_ref,
+    codes_ref,
+    target_ref,
+    rendered_ref,
+    codes_grad_ref,
+    keep_ref,
+    send_ref,
+    first_ref,
+    second_ref,
+    forward1_ref,
+    forward2_ref,
+    backward2_ref,
+    head_ref,
+    head_turned_ref,
+    outputs_ref,
+    grads_ref,
+    sums_ref,
+    semaphore,
+):
+    tiles, lanes = spacing_ref.shape
+    crossings, rays = cells_ref.shape
+    segments = crossings * rays
+    width = codes_ref.shape[1]
+    used = tile_start_ref[cells, 0]
+    trips = (used + UNROLL - 1) // UNROLL
+
+    appearance = []
+    for group, ref in enumerate((near_ref, flip_ref, core_near_ref, core_flip_ref)):
+        for s in range(num_cell):
+            v = group * num_cell + s
+            forward1_ref[v] = ref[s, 0:128, :].astype(BF16)
+            second = ref[s, 128:256, :]
+            forward2_ref[v] = second.astype(BF16)
+            backward2_ref[v] = second.T.astype(BF16)
+            tail = ref[s, HEAD_ROW:ROWS, :]
+            head = jnp.where(iota((8, 128), 0) < 4, tail, 0.0)
+            head_ref[v] = head.astype(BF16)
+            square = jnp.concatenate([head, jnp.zeros((120, 128), F32)], axis=0)
+            head_turned_ref[v] = square.T[:, 0:8].astype(BF16)
+            appearance.append(tail)
+    outputs_ref[...] = jnp.zeros_like(outputs_ref)
+    sums_ref[...] = jnp.zeros_like(sums_ref)
+
+    def forward(trip, carry):
+        for u in range(UNROLL):
+            t = trip * UNROLL + u
+            v = tile_cell_ref[0, t]
+            first = jnp.maximum(dot_nn(forward1_ref[v], encoded_ref[t]), 0.0).astype(BF16)
+            first_ref[t] = first
+            second = jnp.maximum(dot_nn(forward2_ref[v], first), 0.0).astype(BF16)
+            second_ref[t] = second
+            put_tile(outputs_ref, t, dot_nn(head_ref[v], second))
+        return carry
+
+    lax.fori_loop(0, trips, forward, 0)
+
+    tile_row, place_row = meta_ref[0:1, :], meta_ref[1:2, :]
+    mask = slot_mask(place_row)
+    place = tile_onehot(tile_row, tiles)
+    onehots = cell_onehot(cells_ref, cells)
+    maps = jnp.concatenate(
+        [jnp.concatenate([tail[4 + c : 5 + c, :] for tail in appearance], axis=0) for c in range(3)],
+        axis=0,
+    )[:, 0:width]
+    codes = codes_ref[...]
+    shifts = lax.dot_general(
+        maps,
+        codes,
+        (((1,), (1,)), ((), ())),
+        precision=HIGHEST_PRECISION,
+        preferred_element_type=F32,
+    )
+    rows = [
+        jnp.concatenate(
+            [
+                jnp.sum(onehots[k] * shifts[cells * c : cells * (c + 1), :], axis=0, keepdims=True)
+                for k in range(crossings)
+            ],
+            axis=1,
+        )
+        for c in range(3)
+    ]
+    spread3 = lane_select(4, lanes)
+    shift = pick_nt(place, jnp.concatenate([mask * row for row in rows], axis=0))
+    shift = pick_nn(shift, spread3[0:24, 0 : 3 * lanes])
+
+    spacing = spacing_ref[...]
+    raw = get_channel(outputs_ref, 0)
+    ray = (iota((lanes, lanes), 0) % TILE) == (iota((lanes, lanes), 1) % TILE)
+    earlier = (ray & (iota((lanes, lanes), 0) < iota((lanes, lanes), 1))).astype(F32).astype(BF16)
+    later = (ray & (iota((lanes, lanes), 0) > iota((lanes, lanes), 1))).astype(F32).astype(BF16)
+    total = ((iota((TILE, lanes), 1) % TILE) == iota((TILE, lanes), 0)).astype(F32).astype(BF16)
+    density = jax.nn.softplus(raw)
+    colors = [
+        jax.nn.sigmoid(
+            get_channel(outputs_ref, 1 + c) + shift[:, lanes * c : lanes * (c + 1)]
+        )
+        for c in range(3)
+    ]
+    optical = density * spacing
+    transmit = jnp.exp(-pick_nn(optical, earlier))
+    opacity = 1.0 - jnp.exp(-optical)
+    blend = transmit * opacity
+    sums = [pick_nt(total, blend * color) for color in colors] + [-pick_nt(total, optical)]
+    dealt = pick_nn(jnp.concatenate(sums, axis=0), place)
+    parts = [
+        jnp.sum(mask * dealt[TILE * c : TILE * (c + 1), :], axis=0, keepdims=True) for c in range(4)
+    ]
+
+    def crossed(row, k):
+        return row[:, rays * k : rays * (k + 1)]
+
+    reach, logs = [], jnp.zeros((1, rays), F32)
+    for k in range(crossings):
+        reach.append(jnp.exp(logs))
+        logs = logs + crossed(parts[3], k)
+    residuals, channel_grads = [], [[] for _ in range(3)]
+    for c in range(3):
+        rendered = sum(reach[k] * crossed(parts[c], k) for k in range(crossings))
+        rendered_ref[c : c + 1, :] = rendered
+        residuals.append(rendered - target_ref[c : c + 1, :])
+    log_grads, after = [], jnp.zeros((1, rays), F32)
+    for k in reversed(range(crossings)):
+        log_grads.append(after)
+        weight = sum(residuals[c] * crossed(parts[c], k) for c in range(3))
+        after = after + weight * reach[k]
+    log_row = jnp.concatenate(log_grads[::-1], axis=1)
+    color_rows = [
+        jnp.concatenate([reach[k] * residuals[c] for k in range(crossings)], axis=1)
+        for c in range(3)
+    ]
+    back = pick_nt(place, jnp.concatenate([mask * row for row in color_rows + [log_row]], axis=0))
+    back = pick_nn(back, spread3)
+    color_grads = [back[:, lanes * c : lanes * (c + 1)] for c in range(3)]
+    log_grad = back[:, 3 * lanes : 4 * lanes]
+
+    blend_grad = sum(color_grads[c] * colors[c] for c in range(3))
+    before_grad = -(blend_grad * opacity) * transmit
+    optical_grad = blend_grad * transmit * (1.0 - opacity) - log_grad
+    optical_grad = optical_grad + pick_nn(before_grad, later)
+    put_channel(grads_ref, 0, optical_grad * spacing * jax.nn.sigmoid(raw))
+    logits = []
+    for c in range(3):
+        logit = color_grads[c] * blend * colors[c] * (1.0 - colors[c])
+        put_channel(grads_ref, 1 + c, logit)
+        put_channel(grads_ref, 4 + c, jnp.zeros((tiles, lanes), F32))
+        logits.append(pick_nt(total, logit))
+    put_channel(grads_ref, 7, jnp.zeros((tiles, lanes), F32))
+    dealt = pick_nn(jnp.concatenate(logits, axis=0), place)
+    per_cell = []
+    for c in range(3):
+        row = jnp.sum(mask * dealt[TILE * c : TILE * (c + 1), :], axis=0, keepdims=True)
+        per_cell.append(sum(onehots[k] * crossed(row, k) for k in range(crossings)))
+    per_cell = jnp.concatenate(per_cell, axis=0)
+    map_grads = exact_nn(per_cell, codes)
+    codes_grad_ref[...] = exact_nn(per_cell.T, maps)
+    for v in range(cells):
+        for c in range(3):
+            sums_ref[v, APP_ROW + c : APP_ROW + c + 1, 0:width] = map_grads[
+                cells * c + v : cells * c + v + 1, :
+            ]
+
+    def backward(trip, carry):
+        for u in range(UNROLL):
+            t = trip * UNROLL + u
+            v = tile_cell_ref[0, t]
+            output = get_tile(grads_ref, t).astype(BF16)
+            first, second, encoded = first_ref[t], second_ref[t], encoded_ref[t]
+            second_grad = dot_nn(head_turned_ref[v], output)
+            second_grad = jnp.where(second.astype(F32) > 0, second_grad, 0.0).astype(BF16)
+            first_grad = dot_nn(backward2_ref[v], second_grad)
+            first_grad = jnp.where(first.astype(F32) > 0, first_grad, 0.0).astype(BF16)
+            sums_ref[v, HEAD_ROW:ROWS, :] += dot_nt(output, second)
+            sums_ref[v, 128:256, :] += dot_nt(first, second_grad)
+            sums_ref[v, 0:128, :] += dot_nt(encoded, first_grad)
+        return carry
+
+    lax.fori_loop(0, trips, backward, 0)
+    half = cells // 2
+    copies = [
+        pltpu.make_async_copy(sums_ref.at[pl.ds(0, half)], keep_ref, semaphore.at[0]),
+        pltpu.make_async_copy(sums_ref.at[pl.ds(half, half)], send_ref, semaphore.at[1]),
+    ]
+    for copy in copies:
+        copy.start()
+    for copy in copies:
+        copy.wait()
+
+
+def resident(
+    ray_geometry,
+    segment_length,
+    jitter,
+    appearance_codes,
+    target,
+    crossing,
+    frequencies,
+    cell_layers,
+    district_prior,
+    head_weight,
+    appearance_weight,
+):
+    num_cell = lax.axis_size("cell")
+    num_district = lax.axis_size("district")
+    cells = num_cell * num_district
+    rays, crossings = crossing.shape
+    samples = jitter.shape[1] // crossings
+    segments = rays * crossings
+    width = appearance_codes.shape[1]
+    lanes = TILE * samples
+    tiles = -(-(segments // TILE + cells) // 8) * 8
+    me_cell, me_district = lax.axis_index("cell"), lax.axis_index("district")
+
+    def along_cell(x, steps):
+        return lax.ppermute(x, "cell", [(i, (i + steps) % num_cell) for i in range(num_cell)])
+
+    def flip(x, bit):
+        return lax.ppermute(x, "district", [(i, i ^ bit) for i in range(num_district)])
+
+    own = pl.pallas_call(
+        pack_kernel, out_shape=jax.ShapeDtypeStruct((ROWS, 128), F32), name="pack"
+    )(cell_layers, district_prior, head_weight, appearance_weight)
+    near = jnp.stack([own] + [along_cell(own, s) for s in range(1, num_cell)])
+    flipped = flip(near, 2)
+    core_near, core_flipped = flip(near, 1), flip(flipped, 1)
+
+    away = (crossing % num_district) ^ me_district
+    steps = (me_cell - crossing // num_district) % num_cell
+    virtual = ((away & 1) * 2 + (away >> 1)) * num_cell + steps
+    whole = lambda shape: pl.BlockSpec(shape, lambda i: (0,) * len(shape))
+    encoded, meta, spacing, tile_cell, tile_start = pl.pallas_call(
+        functools.partial(encode_kernel, cells, samples),
+        grid=(tiles // UNROLL,),
+        in_specs=[
+            whole((crossings, rays)),
+            whole((6, rays)),
+            whole((rays, crossings)),
+            whole((rays, crossings * samples)),
+            whole(frequencies.shape),
+        ],
+        out_specs=[
+            pl.BlockSpec((UNROLL, 128, lanes), lambda i: (i, 0, 0)),
+            whole((8, segments)),
+            whole((tiles, lanes)),
+            whole((8, 256)),
+            whole((cells + 8, 128)),
+        ],
+        out_shape=[
+            jax.ShapeDtypeStruct((tiles, 128, lanes), BF16),
+            jax.ShapeDtypeStruct((8, segments), F32),
+            jax.ShapeDtypeStruct((tiles, lanes), F32),
+            jax.ShapeDtypeStruct((8, 256), jnp.int32),
+            jax.ShapeDtypeStruct((cells + 8, 128), jnp.int32),
+        ],
+        scratch_shapes=[
+            pltpu.VMEM((lanes // 128, tiles * 8, 128), F32),
+            pltpu.VMEM((128, 48), BF16),
+        ],
+        compiler_params=pltpu.CompilerParams(vmem_limit_bytes=VMEM_LIMIT),
+        name="encode",
+    )(virtual.T, ray_geometry, segment_length, jitter, frequencies)
+
+    vmem, smem = pl.BlockSpec(memory_space=pltpu.VMEM), pl.BlockSpec(memory_space=pltpu.SMEM)
+    half = cells // 2
+    rendered, codes_grad, keep, send = pl.pallas_call(
+        functools.partial(step_kernel, cells, samples, num_cell),
+        in_specs=[smem, smem] + [vmem] * 10,
+        out_specs=[vmem, vmem, pl.BlockSpec(memory_space=pl.ANY), pl.BlockSpec(memory_space=pl.ANY)],
+        out_shape=[
+            jax.ShapeDtypeStruct((3, rays), F32),
+            jax.ShapeDtypeStruct((rays, width), F32),
+            jax.ShapeDtypeStruct((half, ROWS, 128), F32),
+            jax.ShapeDtypeStruct((half, ROWS, 128), F32),
+        ],
+        scratch_shapes=[
+            pltpu.VMEM((tiles, 128, lanes), BF16),
+            pltpu.VMEM((tiles, 128, lanes), BF16),
+            pltpu.VMEM((cells, 128, 128), BF16),
+            pltpu.VMEM((cells, 128, 128), BF16),
+            pltpu.VMEM((cells, 128, 128), BF16),
+            pltpu.VMEM((cells, 8, 128), BF16),
+            pltpu.VMEM((cells, 128, 8), BF16),
+            pltpu.VMEM((lanes // 128, tiles * 8, 128), F32),
+            pltpu.VMEM((lanes // 128, tiles * 8, 128), F32),
+            pltpu.VMEM((cells, ROWS, 128), F32),
+            pltpu.SemaphoreType.DMA((2,)),
+        ],
+        compiler_params=pltpu.CompilerParams(vmem_limit_bytes=VMEM_LIMIT),
+        name="step",
+    )(
+        tile_cell,
+        tile_start,
+        near,
+        flipped,
+        core_near,
+        core_flipped,
+        encoded,
+        meta,
+        virtual.T,
+        spacing,
+        appearance_codes,
+        target,
+    )
+
+    summed = keep + flip(send, 1)
+    summed = summed[:num_cell] + flip(summed[num_cell:], 2)
+    arrived = [along_cell(summed[s], -s) for s in range(1, num_cell)]
+    own_sum = summed[0] + sum(arrived)
+    layers = own_sum[0:HEAD_ROW].reshape(2, 128, 128)
+    others = [along_cell(layers, s) for s in range(1, num_cell)]
+    prior = (layers + sum(others)) / num_cell
+    return (
+        rendered,
+        layers[None],
+        prior[None],
+        own_sum[None, HEAD_ROW : HEAD_ROW + 4],
+        own_sum[None, APP_ROW : APP_ROW + 3, 0:width],
+        codes_grad,
+    )
+
+
+def local(*args):
+    cells = lax.axis_size("cell") * lax.axis_size("district")
+    if cells <= 16 and lax.axis_size("district") == 4:
+        return resident(*args)
+    return routed(*args)
+
+
 def solution(mesh):
     placed = (
         P(None, ("scene", "cell", "district")),

time: 501 us -> 197 us (0.39); the launches traced: 494 us -> 196 us
  other arithmetic: 188 us -> 3.72 us
  matrix products: 127 us -> 0 us
  Pallas kernels: 0 us -> 111 us
  local copies, waits for them, and re-layouts: 80.1 us -> 5.79 us
  between operations: 15.1 us -> 0.78 us
  waiting for transfers between devices: 62.6 us -> 54.8 us
    concatenate x5 -> x0, other arithmetic: 133 us -> none  [the longest x4 133 us: cell_forward(): encoded = jnp.concatenate([jnp.sin(phases), jnp.cos(phases)], axis=2)]
    dot_general x45 -> x0, matrix products: 127 us -> none  [the longest x4 31.2 us: cell_backward(): lax.dot_general(encoded, first_grad, (((0,), (0,)), ((), ())), preferred_...]
    pallas_call x0 -> x3, Pallas kernels: none -> 111 us  [the longest x1 86.5 us: resident(): pl.pallas_call(functools.partial(step_kernel, cells, samples, num_cell),...]
    ppermute x0 -> x14, waiting for transfers between devices: none -> 54.8 us  [the longest x5 27.6 us: flip(): lax.ppermute(x, 'district', [(i, i ^ bit) for i in range(num_district)])]
    psum x1 -> x0, waiting for transfers between devices: 32 us -> none  [local(): grad_prior = lax.psum(grad_pair, 'cell') / num_cell]
    all_to_all x4 -> x0, waiting for transfers between devices: 30.5 us -> none  [the longest x1 17.5 us: local(): lax.all_to_all(outbox, ('cell', 'district'), split_axis=0, concat_axis=0,...]
    dynamic_update_slice x8 -> x0, other arithmetic: 23.9 us -> none  [local(): partials, stored = lax.map(forward_keep, blocked)]
    ppermute x0 -> x14, starting transfers between devices: none -> 19.9 us  [the longest x9 16.2 us: along_cell(): lax.ppermute(x, 'cell', [(i, (i + steps) % num_cell) for i in range(num_c...]
  transfers between devices with their start and end apart: 5 -> 14, of which waited for: 4 -> 9; matrix products, arithmetic and copies ran while one was open for 2% -> 2% of each run, Pallas kernels for 0% -> 12%
where the time goes in v1:
time: 197 us; the launch traced here: 196 us
  Pallas kernels  111 us (56%)
  waiting for transfers between devices  54.8 us (28%)
  starting transfers between devices  19.9 us (10%)
  local copies, waits for them, and re-layouts  5.79 us (3%)
  other arithmetic  3.72 us (2%)
    pallas_call x1, Pallas kernels, resident(): pl.pallas_call(functools.partial(step_kernel, cells, samples, num_cell),...  86.5 us
    ppermute x5, waiting for transfers between devices, flip(): lax.ppermute(x, 'district', [(i, i ^ bit) for i in range(num_district)])  27.6 us
    ppermute x9, waiting for transfers between devices, along_cell(): lax.ppermute(x, 'cell', [(i, (i + steps) % num_cell) for i in range(num_c...  27.2 us
    pallas_call x1, Pallas kernels, resident(): pl.pallas_call(functools.partial(encode_kernel, cells, samples), grid=(ti...  23.2 us
    ppermute x9, starting transfers between devices, along_cell(): lax.ppermute(x, 'cell', [(i, (i + steps) % num_cell) for i in range(num_c...  16.2 us
    unnamed x23, local copies, waits for them, and re-layouts  5.13 us
  transfers between devices with their start and end apart: 14, of which 9 were waited for; matrix products, arithmetic and copies ran while one was open for 2% of the time, Pallas kernels for 12%

profile of v1, /device:TPU:0, one launch (start us, length us, event | category | flops | bytes accessed | tf_op | source)
XLA Modules:
  0.0 196.3 jit_solution(9039117461231144721)
XLA Ops:
  0.7 1.3 copy.18.app_ref
  1.9 1.6 pack.1
  3.6 5.0 %collective-permute-start.2 = (f32[264,128]{1,0:T(8,128)}, f32[264,128]{1,0:T(8,128)S(1)}, u32[]{:S(2)}, u32[]{:S(2)}) collective-permute-start(f32[264,128]{1,0:T(8,128)} %pack.1), channel_id=1, source_target_pairs={{0,12},{4,0},{8,4},{12,8},{1,13},{5,1},{9,5},{13,9},{2,14},{6,2},{... | collective-permute-start | bytes 405512 | tf_op jit(solution)/shard_map/ppermute | solution.py:714
  8.6 1.0 collective-permute-start
  9.6 3.3 %collective-permute-done.2 = f32[264,128]{1,0:T(8,128)S(1)} collective-permute-done((f32[264,128]{1,0:T(8,128)}, f32[264,128]{1,0:T(8,128)S(1)}, u32[]{:S(2)}, u32[]{:S(2)}) %collective-permute-start.2) | collective-permute-done | bytes 135200 | tf_op jit(solution)/shard_map/ppermute | solution.py:714
  12.9 7.4 %collective-permute-done.1 = f32[264,128]{1,0:T(8,128)S(1)} collective-permute-done((f32[264,128]{1,0:T(8,128)}, f32[264,128]{1,0:T(8,128)S(1)}, u32[]{:S(2)}, u32[]{:S(2)}) %collective-permute-start.1) | collective-permute-done | bytes 135200 | tf_op jit(solution)/shard_map/ppermute | solution.py:714
  20.3 1.0 pad_maximum_fusion.near_ref
  21.3 1.6 collective-permute-start.3
  22.9 12.0 %collective-permute-done.3.flip_ref = f32[4,264,128]{2,1,0:T(8,128)S(1)} collective-permute-done((f32[4,264,128]{2,1,0:T(8,128)S(1)}, f32[4,264,128]{2,1,0:T(8,128)S(1)}, u32[]{:S(2)}, u32[]{:S(2)}) %collective-permute-start.3) | collective-permute-done | bytes 540704 | tf_op jit(solution)/shard_map/ppermute | solution.py:717
  34.9 0.8 copy.17.length_ref
  37.1 23.2 %encode.1 = (bf16[144,128,256]{2,1,0:T(8,128)(2,1)}, f32[8,1024]{1,0:T(8,128)}, f32[144,256]{1,0:T(8,128)}, s32[8,256]{1,0:T(8,128)}, s32[24,128]{1,0:T(8,128)}) custom-call(s32[4,256]{1,0:T(4,128)} %fusion.5.cells_ref, f32[6,256]{1,0:T(8,128)} %geometry_ref.1, f32[256,4]{1,0:T(8,128)} %copy.17.length_ref, f32[256,128]{1,0:T(8,128)} %jitter_ref.1, ...), custom_call_target="tpu_custom_call" | custom-call | tf_op jit(solution)/shard_map/encode/pallas_call | solution.py:730
  61.3 86.5 %step.1 = (f32[3,256]{1,0:T(4,128)}, f32[256,48]{1,0:T(8,128)}, f32[8,264,128]{2,1,0:T(8,128)}, f32[8,264,128]{2,1,0:T(8,128)}) custom-call(s32[8,256]{1,0:T(8,128)} %get-tuple-element.15.tile_cell_ref, s32[24,128]{1,0:T(8,128)} %get-tuple-element.16.tile_start_ref, f32[4,264,128]{2,1,0:T(8,128)} %copy-done, f32[4,264,128]{2,1,0:T(8,128)} %copy-done.1, ...), custom_call_target="tpu_custom_call" | custom-call | tf_op jit(solution)/shard_map/step/pallas_call | solution.py:764
  148.4 2.5 %collective-permute-done.6 = f32[8,264,128]{2,1,0:T(8,128)S(1)} collective-permute-done((f32[8,264,128]{2,1,0:T(8,128)}, f32[8,264,128]{2,1,0:T(8,128)S(1)}, u32[]{:S(2)}, u32[]{:S(2)}) %collective-permute-start.6) | collective-permute-done | bytes 1081376 | tf_op jit(solution)/shard_map/ppermute | solution.py:717
  151.0 1.4 add.45
  152.4 1.6 collective-permute-start.7
  153.9 13.1 %collective-permute-done.7 = f32[4,264,128]{2,1,0:T(8,128)S(1)} collective-permute-done((f32[4,264,128]{2,1,0:T(8,128)S(1)}, f32[4,264,128]{2,1,0:T(8,128)S(1)}, u32[]{:S(2)}, u32[]{:S(2)}) %collective-permute-start.7) | collective-permute-done | bytes 540704 | tf_op jit(solution)/shard_map/ppermute | solution.py:717
  167.1 2.6 %collective-permute-start.9 = (f32[264,128]{1,0:T(8,128)S(1)}, f32[264,128]{1,0:T(8,128)S(1)}, u32[]{:S(2)}, u32[]{:S(2)}) collective-permute-start(f32[264,128]{1,0:T(8,128)S(1)} %get-tuple-element.30), channel_id=1, source_target_pairs={{0,8},{4,12},{8,0},{12,4},{1,9},{5,13},{9,1},{13,5},{2,10},{6,14},... | collective-permute-start | bytes 405512 | tf_op jit(solution)/shard_map/ppermute | solution.py:714
  169.7 3.8 %collective-permute-start.8 = (f32[264,128]{1,0:T(8,128)S(1)}, f32[264,128]{1,0:T(8,128)S(1)}, u32[]{:S(2)}, u32[]{:S(2)}) collective-permute-start(f32[264,128]{1,0:T(8,128)S(1)} %get-tuple-element.32), channel_id=1, source_target_pairs={{0,12},{4,0},{8,4},{12,8},{1,13},{5,1},{9,5},{13,9},{2,14},{6,2},{... | collective-permute-start | bytes 405512 | tf_op jit(solution)/shard_map/ppermute | solution.py:714
  174.3 5.0 %collective-permute-done.9 = f32[264,128]{1,0:T(8,128)S(1)} collective-permute-done((f32[264,128]{1,0:T(8,128)S(1)}, f32[264,128]{1,0:T(8,128)S(1)}, u32[]{:S(2)}, u32[]{:S(2)}) %collective-permute-start.9) | collective-permute-done | bytes 135200 | tf_op jit(solution)/shard_map/ppermute | solution.py:714
  179.2 1.0 collective-permute-done.8
  180.3 2.2 %collective-permute-start.13 = (f32[2,128,128]{2,1,0:T(8,128)S(1)}, f32[2,128,128]{2,1,0:T(8,128)S(1)}, u32[]{:S(2)}, u32[]{:S(2)}) collective-permute-start(f32[2,128,128]{2,1,0:T(8,128)S(1)} %bitcast.25), channel_id=1, source_target_pairs={{0,12},{4,0},{8,4},{12,8},{1,13},{5,1},{9,5},{13,9},{2,14},{6,2},{... | collective-permute-start | bytes 393224 | tf_op jit(solution)/shard_map/ppermute | solution.py:714
  182.5 1.5 collective-permute-start.12
  185.2 1.3 collective-permute-done.13
  186.4 9.2 %collective-permute-done.12 = f32[2,128,128]{2,1,0:T(8,128)S(1)} collective-permute-done((f32[2,128,128]{2,1,0:T(8,128)S(1)}, f32[2,128,128]{2,1,0:T(8,128)S(1)}, u32[]{:S(2)}, u32[]{:S(2)}) %collective-permute-start.12) | collective-permute-done | bytes 131104 | tf_op jit(solution)/shard_map/ppermute | solution.py:714
  (41 shorter events, 5.7 us)
Async XLA Ops:
  0.6 34.3 %copy-start.7 = (f32[256,4]{0,1:T(4,128)S(1)}, f32[256,4]{0,1:T(4,128)}, u32[]{:S(2)}) copy-start(f32[256,4]{0,1:T(4,128)} %param.12) | copy-start | bytes 12292
  0.6 35.1 %copy-start.6 = (f32[256,48]{0,1:T(8,128)S(1)}, f32[256,48]{0,1:T(8,128)}, u32[]{:S(2)}) copy-start(f32[256,48]{0,1:T(8,128)} %param.14) | copy-start | bytes 147460
  0.7 35.8 %copy-start.8 = (s32[256,4]{0,1:T(4,128)S(1)}, s32[256,4]{0,1:T(4,128)}, u32[]{:S(2)}) copy-start(s32[256,4]{0,1:T(4,128)} %param.16) | copy-start | bytes 12292
  3.6 9.4 %collective-permute-start.2 = (f32[264,128]{1,0:T(8,128)}, f32[264,128]{1,0:T(8,128)S(1)}, u32[]{:S(2)}, u32[]{:S(2)}) collective-permute-start(f32[264,128]{1,0:T(8,128)} %pack.1), channel_id=1, source_target_pairs={{0,12},{4,0},{8,4},{12,8},{1,13},{5,1},{9,5},{13,9},{2,14},{6,2},{... | collective-permute-start | bytes 405512 | tf_op jit(solution)/shard_map/ppermute | solution.py:714
  8.6 11.7 %collective-permute-start.1 = (f32[264,128]{1,0:T(8,128)}, f32[264,128]{1,0:T(8,128)S(1)}, u32[]{:S(2)}, u32[]{:S(2)}) collective-permute-start(f32[264,128]{1,0:T(8,128)} %pack.1), channel_id=1, source_target_pairs={{0,8},{4,12},{8,0},{12,4},{1,9},{5,13},{9,1},{13,5},{2,10},{6,14},... | collective-permute-start | bytes 405512 | tf_op jit(solution)/shard_map/ppermute | solution.py:714
  8.6 11.7 %collective-permute-start = (f32[264,128]{1,0:T(8,128)}, f32[264,128]{1,0:T(8,128)S(1)}, u32[]{:S(2)}, u32[]{:S(2)}) collective-permute-start(f32[264,128]{1,0:T(8,128)} %pack.1), channel_id=1, source_target_pairs={{0,4},{4,8},{8,12},{12,0},{1,5},{5,9},{9,13},{13,1},{2,6},{6,10},{... | collective-permute-start | bytes 405512 | tf_op jit(solution)/shard_map/ppermute | solution.py:714
  21.3 39.0 %copy-start = (f32[4,264,128]{2,1,0:T(8,128)}, f32[4,264,128]{2,1,0:T(8,128)S(1)}, u32[]{:S(2)}) copy-start(f32[4,264,128]{2,1,0:T(8,128)S(1)} %pad_maximum_fusion.near_ref) | copy-start | bytes 1622020
  21.3 13.6 %collective-permute-start.3 = (f32[4,264,128]{2,1,0:T(8,128)S(1)}, f32[4,264,128]{2,1,0:T(8,128)S(1)}, u32[]{:S(2)}, u32[]{:S(2)}) collective-permute-start(f32[4,264,128]{2,1,0:T(8,128)S(1)} %pad_maximum_fusion.near_ref), channel_id=1, source_target_pairs={{0,2},{1,3},{2,0},{3,1},{4,6},{5,7},{6,4},{7,5},{8,10},{9,11},{10,... | collective-permute-start | bytes 1622024 | tf_op jit(solution)/shard_map/ppermute | solution.py:717
  22.9 37.4 %collective-permute-start.4 = (f32[4,264,128]{2,1,0:T(8,128)S(1)}, f32[4,264,128]{2,1,0:T(8,128)S(1)}, u32[]{:S(2)}, u32[]{:S(2)}) collective-permute-start(f32[4,264,128]{2,1,0:T(8,128)S(1)} %pad_maximum_fusion.near_ref), channel_id=1, source_target_pairs={{0,1},{1,0},{2,3},{3,2},{4,5},{5,4},{6,7},{7,6},{8,9},{9,8},{10,11... | collective-permute-start | bytes 1622024 | tf_op jit(solution)/shard_map/ppermute | solution.py:717
  34.9 25.4 %copy-start.1 = (f32[4,264,128]{2,1,0:T(8,128)}, f32[4,264,128]{2,1,0:T(8,128)S(1)}, u32[]{:S(2)}) copy-start(f32[4,264,128]{2,1,0:T(8,128)S(1)} %collective-permute-done.3.flip_ref) | copy-start | bytes 1622020
  34.9 25.4 %collective-permute-start.5 = (f32[4,264,128]{2,1,0:T(8,128)S(1)}, f32[4,264,128]{2,1,0:T(8,128)S(1)}, u32[]{:S(2)}, u32[]{:S(2)}) collective-permute-start(f32[4,264,128]{2,1,0:T(8,128)S(1)} %collective-permute-done.3.flip_ref), channel_id=1, source_target_pairs={{0,1},{1,0},{2,3},{3,2},{4,5},{5,4},{6,7},{7,6},{8,9},{9,8},{10,11... | collective-permute-start | bytes 1622024 | tf_op jit(solution)/shard_map/ppermute | solution.py:717
  60.3 0.8 copy-start.2
  60.3 1.0 copy-start.3
  147.9 3.1 %collective-permute-start.6 = (f32[8,264,128]{2,1,0:T(8,128)}, f32[8,264,128]{2,1,0:T(8,128)S(1)}, u32[]{:S(2)}, u32[]{:S(2)}) collective-permute-start(f32[8,264,128]{2,1,0:T(8,128)} %get-tuple-element.22), channel_id=1, source_target_pairs={{0,1},{1,0},{2,3},{3,2},{4,5},{5,4},{6,7},{7,6},{8,9},{9,8},{10,11... | collective-permute-start | bytes 3244040 | tf_op jit(solution)/shard_map/ppermute | solution.py:717
  152.4 21.2 %copy-start.5 = (f32[256,48]{1,0:T(8,128)S(1)}, f32[256,48]{1,0:T(8,128)}, u32[]{:S(2)}) copy-start(f32[256,48]{1,0:T(8,128)} %get-tuple-element.29) | copy-start | bytes 147460
  152.4 14.6 %collective-permute-start.7 = (f32[4,264,128]{2,1,0:T(8,128)S(1)}, f32[4,264,128]{2,1,0:T(8,128)S(1)}, u32[]{:S(2)}, u32[]{:S(2)}) collective-permute-start(f32[4,264,128]{2,1,0:T(8,128)S(1)} %slice.37), channel_id=1, source_target_pairs={{0,2},{1,3},{2,0},{3,1},{4,6},{5,7},{6,4},{7,5},{8,10},{9,11},{10,... | collective-permute-start | bytes 1622024 | tf_op jit(solution)/shard_map/ppermute | solution.py:717
  167.1 12.1 %collective-permute-start.9 = (f32[264,128]{1,0:T(8,128)S(1)}, f32[264,128]{1,0:T(8,128)S(1)}, u32[]{:S(2)}, u32[]{:S(2)}) collective-permute-start(f32[264,128]{1,0:T(8,128)S(1)} %get-tuple-element.30), channel_id=1, source_target_pairs={{0,8},{4,12},{8,0},{12,4},{1,9},{5,13},{9,1},{13,5},{2,10},{6,14},... | collective-permute-start | bytes 405512 | tf_op jit(solution)/shard_map/ppermute | solution.py:714
  169.7 9.5 %collective-permute-start.10 = (f32[264,128]{1,0:T(8,128)S(1)}, f32[264,128]{1,0:T(8,128)S(1)}, u32[]{:S(2)}, u32[]{:S(2)}) collective-permute-start(f32[264,128]{1,0:T(8,128)S(1)} %get-tuple-element.31), channel_id=1, source_target_pairs={{0,4},{4,8},{8,12},{12,0},{1,5},{5,9},{9,13},{13,1},{2,6},{6,10},{... | collective-permute-start | bytes 405512 | tf_op jit(solution)/shard_map/ppermute | solution.py:714
  169.7 10.5 %collective-permute-start.8 = (f32[264,128]{1,0:T(8,128)S(1)}, f32[264,128]{1,0:T(8,128)S(1)}, u32[]{:S(2)}, u32[]{:S(2)}) collective-permute-start(f32[264,128]{1,0:T(8,128)S(1)} %get-tuple-element.32), channel_id=1, source_target_pairs={{0,12},{4,0},{8,4},{12,8},{1,13},{5,1},{9,5},{13,9},{2,14},{6,2},{... | collective-permute-start | bytes 405512 | tf_op jit(solution)/shard_map/ppermute | solution.py:714
  180.3 16.0 %copy-start.4 = (f32[256,128]{1,0:T(8,128)}, f32[256,128]{1,0:T(8,128)S(1)}, u32[]{:S(2)}) copy-start(f32[256,128]{1,0:T(8,128)S(1)} %slice.42) | copy-start | bytes 393220
  180.3 6.1 %collective-permute-start.13 = (f32[2,128,128]{2,1,0:T(8,128)S(1)}, f32[2,128,128]{2,1,0:T(8,128)S(1)}, u32[]{:S(2)}, u32[]{:S(2)}) collective-permute-start(f32[2,128,128]{2,1,0:T(8,128)S(1)} %bitcast.25), channel_id=1, source_target_pairs={{0,12},{4,0},{8,4},{12,8},{1,13},{5,1},{9,5},{13,9},{2,14},{6,2},{... | collective-permute-start | bytes 393224 | tf_op jit(solution)/shard_map/ppermute | solution.py:714
  182.5 13.1 %collective-permute-start.12 = (f32[2,128,128]{2,1,0:T(8,128)S(1)}, f32[2,128,128]{2,1,0:T(8,128)S(1)}, u32[]{:S(2)}, u32[]{:S(2)}) collective-permute-start(f32[2,128,128]{2,1,0:T(8,128)S(1)} %bitcast.26), channel_id=1, source_target_pairs={{0,8},{4,12},{8,0},{12,4},{1,9},{5,13},{9,1},{13,5},{2,10},{6,14},... | collective-permute-start | bytes 393224 | tf_op jit(solution)/shard_map/ppermute | solution.py:714
  184.0 11.6 %collective-permute-start.11 = (f32[2,128,128]{2,1,0:T(8,128)S(1)}, f32[2,128,128]{2,1,0:T(8,128)S(1)}, u32[]{:S(2)}, u32[]{:S(2)}) collective-permute-start(f32[2,128,128]{2,1,0:T(8,128)S(1)} %bitcast.27), channel_id=1, source_target_pairs={{0,4},{4,8},{8,12},{12,0},{1,5},{5,9},{9,13},{13,1},{2,6},{6,10},{... | collective-permute-start | bytes 393224 | tf_op jit(solution)/shard_map/ppermute | solution.py:714

commit v2 on v1

--- a/solution.py
+++ b/solution.py
@@ -268,7 +268,7 @@
 
 
 TILE = 8
-UNROLL = 4
+UNROLL = 16
 ROWS = 264
 HEAD_ROW = 256
 APP_ROW = 260
@@ -346,7 +346,8 @@
         out_ref[128 * layer : 128 * (layer + 1), :] = both.T
     out_ref[HEAD_ROW:ROWS, :] = jnp.zeros((ROWS - HEAD_ROW, 128), F32)
     out_ref[HEAD_ROW : HEAD_ROW + 4, :] = head_ref[0].astype(F32)
-    out_ref[APP_ROW : APP_ROW + 3, 0 : app_ref.shape[2]] = app_ref[0]
+    for c in range(3):
+        out_ref[APP_ROW + c : APP_ROW + c + 1, 0 : app_ref.shape[2]] = app_ref[c]
 
 
 def slot_mask(place_row):
@@ -371,7 +372,7 @@
     return same.astype(F32).astype(BF16)
 
 
-def encode_kernel(
+def deal_kernel(
     cells,
     samples,
     cells_ref,
@@ -379,7 +380,6 @@
     length_ref,
     jitter_ref,
     frequency_ref,
-    encoded_ref,
     meta_ref,
     spacing_ref,
     tile_cell_ref,
@@ -392,163 +392,172 @@
     crossings, rays = cells_ref.shape
     segments = crossings * rays
 
-    @pl.when(pl.program_id(0) == 0)
-    def _():
-        onehot = jnp.concatenate(cell_onehot(cells_ref, cells), axis=1)
-        chunks = [onehot[:, 128 * c : 128 * (c + 1)] for c in range(segments // 128)]
-        before = (iota((128, 128), 0) < iota((128, 128), 1)).astype(F32).astype(BF16)
-        prefix = dot_nn(jnp.concatenate(chunks, axis=0).astype(BF16), before)
-        running = jnp.zeros((cells, 1), F32)
-        ranks = []
-        for c, chunk in enumerate(chunks):
-            earlier = prefix[cells * c : cells * (c + 1), :] + running
-            ranks.append(jnp.sum(chunk * earlier, axis=0, keepdims=True))
-            running = running + jnp.sum(chunk, axis=1, keepdims=True)
-        rank = jnp.concatenate(ranks, axis=1)
-        needed = jnp.broadcast_to(jnp.floor((running + (TILE - 1)) * (1.0 / TILE)), (cells, 128))
-        lower = (iota((cells, cells), 1) < iota((cells, cells), 0)).astype(F32).astype(BF16)
-        start = dot_nn(lower, needed.astype(BF16))
-        inside = jnp.floor(rank * (1.0 / TILE))
-        tile_row = jnp.sum(onehot * start[:, 0:1], axis=0, keepdims=True) + inside
-        place_row = rank - inside * TILE
-        meta_ref[...] = jnp.concatenate(
-            [tile_row, place_row, jnp.zeros((6, segments), F32)], axis=0
-        )
-        ends = start[:, 0:1] + needed[:, 0:1]
-        owner = jnp.sum(
-            (ends <= iota((cells, tile_cell_ref.shape[1]), 1).astype(F32)).astype(F32),
-            axis=0,
-            keepdims=True,
-        )
-        owner = jnp.minimum(owner, cells - 1.0).astype(jnp.int32)
-        tile_cell_ref[...] = jnp.broadcast_to(owner, tile_cell_ref.shape)
-        tile_start_ref[0:cells, :] = start.astype(jnp.int32)
-        tile_start_ref[cells : cells + 8, :] = jnp.broadcast_to(
-            ends[cells - 1 : cells, :], (8, 128)
-        ).astype(jnp.int32)
-
-        mask = slot_mask(place_row)
-        place = tile_onehot(tile_row, tiles)
-        lengths = length_ref[...].T
-        near = jnp.zeros((1, rays), F32)
-        nears, extents = [], []
-        for k in range(crossings):
-            nears.append(near)
-            extents.append(lengths[k : k + 1, :])
-            near = near + lengths[k : k + 1, :]
-        rows = [
-            jnp.concatenate([geometry_ref[c : c + 1, :]] * crossings, axis=1) for c in range(6)
-        ]
-        rows += [jnp.concatenate(nears, axis=1), jnp.concatenate(extents, axis=1)]
-        wide = pick_nt(place, jnp.concatenate([mask * row for row in rows], axis=0))
-        wide = pick_nn(wide, lane_select(8, lanes))
-        channel = [wide[:, lanes * c : lanes * (c + 1)] for c in range(8)]
-        turned = jitter_ref[...].T
-        offsets = jnp.concatenate(
-            [turned[samples * k : samples * (k + 1), :] for k in range(crossings)], axis=1
-        )
-        dealt = jnp.concatenate([mask * offsets[i : i + 1, :] for i in range(samples)], axis=0)
-        jitter = pick_nt(place, dealt)
-        step = (iota((tiles, lanes), 1) // TILE).astype(F32)
-        near, extent = channel[6], channel[7]
-        depths = near + extent * (step + jitter) / samples
-        following = pltpu.roll(depths, lanes - TILE, 1)
-        ending = jnp.where(iota((tiles, lanes), 1) >= lanes - TILE, near + extent, following)
-        spacing_ref[...] = ending - depths
-        for c in range(3):
-            put_channel(position_ref, c, channel[c] + depths * channel[3 + c])
-        put_channel(position_ref, 3, jnp.ones((tiles, lanes), F32))
-        for c in range(4, 8):
-            put_channel(position_ref, c, jnp.zeros((tiles, lanes), F32))
-        turns = frequency_ref[...] * 0.15915494309189535
-        turns = jnp.concatenate([turns, turns], axis=1)
-        features = turns.shape[1]
-        quarter = jnp.where(iota((1, features), 1) < features // 2, -0.25, 0.0)
-        block = jnp.concatenate([turns, quarter, jnp.zeros((4, features), F32)], axis=0)
-        high, mid, low = [part.astype(F32) for part in split3(block)]
-        stack = [high, high, high, mid, mid, low, jnp.zeros((features - 48, features), F32)]
-        factor_ref[...] = jnp.concatenate(stack, axis=0).T[:, 0:48].astype(BF16)
-
-    factor = factor_ref[...]
-    for u in range(UNROLL):
-        t = pl.program_id(0) * UNROLL + u
+    onehot = jnp.concatenate(cell_onehot(cells_ref, cells), axis=1)
+    chunks = [onehot[:, 128 * c : 128 * (c + 1)] for c in range(segments // 128)]
+    before = (iota((128, 128), 0) < iota((128, 128), 1)).astype(F32).astype(BF16)
+    prefix = dot_nn(jnp.concatenate(chunks, axis=0).astype(BF16), before)
+    running = jnp.zeros((cells, 1), F32)
+    ranks = []
+    for c, chunk in enumerate(chunks):
+        earlier = prefix[cells * c : cells * (c + 1), :] + running
+        ranks.append(jnp.sum(chunk * earlier, axis=0, keepdims=True))
+        running = running + jnp.sum(chunk, axis=1, keepdims=True)
+    rank = jnp.concatenate(ranks, axis=1)
+    needed = jnp.broadcast_to(jnp.floor((running + (TILE - 1)) * (1.0 / TILE)), (cells, 128))
+    lower = (iota((cells, cells), 1) < iota((cells, cells), 0)).astype(F32).astype(BF16)
+    start = dot_nn(lower, needed.astype(BF16))
+    inside = jnp.floor(rank * (1.0 / TILE))
+    tile_row = jnp.sum(onehot * start[:, 0:1], axis=0, keepdims=True) + inside
+    place_row = rank - inside * TILE
+    meta_ref[...] = jnp.concatenate(
+        [tile_row, place_row, jnp.zeros((6, segments), F32)], axis=0
+    )
+    ends = start[:, 0:1] + needed[:, 0:1]
+    owner = jnp.sum(
+        (ends <= iota((cells, tile_cell_ref.shape[1]), 1).astype(F32)).astype(F32),
+        axis=0,
+        keepdims=True,
+    )
+    owner = jnp.minimum(owner, cells - 1.0).astype(jnp.int32)
+    tile_cell_ref[...] = jnp.broadcast_to(owner, tile_cell_ref.shape)
+    tile_start_ref[0:cells, :] = start.astype(jnp.int32)
+    tile_start_ref[cells : cells + 8, :] = jnp.broadcast_to(
+        ends[cells - 1 : cells, :], (8, 128)
+    ).astype(jnp.int32)
+
+    mask = slot_mask(place_row)
+    place = tile_onehot(tile_row, tiles)
+    lengths = length_ref[...]
+    near = jnp.zeros((1, rays), F32)
+    nears, extents = [], []
+    for k in range(crossings):
+        nears.append(near)
+        extents.append(lengths[k : k + 1, :])
+        near = near + lengths[k : k + 1, :]
+    rows = [
+        jnp.concatenate([geometry_ref[c : c + 1, :]] * crossings, axis=1) for c in range(6)
+    ]
+    rows += [jnp.concatenate(nears, axis=1), jnp.concatenate(extents, axis=1)]
+    wide = pick_nt(place, jnp.concatenate([mask * row for row in rows], axis=0))
+    wide = pick_nn(wide, lane_select(8, lanes))
+    channel = [wide[:, lanes * c : lanes * (c + 1)] for c in range(8)]
+    turned = jitter_ref[...].T
+    offsets = jnp.concatenate(
+        [turned[samples * k : samples * (k + 1), :] for k in range(crossings)], axis=1
+    )
+    dealt = jnp.concatenate([mask * offsets[i : i + 1, :] for i in range(samples)], axis=0)
+    jitter = pick_nt(place, dealt)
+    step = (iota((tiles, lanes), 1) // TILE).astype(F32)
+    near, extent = channel[6], channel[7]
+    depths = near + extent * (step + jitter) / samples
+    following = pltpu.roll(depths, lanes - TILE, 1)
+    ending = jnp.where(iota((tiles, lanes), 1) >= lanes - TILE, near + extent, following)
+    spacing_ref[...] = ending - depths
+    for c in range(3):
+        put_channel(position_ref, c, channel[c] + depths * channel[3 + c])
+    put_channel(position_ref, 3, jnp.ones((tiles, lanes), F32))
+    for c in range(4, 8):
+        put_channel(position_ref, c, jnp.zeros((tiles, lanes), F32))
+    turns = frequency_ref[...] * 0.15915494309189535
+    turns = jnp.concatenate([turns, turns], axis=1)
+    features = turns.shape[1]
+    quarter = jnp.where(iota((1, features), 1) < features // 2, -0.25, 0.0)
+    block = jnp.concatenate([turns, quarter, jnp.zeros((4, features), F32)], axis=0)
+    high, mid, low = [part.astype(F32) for part in split3(block)]
+    stack = [high, high, high, mid, mid, low, jnp.zeros((features - 48, features), F32)]
+    factor_ref[...] = jnp.concatenate(stack, axis=0).T[:, 0:48].astype(BF16)
+
+
+def encode(position_ref, factor, encoded_ref, some):
+    phases = []
+    for t in some:
         high, mid, low = split3(get_tile(position_ref, t))
         high, mid, low = high.astype(F32), mid.astype(F32), low.astype(F32)
         points = jnp.concatenate([high, mid, low, high, mid, high], axis=0).astype(BF16)
-        phase = dot_nn(factor, points)
+        phases.append(dot_nn(factor, points))
+    for t, phase in zip(some, phases):
         phase = phase - jnp.round(phase)
         square = phase * phase
-        value = jnp.full_like(square, COS[5])
-        for c in (4, 3, 2, 1, 0):
+        value = square * COS[5] + COS[4]
+        for c in (3, 2, 1, 0):
             value = value * square + COS[c]
-        encoded_ref[u] = value.astype(BF16)
+        encoded_ref[t] = value.astype(BF16)
 
 
 def step_kernel(
     cells,
     samples,
-    num_cell,
     tile_cell_ref,
     tile_start_ref,
-    near_ref,
-    flip_ref,
-    core_near_ref,
-    core_flip_ref,
-    encoded_ref,
     meta_ref,
     cells_ref,
     spacing_ref,
+    position_ref,
+    factor_ref,
     codes_ref,
     target_ref,
-    rendered_ref,
-    codes_grad_ref,
-    keep_ref,
-    send_ref,
-    first_ref,
-    second_ref,
-    forward1_ref,
-    forward2_ref,
-    backward2_ref,
-    head_ref,
-    head_turned_ref,
-    outputs_ref,
-    grads_ref,
-    sums_ref,
-    semaphore,
+    *refs,
 ):
+    weights, refs = refs[:cells], refs[cells:]
+    (
+        rendered_ref,
+        codes_grad_ref,
+        keep_ref,
+        send_ref,
+        encoded_ref,
+        first_ref,
+        second_ref,
+        forward1_ref,
+        forward2_ref,
+        backward2_ref,
+        head_ref,
+        head_turned_ref,
+        outputs_ref,
+        grads_ref,
+        sums_ref,
+        semaphore,
+    ) = refs
     tiles, lanes = spacing_ref.shape
     crossings, rays = cells_ref.shape
     segments = crossings * rays
-    width = codes_ref.shape[1]
+    width = codes_ref.shape[0]
     used = tile_start_ref[cells, 0]
     trips = (used + UNROLL - 1) // UNROLL
 
     appearance = []
-    for group, ref in enumerate((near_ref, flip_ref, core_near_ref, core_flip_ref)):
-        for s in range(num_cell):
-            v = group * num_cell + s
-            forward1_ref[v] = ref[s, 0:128, :].astype(BF16)
-            second = ref[s, 128:256, :]
-            forward2_ref[v] = second.astype(BF16)
-            backward2_ref[v] = second.T.astype(BF16)
-            tail = ref[s, HEAD_ROW:ROWS, :]
-            head = jnp.where(iota((8, 128), 0) < 4, tail, 0.0)
-            head_ref[v] = head.astype(BF16)
-            square = jnp.concatenate([head, jnp.zeros((120, 128), F32)], axis=0)
-            head_turned_ref[v] = square.T[:, 0:8].astype(BF16)
-            appearance.append(tail)
+    for v, ref in enumerate(weights):
+        forward1_ref[v] = ref[0:128, :].astype(BF16)
+        second = ref[128:256, :]
+        forward2_ref[v] = second.astype(BF16)
+        backward2_ref[v] = second.T.astype(BF16)
+        tail = ref[HEAD_ROW:ROWS, :]
+        head = jnp.where(iota((8, 128), 0) < 4, tail, 0.0)
+        head_ref[v] = head.astype(BF16)
+        square = jnp.concatenate([head, jnp.zeros((120, 128), F32)], axis=0)
+        head_turned_ref[v] = square.T[:, 0:8].astype(BF16)
+        appearance.append(tail)
     outputs_ref[...] = jnp.zeros_like(outputs_ref)
     sums_ref[...] = jnp.zeros_like(sums_ref)
 
+    factor = factor_ref[...]
+    encode(position_ref, factor, encoded_ref, range(UNROLL))
+
     def forward(trip, carry):
-        for u in range(UNROLL):
-            t = trip * UNROLL + u
-            v = tile_cell_ref[0, t]
-            first = jnp.maximum(dot_nn(forward1_ref[v], encoded_ref[t]), 0.0).astype(BF16)
+        following = jnp.minimum(trip + 1, trips - 1) * UNROLL
+        some = [trip * UNROLL + u for u in range(UNROLL)]
+        owner = [tile_cell_ref[0, t] for t in some]
+        firsts = [dot_nn(forward1_ref[v], encoded_ref[t]) for t, v in zip(some, owner)]
+        firsts = [jnp.maximum(first, 0.0).astype(BF16) for first in firsts]
+        for t, first in zip(some, firsts):
             first_ref[t] = first
-            second = jnp.maximum(dot_nn(forward2_ref[v], first), 0.0).astype(BF16)
+        seconds = [dot_nn(forward2_ref[v], first) for v, first in zip(owner, firsts)]
+        seconds = [jnp.maximum(second, 0.0).astype(BF16) for second in seconds]
+        for t, second in zip(some, seconds):
             second_ref[t] = second
-            put_tile(outputs_ref, t, dot_nn(head_ref[v], second))
+        outputs = [dot_nn(head_ref[v], second) for v, second in zip(owner, seconds)]
+        for t, output in zip(some, outputs):
+            put_tile(outputs_ref, t, output)
+        encode(position_ref, factor, encoded_ref, [following + u for u in range(UNROLL)])
         return carry
 
     lax.fori_loop(0, trips, forward, 0)
@@ -562,13 +571,7 @@
         axis=0,
     )[:, 0:width]
     codes = codes_ref[...]
-    shifts = lax.dot_general(
-        maps,
-        codes,
-        (((1,), (1,)), ((), ())),
-        precision=HIGHEST_PRECISION,
-        preferred_element_type=F32,
-    )
+    shifts = exact_nn(maps, codes)
     rows = [
         jnp.concatenate(
             [
@@ -651,8 +654,8 @@
         row = jnp.sum(mask * dealt[TILE * c : TILE * (c + 1), :], axis=0, keepdims=True)
         per_cell.append(sum(onehots[k] * crossed(row, k) for k in range(crossings)))
     per_cell = jnp.concatenate(per_cell, axis=0)
-    map_grads = exact_nn(per_cell, codes)
-    codes_grad_ref[...] = exact_nn(per_cell.T, maps)
+    map_grads = exact_nn(per_cell, codes.T)
+    codes_grad_ref[...] = exact_nn(maps.T, per_cell)
     for v in range(cells):
         for c in range(3):
             sums_ref[v, APP_ROW + c : APP_ROW + c + 1, 0:width] = map_grads[
@@ -660,26 +663,48 @@
             ]
 
     def backward(trip, carry):
-        for u in range(UNROLL):
-            t = trip * UNROLL + u
-            v = tile_cell_ref[0, t]
-            output = get_tile(grads_ref, t).astype(BF16)
-            first, second, encoded = first_ref[t], second_ref[t], encoded_ref[t]
-            second_grad = dot_nn(head_turned_ref[v], output)
-            second_grad = jnp.where(second.astype(F32) > 0, second_grad, 0.0).astype(BF16)
-            first_grad = dot_nn(backward2_ref[v], second_grad)
-            first_grad = jnp.where(first.astype(F32) > 0, first_grad, 0.0).astype(BF16)
-            sums_ref[v, HEAD_ROW:ROWS, :] += dot_nt(output, second)
-            sums_ref[v, 128:256, :] += dot_nt(first, second_grad)
-            sums_ref[v, 0:128, :] += dot_nt(encoded, first_grad)
+        some = [trip * UNROLL + u for u in range(UNROLL)]
+        owner = [tile_cell_ref[0, t] for t in some]
+        outputs = [get_tile(grads_ref, t).astype(BF16) for t in some]
+        second_grads = [dot_nn(head_turned_ref[v], output) for v, output in zip(owner, outputs)]
+        second_grads = [
+            jnp.where(second_ref[t].astype(F32) > 0, grad, 0.0).astype(BF16)
+            for t, grad in zip(some, second_grads)
+        ]
+        first_grads = [dot_nn(backward2_ref[v], grad) for v, grad in zip(owner, second_grads)]
+        first_grads = [
+            jnp.where(first_ref[t].astype(F32) > 0, grad, 0.0).astype(BF16)
+            for t, grad in zip(some, first_grads)
+        ]
+        head_parts = [dot_nt(output, second_ref[t]) for t, output in zip(some, outputs)]
+        second_parts = [dot_nt(first_ref[t], grad) for t, grad in zip(some, second_grads)]
+        first_parts = [dot_nt(encoded_ref[t], grad) for t, grad in zip(some, first_grads)]
+        for v, head, second, first in zip(owner, head_parts, second_parts, first_parts):
+            sums_ref[v, HEAD_ROW:ROWS, :] += head
+            sums_ref[v, 128:256, :] += second
+            sums_ref[v, 0:128, :] += first
         return carry
 
     lax.fori_loop(0, trips, backward, 0)
-    half = cells // 2
-    copies = [
-        pltpu.make_async_copy(sums_ref.at[pl.ds(0, half)], keep_ref, semaphore.at[0]),
-        pltpu.make_async_copy(sums_ref.at[pl.ds(half, half)], send_ref, semaphore.at[1]),
-    ]
+    num_cell = cells // 4
+    copies = []
+    for district in range(4):
+        members = sums_ref.at[pl.ds(district * num_cell, num_cell)]
+        total = sums_ref[district * num_cell]
+        for s in range(1, num_cell):
+            total = total + sums_ref[district * num_cell + s]
+        sums_ref[cells + district] = total
+        out_ref = (keep_ref, send_ref)[district // 2]
+        at = (district % 2) * (num_cell + 1)
+        for n, (source, sink) in enumerate(
+            [
+                (members, out_ref.at[pl.ds(at, num_cell)]),
+                (sums_ref.at[cells + district], out_ref.at[at + num_cell]),
+            ]
+        ):
+            copies.append(
+                pltpu.make_async_copy(source, sink, semaphore.at[district * 2 + n])
+            )
     for copy in copies:
         copy.start()
     for copy in copies:
@@ -707,7 +732,7 @@
     segments = rays * crossings
     width = appearance_codes.shape[1]
     lanes = TILE * samples
-    tiles = -(-(segments // TILE + cells) // 8) * 8
+    tiles = -(-(segments // TILE + cells) // UNROLL) * UNROLL
     me_cell, me_district = lax.axis_index("cell"), lax.axis_index("district")
 
     def along_cell(x, steps):
@@ -718,60 +743,47 @@
 
     own = pl.pallas_call(
         pack_kernel, out_shape=jax.ShapeDtypeStruct((ROWS, 128), F32), name="pack"
-    )(cell_layers, district_prior, head_weight, appearance_weight)
-    near = jnp.stack([own] + [along_cell(own, s) for s in range(1, num_cell)])
-    flipped = flip(near, 2)
-    core_near, core_flipped = flip(near, 1), flip(flipped, 1)
+    )(cell_layers, district_prior, head_weight, jnp.transpose(appearance_weight, (1, 0, 2)))
+    vmem, smem = pl.BlockSpec(memory_space=pltpu.VMEM), pl.BlockSpec(memory_space=pltpu.SMEM)
+    anywhere = pl.BlockSpec(memory_space=pl.ANY)
+    params = pltpu.CompilerParams(vmem_limit_bytes=VMEM_LIMIT)
+
+    near = [own] + [along_cell(own, s) for s in range(1, num_cell)]
+    flipped = [flip(piece, 2) for piece in near]
+    weights = near + flipped + [flip(piece, 1) for piece in near + flipped]
 
     away = (crossing % num_district) ^ me_district
     steps = (me_cell - crossing // num_district) % num_cell
-    virtual = ((away & 1) * 2 + (away >> 1)) * num_cell + steps
-    whole = lambda shape: pl.BlockSpec(shape, lambda i: (0,) * len(shape))
-    encoded, meta, spacing, tile_cell, tile_start = pl.pallas_call(
-        functools.partial(encode_kernel, cells, samples),
-        grid=(tiles // UNROLL,),
-        in_specs=[
-            whole((crossings, rays)),
-            whole((6, rays)),
-            whole((rays, crossings)),
-            whole((rays, crossings * samples)),
-            whole(frequencies.shape),
-        ],
-        out_specs=[
-            pl.BlockSpec((UNROLL, 128, lanes), lambda i: (i, 0, 0)),
-            whole((8, segments)),
-            whole((tiles, lanes)),
-            whole((8, 256)),
-            whole((cells + 8, 128)),
-        ],
+    virtual = (((away & 1) * 2 + (away >> 1)) * num_cell + steps).T
+    halves = lanes // 128
+    meta, spacing, tile_cell, tile_start, position, factor = pl.pallas_call(
+        functools.partial(deal_kernel, cells, samples),
         out_shape=[
-            jax.ShapeDtypeStruct((tiles, 128, lanes), BF16),
             jax.ShapeDtypeStruct((8, segments), F32),
             jax.ShapeDtypeStruct((tiles, lanes), F32),
             jax.ShapeDtypeStruct((8, 256), jnp.int32),
             jax.ShapeDtypeStruct((cells + 8, 128), jnp.int32),
+            jax.ShapeDtypeStruct((halves, tiles * 8, 128), F32),
+            jax.ShapeDtypeStruct((128, 48), BF16),
         ],
-        scratch_shapes=[
-            pltpu.VMEM((lanes // 128, tiles * 8, 128), F32),
-            pltpu.VMEM((128, 48), BF16),
-        ],
-        compiler_params=pltpu.CompilerParams(vmem_limit_bytes=VMEM_LIMIT),
-        name="encode",
-    )(virtual.T, ray_geometry, segment_length, jitter, frequencies)
-
-    vmem, smem = pl.BlockSpec(memory_space=pltpu.VMEM), pl.BlockSpec(memory_space=pltpu.SMEM)
-    half = cells // 2
+        compiler_params=params,
+        cost_estimate=pl.CostEstimate(flops=6 << 30, bytes_accessed=4 << 20, transcendentals=0),
+        name="deal",
+    )(virtual, ray_geometry, segment_length.T, jitter, frequencies)
+
+    half = 2 * (num_cell + 1)
     rendered, codes_grad, keep, send = pl.pallas_call(
-        functools.partial(step_kernel, cells, samples, num_cell),
-        in_specs=[smem, smem] + [vmem] * 10,
-        out_specs=[vmem, vmem, pl.BlockSpec(memory_space=pl.ANY), pl.BlockSpec(memory_space=pl.ANY)],
+        functools.partial(step_kernel, cells, samples),
+        in_specs=[smem, smem] + [vmem] * (7 + cells),
+        out_specs=[vmem, vmem, anywhere, anywhere],
         out_shape=[
             jax.ShapeDtypeStruct((3, rays), F32),
-            jax.ShapeDtypeStruct((rays, width), F32),
+            jax.ShapeDtypeStruct((width, rays), F32),
             jax.ShapeDtypeStruct((half, ROWS, 128), F32),
             jax.ShapeDtypeStruct((half, ROWS, 128), F32),
         ],
         scratch_shapes=[
+            pltpu.VMEM((tiles, 128, lanes), BF16),
             pltpu.VMEM((tiles, 128, lanes), BF16),
             pltpu.VMEM((tiles, 128, lanes), BF16),
             pltpu.VMEM((cells, 128, 128), BF16),
@@ -779,42 +791,49 @@
             pltpu.VMEM((cells, 128, 128), BF16),
             pltpu.VMEM((cells, 8, 128), BF16),
             pltpu.VMEM((cells, 128, 8), BF16),
-            pltpu.VMEM((lanes // 128, tiles * 8, 128), F32),
-            pltpu.VMEM((lanes // 128, tiles * 8, 128), F32),
-            pltpu.VMEM((cells, ROWS, 128), F32),
-            pltpu.SemaphoreType.DMA((2,)),
+            pltpu.VMEM((halves, tiles * 8, 128), F32),
+            pltpu.VMEM((halves, tiles * 8, 128), F32),
+            pltpu.VMEM((cells + 4, ROWS, 128), F32),
+            pltpu.SemaphoreType.DMA((8,)),
         ],
-        compiler_params=pltpu.CompilerParams(vmem_limit_bytes=VMEM_LIMIT),
+        compiler_params=params,
         name="step",
     )(
         tile_cell,
         tile_start,
-        near,
-        flipped,
-        core_near,
-        core_flipped,
-        encoded,
         meta,
-        virtual.T,
+        virtual,
         spacing,
-        appearance_codes,
+        position,
+        factor,
+        appearance_codes.T,
         target,
-    )
-
-    summed = keep + flip(send, 1)
-    summed = summed[:num_cell] + flip(summed[num_cell:], 2)
-    arrived = [along_cell(summed[s], -s) for s in range(1, num_cell)]
-    own_sum = summed[0] + sum(arrived)
-    layers = own_sum[0:HEAD_ROW].reshape(2, 128, 128)
-    others = [along_cell(layers, s) for s in range(1, num_cell)]
-    prior = (layers + sum(others)) / num_cell
+        *weights,
+    )
+
+    crossed = flip(send, 1)
+    order = [num_cell, num_cell // 2]
+    order += [s for s in range(1, num_cell) if s != num_cell // 2] + [0]
+    far = num_cell + 1
+    pieces = {s: flip(keep[far + s] + crossed[far + s], 2) for s in order}
+    for s in order:
+        near_part, cross_part, other = lax.optimization_barrier((keep[s], crossed[s], pieces[s]))
+        pieces[s] = near_part + cross_part + other
+    prior = pieces[num_cell][0:HEAD_ROW]
+    bit = 1
+    while bit < num_cell:
+        prior = prior + lax.ppermute(prior, "cell", [(i, i ^ bit) for i in range(num_cell)])
+        bit *= 2
+    prior = (prior / num_cell).reshape(2, 128, 128)
+    arrived = [along_cell(pieces[s], -s) for s in order[1:-1]]
+    own_sum = pieces[0] + sum(arrived)
     return (
         rendered,
-        layers[None],
+        own_sum[0:HEAD_ROW].reshape(1, 2, 128, 128),
         prior[None],
         own_sum[None, HEAD_ROW : HEAD_ROW + 4],
         own_sum[None, APP_ROW : APP_ROW + 3, 0:width],
-        codes_grad,
+        codes_grad.T,
     )
 
 

time: 197 us -> 110 us (0.56)
  Pallas kernels: 111 us -> 47.8 us
  waiting for transfers between devices: 54.8 us -> 35.4 us
  local copies, waits for them, and re-layouts: 5.79 us -> 2.63 us
    pallas_call x2, Pallas kernels: 110 us -> 46.1 us  [the longest x1 41.8 us: resident(): pl.pallas_call(functools.partial(step_kernel, cells, samples), in_specs=[...]
    ppermute x9 -> x6, waiting for transfers between devices: 27.2 us -> 16.4 us  [along_cell(): lax.ppermute(x, 'cell', [(i, (i + steps) % num_cell) for i in range(num_c...]
    ppermute x9 -> x6, starting transfers between devices: 16.2 us -> 7.26 us  [along_cell(): lax.ppermute(x, 'cell', [(i, (i + steps) % num_cell) for i in range(num_c...]
    ppermute x5 -> x18, waiting for transfers between devices: 27.6 us -> 18.8 us  [flip(): lax.ppermute(x, 'district', [(i, i ^ bit) for i in range(num_district)])]
    ppermute x5 -> x18, starting transfers between devices: 3.68 us -> 11.7 us  [flip(): lax.ppermute(x, 'district', [(i, i ^ bit) for i in range(num_district)])]
    unnamed x23 -> x31, local copies, waits for them, and re-layouts: 5.13 us -> 1.37 us
  transfers between devices with their start and end apart: 14 -> 26, of which waited for: 9 -> 14; matrix products, arithmetic and copies ran while one was open for 2% -> 3% of each run, Pallas kernels for 12% -> 4%
where the time goes in v2:
time: 110 us
  Pallas kernels  47.8 us (43%)
  waiting for transfers between devices  35.4 us (32%)
  starting transfers between devices  19.8 us (18%)
  other arithmetic  3.68 us (3%)
  local copies, waits for them, and re-layouts  2.63 us (2%)
    pallas_call x1, Pallas kernels, resident(): pl.pallas_call(functools.partial(step_kernel, cells, samples), in_specs=[...  41.8 us
    ppermute x18, waiting for transfers between devices, flip(): lax.ppermute(x, 'district', [(i, i ^ bit) for i in range(num_district)])  18.8 us
    ppermute x6, waiting for transfers between devices, along_cell(): lax.ppermute(x, 'cell', [(i, (i + steps) % num_cell) for i in range(num_c...  16.4 us
    ppermute x18, starting transfers between devices, flip(): lax.ppermute(x, 'district', [(i, i ^ bit) for i in range(num_district)])  11.7 us
    ppermute x6, starting transfers between devices, along_cell(): lax.ppermute(x, 'cell', [(i, (i + steps) % num_cell) for i in range(num_c...  7.26 us
    pallas_call x1, Pallas kernels, resident(): pl.pallas_call(functools.partial(deal_kernel, cells, samples), out_shape=...  4.34 us
  transfers between devices with their start and end apart: 26, of which 14 were waited for; matrix products, arithmetic and copies ran while one was open for 3% of the time, Pallas kernels for 4%

profile of v2, /device:TPU:0, one launch (start us, length us, event | category | flops | bytes accessed | tf_op | source)
XLA Modules:
  0.0 110.2 jit_solution(83267337966223611)
XLA Ops:
  0.6 1.6 %pack.1.refs_0_ = f32[264,128]{1,0:T(8,128)} custom-call(bf16[1,2,128,128]{3,2,1,0:T(8,128)(2,1)} %layers_ref.1, bf16[1,2,128,128]{3,2,1,0:T(8,128)(2,1)} %prior_ref.1, bf16[1,4,128]{2,1,0:T(4,128)(2,1)} %head_ref.1, f32[3,1,48]{2,1,0:T(1,128)} %bitcast.45), custom_call_target="tpu_custom_call" | custom-call | tf_op jit(solution)/shard_map/pack/pallas_call | solution.py:744
  2.3 5.0 %collective-permute-start.2 = (f32[264,128]{1,0:T(8,128)}, f32[264,128]{1,0:T(8,128)S(1)}, u32[]{:S(2)}, u32[]{:S(2)}) collective-permute-start(f32[264,128]{1,0:T(8,128)} %pack.1.refs_0_), channel_id=1, source_target_pairs={{0,12},{4,0},{8,4},{12,8},{1,13},{5,1},{9,5},{13,9},{2,14},{6,2},{... | collective-permute-start | bytes 405512 | tf_op jit(solution)/shard_map/ppermute | solution.py:739
  7.3 1.5 %collective-permute-start.3 = (f32[264,128]{1,0:T(8,128)}, f32[264,128]{1,0:T(8,128)S(1)}, u32[]{:S(2)}, u32[]{:S(2)}) collective-permute-start(f32[264,128]{1,0:T(8,128)} %pack.1.refs_0_), channel_id=1, source_target_pairs={{0,2},{1,3},{2,0},{3,1},{4,6},{5,7},{6,4},{7,5},{8,10},{9,11},{10,... | collective-permute-start | bytes 405512 | tf_op jit(solution)/shard_map/ppermute | solution.py:742
  8.8 1.0 collective-permute-start
  9.8 1.4 %collective-permute-done.2.refs_3_ = f32[264,128]{1,0:T(8,128)S(1)} collective-permute-done((f32[264,128]{1,0:T(8,128)}, f32[264,128]{1,0:T(8,128)S(1)}, u32[]{:S(2)}, u32[]{:S(2)}) %collective-permute-start.2) | collective-permute-done | bytes 135200 | tf_op jit(solution)/shard_map/ppermute | solution.py:739
  11.2 2.0 %collective-permute-start.6 = (f32[264,128]{1,0:T(8,128)S(1)}, f32[264,128]{1,0:T(8,128)S(1)}, u32[]{:S(2)}, u32[]{:S(2)}) collective-permute-start(f32[264,128]{1,0:T(8,128)S(1)} %collective-permute-done.2.refs_3_), channel_id=1, source_target_pairs={{0,2},{1,3},{2,0},{3,1},{4,6},{5,7},{6,4},{7,5},{8,10},{9,11},{10,... | collective-permute-start | bytes 405512 | tf_op jit(solution)/shard_map/ppermute | solution.py:742
  13.5 6.4 %collective-permute-done.1.refs_2_ = f32[264,128]{1,0:T(8,128)S(1)} collective-permute-done((f32[264,128]{1,0:T(8,128)}, f32[264,128]{1,0:T(8,128)S(1)}, u32[]{:S(2)}, u32[]{:S(2)}) %collective-permute-start.1) | collective-permute-done | bytes 135200 | tf_op jit(solution)/shard_map/ppermute | solution.py:739
  20.0 1.2 %collective-permute-start.5 = (f32[264,128]{1,0:T(8,128)S(1)}, f32[264,128]{1,0:T(8,128)S(1)}, u32[]{:S(2)}, u32[]{:S(2)}) collective-permute-start(f32[264,128]{1,0:T(8,128)S(1)} %collective-permute-done.1.refs_2_), channel_id=1, source_target_pairs={{0,2},{1,3},{2,0},{3,1},{4,6},{5,7},{6,4},{7,5},{8,10},{9,11},{10,... | collective-permute-start | bytes 405512 | tf_op jit(solution)/shard_map/ppermute | solution.py:742
  22.0 1.3 %fusion.9.cells_ref = s32[4,256]{1,0:T(4,128)} fusion(s32[256,4]{0,1:T(4,128)} %param.16, s32[]{:T(128)S(6)} %axis_index.25, s32[]{:T(128)S(6)} %axis_index.22), kind=kLoop, calls=%fused_computation.39 | loop fusion | flops 38912 | bytes 8200 | tf_op jit(solution)/shard_map/transpose | solution.py:757
  23.9 2.5 %collective-permute-done.5.refs_6_ = f32[264,128]{1,0:T(8,128)S(1)} collective-permute-done((f32[264,128]{1,0:T(8,128)S(1)}, f32[264,128]{1,0:T(8,128)S(1)}, u32[]{:S(2)}, u32[]{:S(2)}) %collective-permute-start.5) | collective-permute-done | bytes 135200 | tf_op jit(solution)/shard_map/ppermute | solution.py:742
  26.4 2.0 %collective-permute-done.4.refs_5_ = f32[264,128]{1,0:T(8,128)S(1)} collective-permute-done((f32[264,128]{1,0:T(8,128)S(1)}, f32[264,128]{1,0:T(8,128)S(1)}, u32[]{:S(2)}, u32[]{:S(2)}) %collective-permute-start.4) | collective-permute-done | bytes 135200 | tf_op jit(solution)/shard_map/ppermute | solution.py:742
  28.4 4.3 %deal.1 = (f32[8,1024]{1,0:T(8,128)}, f32[144,256]{1,0:T(8,128)}, s32[8,256]{1,0:T(8,128)}, s32[24,128]{1,0:T(8,128)}, f32[2,1152,128]{2,1,0:T(8,128)}, /*index=5*/bf16[128,48]{1,0:T(8,128)(2,1)}) custom-call(s32[4,256]{1,0:T(4,128)} %fusion.9.cells_ref, f32[6,256]{1,0:T(8,128)} %geometry_ref.1, f32[4,256]{1,0:T(4,128)} %bitcast.47, f32[256,128]{1,0:T(8,128)} %jitter_ref.1, ...), custom_call_target="tpu_custom_call" | custom-call | flops 6442450944 | bytes 4194304 | tf_op jit(solution)/shard_map/deal/pallas_call | solution.py:759
  33.7 41.8 %step.1 = (f32[3,256]{1,0:T(4,128)}, f32[48,256]{1,0:T(8,128)}, f32[10,264,128]{2,1,0:T(8,128)}, f32[10,264,128]{2,1,0:T(8,128)}) custom-call(s32[8,256]{1,0:T(8,128)} %get-tuple-element.31.tile_cell_ref, s32[24,128]{1,0:T(8,128)} %get-tuple-element.32.tile_start_ref, f32[8,1024]{1,0:T(8,128)} %get-tuple-element.33.meta_ref, s32[4,256]{1,0:T(4,128)} %fusion.9.cells_ref, ...), custom_call_target="tpu_custom_call" | custom-call | tf_op jit(solution)/shard_map/step/pallas_call | solution.py:775
  76.0 2.9 %collective-permute-done.15 = f32[10,264,128]{2,1,0:T(8,128)S(1)} collective-permute-done((f32[10,264,128]{2,1,0:T(8,128)}, f32[10,264,128]{2,1,0:T(8,128)S(1)}, u32[]{:S(2)}, u32[]{:S(2)}) %collective-permute-start.15) | collective-permute-done | bytes 1351712 | tf_op jit(solution)/shard_map/ppermute | solution.py:742
  79.0 1.5 %fusion = (f32[264,128]{1,0:T(8,128)S(1)}, f32[264,128]{1,0:T(8,128)S(1)}, f32[264,128]{1,0:T(8,128)S(1)}, f32[264,128]{1,0:T(8,128)S(1)}, f32[264,128]{1,0:T(8,...) fusion(f32[10,264,128]{2,1,0:T(8,128)S(1)} %collective-permute-, ...), kind=kLoop, calls=%fused_computation.1 | loop fusion | flops 168960 | bytes 4460544 | tf_op jit(solution)/shard_map/add | solution.py:818
  81.5 1.1 %collective-permute-start.21 = (f32[264,128]{1,0:T(8,128)S(1)}, f32[264,128]{1,0:T(8,128)S(1)}, u32[]{:S(2)}, u32[]{:S(2)}) collective-permute-start(f32[264,128]{1,0:T(8,128)S(1)} %get-tuple-element.63), channel_id=1, source_target_pairs={{0,2},{1,3},{2,0},{3,1},{4,6},{5,7},{6,4},{7,5},{8,10},{9,11},{10,... | collective-permute-start | bytes 405512 | tf_op jit(solution)/shard_map/ppermute | solution.py:742
  83.5 1.1 %collective-permute-start.17 = (f32[264,128]{1,0:T(8,128)S(1)}, f32[264,128]{1,0:T(8,128)S(1)}, u32[]{:S(2)}, u32[]{:S(2)}) collective-permute-start(f32[264,128]{1,0:T(8,128)S(1)} %get-tuple-element.65), channel_id=1, source_target_pairs={{0,2},{1,3},{2,0},{3,1},{4,6},{5,7},{6,4},{7,5},{8,10},{9,11},{10,... | collective-permute-start | bytes 405512 | tf_op jit(solution)/shard_map/ppermute | solution.py:742
  85.5 1.4 %collective-permute-done.23 = f32[264,128]{1,0:T(8,128)S(1)} collective-permute-done((f32[264,128]{1,0:T(8,128)S(1)}, f32[264,128]{1,0:T(8,128)S(1)}, u32[]{:S(2)}, u32[]{:S(2)}) %collective-permute-start.23) | collective-permute-done | bytes 135200 | tf_op jit(solution)/shard_map/ppermute | solution.py:742
  87.1 2.8 %collective-permute-done.21 = f32[264,128]{1,0:T(8,128)S(1)} collective-permute-done((f32[264,128]{1,0:T(8,128)S(1)}, f32[264,128]{1,0:T(8,128)S(1)}, u32[]{:S(2)}, u32[]{:S(2)}) %collective-permute-start.21) | collective-permute-done | bytes 135200 | tf_op jit(solution)/shard_map/ppermute | solution.py:742
  90.0 2.8 %collective-permute-done.19 = f32[264,128]{1,0:T(8,128)S(1)} collective-permute-done((f32[264,128]{1,0:T(8,128)S(1)}, f32[264,128]{1,0:T(8,128)S(1)}, u32[]{:S(2)}, u32[]{:S(2)}) %collective-permute-start.19) | collective-permute-done | bytes 135200 | tf_op jit(solution)/shard_map/ppermute | solution.py:742
  92.8 1.1 collective-permute-start.20
  93.9 1.8 %collective-permute-done.17 = f32[264,128]{1,0:T(8,128)S(1)} collective-permute-done((f32[264,128]{1,0:T(8,128)S(1)}, f32[264,128]{1,0:T(8,128)S(1)}, u32[]{:S(2)}, u32[]{:S(2)}) %collective-permute-start.17) | collective-permute-done | bytes 135200 | tf_op jit(solution)/shard_map/ppermute | solution.py:742
  95.8 2.2 %collective-permute-done.16 = f32[264,128]{1,0:T(8,128)S(1)} collective-permute-done((f32[264,128]{1,0:T(8,128)S(1)}, f32[264,128]{1,0:T(8,128)S(1)}, u32[]{:S(2)}, u32[]{:S(2)}) %collective-permute-start.16) | collective-permute-done | bytes 135200 | tf_op jit(solution)/shard_map/ppermute | solution.py:742
  99.5 7.9 %collective-permute-done.18 = f32[264,128]{1,0:T(8,128)S(1)} collective-permute-done((f32[264,128]{1,0:T(8,128)S(1)}, f32[264,128]{1,0:T(8,128)S(1)}, u32[]{:S(2)}, u32[]{:S(2)}) %collective-permute-start.18) | collective-permute-done | bytes 135200 | tf_op jit(solution)/shard_map/ppermute | solution.py:739
  (75 shorter events, 10.5 us)
Async XLA Ops:
  2.3 8.9 %collective-permute-start.2 = (f32[264,128]{1,0:T(8,128)}, f32[264,128]{1,0:T(8,128)S(1)}, u32[]{:S(2)}, u32[]{:S(2)}) collective-permute-start(f32[264,128]{1,0:T(8,128)} %pack.1.refs_0_), channel_id=1, source_target_pairs={{0,12},{4,0},{8,4},{12,8},{1,13},{5,1},{9,5},{13,9},{2,14},{6,2},{... | collective-permute-start | bytes 405512 | tf_op jit(solution)/shard_map/ppermute | solution.py:739
  7.3 6.2 %collective-permute-start.3 = (f32[264,128]{1,0:T(8,128)}, f32[264,128]{1,0:T(8,128)S(1)}, u32[]{:S(2)}, u32[]{:S(2)}) collective-permute-start(f32[264,128]{1,0:T(8,128)} %pack.1.refs_0_), channel_id=1, source_target_pairs={{0,2},{1,3},{2,0},{3,1},{4,6},{5,7},{6,4},{7,5},{8,10},{9,11},{10,... | collective-permute-start | bytes 405512 | tf_op jit(solution)/shard_map/ppermute | solution.py:742
  8.8 11.2 %collective-permute-start.1 = (f32[264,128]{1,0:T(8,128)}, f32[264,128]{1,0:T(8,128)S(1)}, u32[]{:S(2)}, u32[]{:S(2)}) collective-permute-start(f32[264,128]{1,0:T(8,128)} %pack.1.refs_0_), channel_id=1, source_target_pairs={{0,8},{4,12},{8,0},{12,4},{1,9},{5,13},{9,1},{13,5},{2,10},{6,14},... | collective-permute-start | bytes 405512 | tf_op jit(solution)/shard_map/ppermute | solution.py:739
  8.8 12.3 %collective-permute-start = (f32[264,128]{1,0:T(8,128)}, f32[264,128]{1,0:T(8,128)S(1)}, u32[]{:S(2)}, u32[]{:S(2)}) collective-permute-start(f32[264,128]{1,0:T(8,128)} %pack.1.refs_0_), channel_id=1, source_target_pairs={{0,4},{4,8},{8,12},{12,0},{1,5},{5,9},{9,13},{13,1},{2,6},{6,10},{... | collective-permute-start | bytes 405512 | tf_op jit(solution)/shard_map/ppermute | solution.py:739
  11.2 12.1 %collective-permute-start.10 = (f32[264,128]{1,0:T(8,128)S(1)}, f32[264,128]{1,0:T(8,128)S(1)}, u32[]{:S(2)}, u32[]{:S(2)}) collective-permute-start(f32[264,128]{1,0:T(8,128)S(1)} %collective-permute-done.2.refs_3_), channel_id=1, source_target_pairs={{0,1},{1,0},{2,3},{3,2},{4,5},{5,4},{6,7},{7,6},{8,9},{9,8},{10,11... | collective-permute-start | bytes 405512 | tf_op jit(solution)/shard_map/ppermute | solution.py:742
  11.2 12.6 %collective-permute-start.6 = (f32[264,128]{1,0:T(8,128)S(1)}, f32[264,128]{1,0:T(8,128)S(1)}, u32[]{:S(2)}, u32[]{:S(2)}) collective-permute-start(f32[264,128]{1,0:T(8,128)S(1)} %collective-permute-done.2.refs_3_), channel_id=1, source_target_pairs={{0,2},{1,3},{2,0},{3,1},{4,6},{5,7},{6,4},{7,5},{8,10},{9,11},{10,... | collective-permute-start | bytes 405512 | tf_op jit(solution)/shard_map/ppermute | solution.py:742
  13.5 9.8 %collective-permute-start.11 = (f32[264,128]{1,0:T(8,128)S(1)}, f32[264,128]{1,0:T(8,128)S(1)}, u32[]{:S(2)}, u32[]{:S(2)}) collective-permute-start(f32[264,128]{1,0:T(8,128)S(1)} %collective-permute-done.3.refs_4_), channel_id=1, source_target_pairs={{0,1},{1,0},{2,3},{3,2},{4,5},{5,4},{6,7},{7,6},{8,9},{9,8},{10,11... | collective-permute-start | bytes 405512 | tf_op jit(solution)/shard_map/ppermute | solution.py:742
  20.0 6.4 %collective-permute-start.5 = (f32[264,128]{1,0:T(8,128)S(1)}, f32[264,128]{1,0:T(8,128)S(1)}, u32[]{:S(2)}, u32[]{:S(2)}) collective-permute-start(f32[264,128]{1,0:T(8,128)S(1)} %collective-permute-done.1.refs_2_), channel_id=1, source_target_pairs={{0,2},{1,3},{2,0},{3,1},{4,6},{5,7},{6,4},{7,5},{8,10},{9,11},{10,... | collective-permute-start | bytes 405512 | tf_op jit(solution)/shard_map/ppermute | solution.py:742
  21.1 7.3 %collective-permute-start.4 = (f32[264,128]{1,0:T(8,128)S(1)}, f32[264,128]{1,0:T(8,128)S(1)}, u32[]{:S(2)}, u32[]{:S(2)}) collective-permute-start(f32[264,128]{1,0:T(8,128)S(1)} %collective-permute-done.refs_1_), channel_id=1, source_target_pairs={{0,2},{1,3},{2,0},{3,1},{4,6},{5,7},{6,4},{7,5},{8,10},{9,11},{10,... | collective-permute-start | bytes 405512 | tf_op jit(solution)/shard_map/ppermute | solution.py:742
  23.3 9.5 %collective-permute-start.9 = (f32[264,128]{1,0:T(8,128)S(1)}, f32[264,128]{1,0:T(8,128)S(1)}, u32[]{:S(2)}, u32[]{:S(2)}) collective-permute-start(f32[264,128]{1,0:T(8,128)S(1)} %collective-permute-done.1.refs_2_), channel_id=1, source_target_pairs={{0,1},{1,0},{2,3},{3,2},{4,5},{5,4},{6,7},{7,6},{8,9},{9,8},{10,11... | collective-permute-start | bytes 405512 | tf_op jit(solution)/shard_map/ppermute | solution.py:742
  23.3 9.5 %collective-permute-start.8 = (f32[264,128]{1,0:T(8,128)S(1)}, f32[264,128]{1,0:T(8,128)S(1)}, u32[]{:S(2)}, u32[]{:S(2)}) collective-permute-start(f32[264,128]{1,0:T(8,128)S(1)} %collective-permute-done.refs_1_), channel_id=1, source_target_pairs={{0,1},{1,0},{2,3},{3,2},{4,5},{5,4},{6,7},{7,6},{8,9},{9,8},{10,11... | collective-permute-start | bytes 405512 | tf_op jit(solution)/shard_map/ppermute | solution.py:742
  23.8 9.1 %collective-permute-start.14 = (f32[264,128]{1,0:T(8,128)S(1)}, f32[264,128]{1,0:T(8,128)S(1)}, u32[]{:S(2)}, u32[]{:S(2)}) collective-permute-start(f32[264,128]{1,0:T(8,128)S(1)} %collective-permute-done.6.refs_7_), channel_id=1, source_target_pairs={{0,1},{1,0},{2,3},{3,2},{4,5},{5,4},{6,7},{7,6},{8,9},{9,8},{10,11... | collective-permute-start | bytes 405512 | tf_op jit(solution)/shard_map/ppermute | solution.py:742
  26.4 6.5 %collective-permute-start.13 = (f32[264,128]{1,0:T(8,128)S(1)}, f32[264,128]{1,0:T(8,128)S(1)}, u32[]{:S(2)}, u32[]{:S(2)}) collective-permute-start(f32[264,128]{1,0:T(8,128)S(1)} %collective-permute-done.5.refs_6_), channel_id=1, source_target_pairs={{0,1},{1,0},{2,3},{3,2},{4,5},{5,4},{6,7},{7,6},{8,9},{9,8},{10,11... | collective-permute-start | bytes 405512 | tf_op jit(solution)/shard_map/ppermute | solution.py:742
  28.4 4.5 %collective-permute-start.12 = (f32[264,128]{1,0:T(8,128)S(1)}, f32[264,128]{1,0:T(8,128)S(1)}, u32[]{:S(2)}, u32[]{:S(2)}) collective-permute-start(f32[264,128]{1,0:T(8,128)S(1)} %collective-permute-done.4.refs_5_), channel_id=1, source_target_pairs={{0,1},{1,0},{2,3},{3,2},{4,5},{5,4},{6,7},{7,6},{8,9},{9,8},{10,11... | collective-permute-start | bytes 405512 | tf_op jit(solution)/shard_map/ppermute | solution.py:742
  80.5 6.5 %collective-permute-start.23 = (f32[264,128]{1,0:T(8,128)S(1)}, f32[264,128]{1,0:T(8,128)S(1)}, u32[]{:S(2)}, u32[]{:S(2)}) collective-permute-start(f32[264,128]{1,0:T(8,128)S(1)} %get-tuple-element.62), channel_id=1, source_target_pairs={{0,2},{1,3},{2,0},{3,1},{4,6},{5,7},{6,4},{7,5},{8,10},{9,11},{10,... | collective-permute-start | bytes 405512 | tf_op jit(solution)/shard_map/ppermute | solution.py:742
  81.5 8.4 %collective-permute-start.21 = (f32[264,128]{1,0:T(8,128)S(1)}, f32[264,128]{1,0:T(8,128)S(1)}, u32[]{:S(2)}, u32[]{:S(2)}) collective-permute-start(f32[264,128]{1,0:T(8,128)S(1)} %get-tuple-element.63), channel_id=1, source_target_pairs={{0,2},{1,3},{2,0},{3,1},{4,6},{5,7},{6,4},{7,5},{8,10},{9,11},{10,... | collective-permute-start | bytes 405512 | tf_op jit(solution)/shard_map/ppermute | solution.py:742
  82.6 10.2 %collective-permute-start.19 = (f32[264,128]{1,0:T(8,128)S(1)}, f32[264,128]{1,0:T(8,128)S(1)}, u32[]{:S(2)}, u32[]{:S(2)}) collective-permute-start(f32[264,128]{1,0:T(8,128)S(1)} %get-tuple-element.64), channel_id=1, source_target_pairs={{0,2},{1,3},{2,0},{3,1},{4,6},{5,7},{6,4},{7,5},{8,10},{9,11},{10,... | collective-permute-start | bytes 405512 | tf_op jit(solution)/shard_map/ppermute | solution.py:742
  83.5 12.2 %collective-permute-start.17 = (f32[264,128]{1,0:T(8,128)S(1)}, f32[264,128]{1,0:T(8,128)S(1)}, u32[]{:S(2)}, u32[]{:S(2)}) collective-permute-start(f32[264,128]{1,0:T(8,128)S(1)} %get-tuple-element.65), channel_id=1, source_target_pairs={{0,2},{1,3},{2,0},{3,1},{4,6},{5,7},{6,4},{7,5},{8,10},{9,11},{10,... | collective-permute-start | bytes 405512 | tf_op jit(solution)/shard_map/ppermute | solution.py:742
  84.6 13.4 %collective-permute-start.16 = (f32[264,128]{1,0:T(8,128)S(1)}, f32[264,128]{1,0:T(8,128)S(1)}, u32[]{:S(2)}, u32[]{:S(2)}) collective-permute-start(f32[264,128]{1,0:T(8,128)S(1)} %get-tuple-element.66), channel_id=1, source_target_pairs={{0,2},{1,3},{2,0},{3,1},{4,6},{5,7},{6,4},{7,5},{8,10},{9,11},{10,... | collective-permute-start | bytes 405512 | tf_op jit(solution)/shard_map/ppermute | solution.py:742
  87.0 11.0 %collective-permute-start.24 = (f32[256,128]{1,0:T(8,128)S(1)}, f32[256,128]{1,0:T(8,128)S(1)}, u32[]{:S(2)}, u32[]{:S(2)}) collective-permute-start(f32[256,128]{1,0:T(8,128)S(1)} %slice_add_fusion.5), channel_id=1, source_target_pairs={{0,4},{4,0},{8,12},{12,8},{1,5},{5,1},{9,13},{13,9},{2,6},{6,2},{1... | collective-permute-start | bytes 393224 | tf_op jit(solution)/shard_map/ppermute | solution.py:825
  89.9 8.9 %collective-permute-start.22 = (f32[264,128]{1,0:T(8,128)S(1)}, f32[264,128]{1,0:T(8,128)S(1)}, u32[]{:S(2)}, u32[]{:S(2)}) collective-permute-start(f32[264,128]{1,0:T(8,128)S(1)} %add_add_fusion.1), channel_id=1, source_target_pairs={{0,4},{4,8},{8,12},{12,0},{1,5},{5,9},{9,13},{13,1},{2,6},{6,10},{... | collective-permute-start | bytes 405512 | tf_op jit(solution)/shard_map/ppermute | solution.py:739
  92.8 6.7 %collective-permute-start.20 = (f32[264,128]{1,0:T(8,128)S(1)}, f32[264,128]{1,0:T(8,128)S(1)}, u32[]{:S(2)}, u32[]{:S(2)}) collective-permute-start(f32[264,128]{1,0:T(8,128)S(1)} %add_add_fusion.2), channel_id=1, source_target_pairs={{0,12},{4,0},{8,4},{12,8},{1,13},{5,1},{9,5},{13,9},{2,14},{6,2},{... | collective-permute-start | bytes 405512 | tf_op jit(solution)/shard_map/ppermute | solution.py:739
  95.7 11.7 %collective-permute-start.18 = (f32[264,128]{1,0:T(8,128)S(1)}, f32[264,128]{1,0:T(8,128)S(1)}, u32[]{:S(2)}, u32[]{:S(2)}) collective-permute-start(f32[264,128]{1,0:T(8,128)S(1)} %add_add_fusion.3), channel_id=1, source_target_pairs={{0,8},{4,12},{8,0},{12,4},{1,9},{5,13},{9,1},{13,5},{2,10},{6,14},... | collective-permute-start | bytes 405512 | tf_op jit(solution)/shard_map/ppermute | solution.py:739
  98.0 11.5 %collective-permute-start.25 = (f32[256,128]{1,0:T(8,128)S(1)}, f32[256,128]{1,0:T(8,128)S(1)}, u32[]{:S(2)}, u32[]{:S(2)}) collective-permute-start(f32[256,128]{1,0:T(8,128)S(1)} %add.119), channel_id=1, source_target_pairs={{0,8},{4,12},{8,0},{12,4},{1,9},{5,13},{9,1},{13,5},{2,10},{6,14},... | collective-permute-start | bytes 393224 | tf_op jit(solution)/shard_map/ppermute | solution.py:825
  (17 other events, 136.5 us)

commit v3 on v2

--- a/solution.py
+++ b/solution.py
@@ -340,7 +340,7 @@
         ref[h, rows, :] = x[:, 128 * h : 128 * (h + 1)]
 
 
-def pack_kernel(layers_ref, prior_ref, head_ref, app_ref, out_ref):
+def pack_kernel(layers_ref, prior_ref, head_ref, app_ref, out_ref, again_ref):
     for layer in range(2):
         both = layers_ref[0, layer].astype(F32) + prior_ref[0, layer].astype(F32)
         out_ref[128 * layer : 128 * (layer + 1), :] = both.T
@@ -348,6 +348,7 @@
     out_ref[HEAD_ROW : HEAD_ROW + 4, :] = head_ref[0].astype(F32)
     for c in range(3):
         out_ref[APP_ROW + c : APP_ROW + c + 1, 0 : app_ref.shape[2]] = app_ref[c]
+    again_ref[...] = out_ref[...]
 
 
 def slot_mask(place_row):
@@ -380,13 +381,16 @@
     length_ref,
     jitter_ref,
     frequency_ref,
+    own_ref,
     meta_ref,
     spacing_ref,
     tile_cell_ref,
     tile_start_ref,
     position_ref,
     factor_ref,
+    passed_ref,
 ):
+    del own_ref, passed_ref
     tiles = spacing_ref.shape[0]
     lanes = TILE * samples
     crossings, rays = cells_ref.shape
@@ -668,12 +672,12 @@
         outputs = [get_tile(grads_ref, t).astype(BF16) for t in some]
         second_grads = [dot_nn(head_turned_ref[v], output) for v, output in zip(owner, outputs)]
         second_grads = [
-            jnp.where(second_ref[t].astype(F32) > 0, grad, 0.0).astype(BF16)
+            jnp.where(second_ref[t] > 0, grad.astype(BF16), jnp.zeros((), BF16))
             for t, grad in zip(some, second_grads)
         ]
         first_grads = [dot_nn(backward2_ref[v], grad) for v, grad in zip(owner, second_grads)]
         first_grads = [
-            jnp.where(first_ref[t].astype(F32) > 0, grad, 0.0).astype(BF16)
+            jnp.where(first_ref[t] > 0, grad.astype(BF16), jnp.zeros((), BF16))
             for t, grad in zip(some, first_grads)
         ]
         head_parts = [dot_nt(output, second_ref[t]) for t, output in zip(some, outputs)]
@@ -735,29 +739,26 @@
     tiles = -(-(segments // TILE + cells) // UNROLL) * UNROLL
     me_cell, me_district = lax.axis_index("cell"), lax.axis_index("district")
 
-    def along_cell(x, steps):
-        return lax.ppermute(x, "cell", [(i, (i + steps) % num_cell) for i in range(num_cell)])
-
-    def flip(x, bit):
-        return lax.ppermute(x, "district", [(i, i ^ bit) for i in range(num_district)])
-
-    own = pl.pallas_call(
-        pack_kernel, out_shape=jax.ShapeDtypeStruct((ROWS, 128), F32), name="pack"
+    def flip(x, bits, axis="district"):
+        return lax.ppermute(x, axis, [(i, i ^ bits) for i in range(lax.axis_size(axis))])
+
+    own, again = pl.pallas_call(
+        pack_kernel, out_shape=[jax.ShapeDtypeStruct((ROWS, 128), F32)] * 2, name="pack"
     )(cell_layers, district_prior, head_weight, jnp.transpose(appearance_weight, (1, 0, 2)))
     vmem, smem = pl.BlockSpec(memory_space=pltpu.VMEM), pl.BlockSpec(memory_space=pltpu.SMEM)
     anywhere = pl.BlockSpec(memory_space=pl.ANY)
     params = pltpu.CompilerParams(vmem_limit_bytes=VMEM_LIMIT)
 
-    near = [own] + [along_cell(own, s) for s in range(1, num_cell)]
-    flipped = [flip(piece, 2) for piece in near]
-    weights = near + flipped + [flip(piece, 1) for piece in near + flipped]
-
     away = (crossing % num_district) ^ me_district
-    steps = (me_cell - crossing // num_district) % num_cell
+    steps = (crossing // num_district) ^ me_cell
     virtual = (((away & 1) * 2 + (away >> 1)) * num_cell + steps).T
     halves = lanes // 128
-    meta, spacing, tile_cell, tile_start, position, factor = pl.pallas_call(
+    default = pl.BlockSpec()
+    meta, spacing, tile_cell, tile_start, position, factor, passed = pl.pallas_call(
         functools.partial(deal_kernel, cells, samples),
+        in_specs=[default] * 5 + [anywhere],
+        out_specs=[default] * 6 + [anywhere],
+        input_output_aliases={5: 6},
         out_shape=[
             jax.ShapeDtypeStruct((8, segments), F32),
             jax.ShapeDtypeStruct((tiles, lanes), F32),
@@ -765,11 +766,18 @@
             jax.ShapeDtypeStruct((cells + 8, 128), jnp.int32),
             jax.ShapeDtypeStruct((halves, tiles * 8, 128), F32),
             jax.ShapeDtypeStruct((128, 48), BF16),
+            jax.ShapeDtypeStruct((ROWS, 128), F32),
         ],
         compiler_params=params,
         cost_estimate=pl.CostEstimate(flops=6 << 30, bytes_accessed=4 << 20, transcendentals=0),
         name="deal",
-    )(virtual, ray_geometry, segment_length.T, jitter, frequencies)
+    )(virtual, ray_geometry, segment_length.T, jitter, frequencies, again)
+    near = [own]
+    for s in range(1, num_cell):
+        near.append(flip(near[s & (s - 1)] if s > 1 else passed, s & -s, "cell"))
+    flipped = [flip(piece, 2) for piece in near]
+    weights = near + flipped + [flip(piece, 1) for piece in near + flipped]
+
 
     half = 2 * (num_cell + 1)
     rendered, codes_grad, keep, send = pl.pallas_call(
@@ -822,10 +830,10 @@
     prior = pieces[num_cell][0:HEAD_ROW]
     bit = 1
     while bit < num_cell:
-        prior = prior + lax.ppermute(prior, "cell", [(i, i ^ bit) for i in range(num_cell)])
+        prior = prior + flip(prior, bit, "cell")
         bit *= 2
     prior = (prior / num_cell).reshape(2, 128, 128)
-    arrived = [along_cell(pieces[s], -s) for s in order[1:-1]]
+    arrived = [flip(pieces[s], s, "cell") for s in order[1:-1]]
     own_sum = pieces[0] + sum(arrived)
     return (
         rendered,

time: 110 us -> 106 us (0.964)
  waiting for transfers between devices: 35.4 us -> 25.8 us
  starting transfers between devices: 19.8 us -> 26.3 us
    ppermute x26, waiting for transfers between devices: 35.4 us -> 25.8 us  [flip(): lax.ppermute(x, axis, [(i, i ^ bits) for i in range(lax.axis_size(axis))])]
    ppermute x26, starting transfers between devices: 19.8 us -> 26.3 us  [flip(): lax.ppermute(x, axis, [(i, i ^ bits) for i in range(lax.axis_size(axis))])]
  transfers between devices with their start and end apart: 26 -> 26, of which waited for: 14 -> 11; matrix products, arithmetic and copies ran while one was open for 3% -> 3% of each run, Pallas kernels for 4% -> 4%
where the time goes in v3:
time: 106 us
  Pallas kernels  46.9 us (44%)
  starting transfers between devices  26.3 us (25%)
  waiting for transfers between devices  25.8 us (24%)
  other arithmetic  3.69 us (3%)
  local copies, waits for them, and re-layouts  2.4 us (2%)
    pallas_call x1, Pallas kernels, resident(): pl.pallas_call(functools.partial(step_kernel, cells, samples), in_specs=[...  41 us
    ppermute x26, starting transfers between devices, flip(): lax.ppermute(x, axis, [(i, i ^ bits) for i in range(lax.axis_size(axis))])  26.3 us
    ppermute x26, waiting for transfers between devices, flip(): lax.ppermute(x, axis, [(i, i ^ bits) for i in range(lax.axis_size(axis))])  25.8 us
    pallas_call x1, Pallas kernels, resident(): pl.pallas_call(functools.partial(deal_kernel, cells, samples), in_specs=[...  4.28 us
  transfers between devices with their start and end apart: 26, of which 11 were waited for; matrix products, arithmetic and copies ran while one was open for 3% of the time, Pallas kernels for 4%

profile of v3, /device:TPU:0, one launch (start us, length us, event | category | flops | bytes accessed | tf_op | source)
XLA Modules:
  0.0 106.0 jit_solution(7414646897418919822)
XLA Ops:
  0.6 1.7 %pack.1 = (f32[264,128]{1,0:T(8,128)}, f32[264,128]{1,0:T(8,128)}) custom-call(bf16[1,2,128,128]{3,2,1,0:T(8,128)(2,1)} %layers_ref.1, bf16[1,2,128,128]{3,2,1,0:T(8,128)(2,1)} %prior_ref.1, bf16[1,4,128]{2,1,0:T(4,128)(2,1)} %head_ref.1, f32[3,1,48]{2,1,0:T(1,128)} %bitcast.45), custom_call_target="tpu_custom_call" | custom-call | tf_op jit(solution)/shard_map/pack/pallas_call | solution.py:745
  2.8 2.5 %collective-permute-start.3 = (f32[264,128]{1,0:T(8,128)}, f32[264,128]{1,0:T(8,128)S(1)}, u32[]{:S(2)}, u32[]{:S(2)}) collective-permute-start(f32[264,128]{1,0:T(8,128)} %get-tuple-element.41.refs_0_), channel_id=1, source_target_pairs={{0,2},{1,3},{2,0},{3,1},{4,6},{5,7},{6,4},{7,5},{8,10},{9,11},{10,... | collective-permute-start | bytes 405512 | tf_op jit(solution)/shard_map/ppermute | solution.py:743
  5.3 2.6 %collective-permute-start.1 = (f32[264,128]{1,0:T(8,128)}, f32[264,128]{1,0:T(8,128)S(1)}, u32[]{:S(2)}, u32[]{:S(2)}) collective-permute-start(f32[264,128]{1,0:T(8,128)} %get-tuple-element.41.refs_0_), channel_id=1, source_target_pairs={{0,8},{4,12},{8,0},{12,4},{1,9},{5,13},{9,1},{13,5},{2,10},{6,14},... | collective-permute-start | bytes 405512 | tf_op jit(solution)/shard_map/ppermute | solution.py:743
  7.8 1.3 %fusion.8.cells_ref = s32[4,256]{1,0:T(4,128)} fusion(s32[256,4]{0,1:T(4,128)} %param.16, s32[]{:T(128)S(6)} %axis_index.25, s32[]{:T(128)S(6)} %axis_index.22), kind=kLoop, calls=%fused_computation.35 | loop fusion | flops 27648 | bytes 8200 | tf_op jit(solution)/shard_map/transpose | solution.py:754
  9.1 4.3 %deal.1 = (f32[8,1024]{1,0:T(8,128)}, f32[144,256]{1,0:T(8,128)}, s32[8,256]{1,0:T(8,128)}, s32[24,128]{1,0:T(8,128)}, f32[2,1152,128]{2,1,0:T(8,128)}, /*index=5*/bf16[128,48]{1,0:T(8,128)(2,1)}, f32[264,128]{1,0:T(8,128)}) custom-call(s32[4,256]{1,0:T(4,128)} %fusion.8.cells_ref, f32[6,256]{1,0:T(8,128)} %geometry_ref.1, ...), custom_call_target="tpu_custom_call", output_to_operand_aliasing={{6}: (5, {})} | custom-call | flops 6442450944 | bytes 4194304 | tf_op jit(solution)/shard_map/deal/pallas_call | solution.py:757
  13.4 1.6 %collective-permute-start = (f32[264,128]{1,0:T(8,128)}, f32[264,128]{1,0:T(8,128)S(1)}, u32[]{:S(2)}, u32[]{:S(2)}) collective-permute-start(f32[264,128]{1,0:T(8,128)} %get-tuple-element.42), channel_id=1, source_target_pairs={{0,4},{4,0},{8,12},{12,8},{1,5},{5,1},{9,13},{13,9},{2,6},{6,2},{1... | collective-permute-start | bytes 405512 | tf_op jit(solution)/shard_map/ppermute | solution.py:743
  16.8 3.3 %collective-permute-done.refs_1_ = f32[264,128]{1,0:T(8,128)S(1)} collective-permute-done((f32[264,128]{1,0:T(8,128)}, f32[264,128]{1,0:T(8,128)S(1)}, u32[]{:S(2)}, u32[]{:S(2)}) %collective-permute-start) | collective-permute-done | bytes 135200 | tf_op jit(solution)/shard_map/ppermute | solution.py:743
  20.6 1.3 %collective-permute-done.2.refs_3_ = f32[264,128]{1,0:T(8,128)S(1)} collective-permute-done((f32[264,128]{1,0:T(8,128)S(1)}, f32[264,128]{1,0:T(8,128)S(1)}, u32[]{:S(2)}, u32[]{:S(2)}) %collective-permute-start.2) | collective-permute-done | bytes 135200 | tf_op jit(solution)/shard_map/ppermute | solution.py:743
  23.1 3.4 %collective-permute-done.4.refs_5_ = f32[264,128]{1,0:T(8,128)S(1)} collective-permute-done((f32[264,128]{1,0:T(8,128)S(1)}, f32[264,128]{1,0:T(8,128)S(1)}, u32[]{:S(2)}, u32[]{:S(2)}) %collective-permute-start.4) | collective-permute-done | bytes 135200 | tf_op jit(solution)/shard_map/ppermute | solution.py:743
  26.5 1.4 %collective-permute-done.6.refs_7_ = f32[264,128]{1,0:T(8,128)S(1)} collective-permute-done((f32[264,128]{1,0:T(8,128)S(1)}, f32[264,128]{1,0:T(8,128)S(1)}, u32[]{:S(2)}, u32[]{:S(2)}) %collective-permute-start.6) | collective-permute-done | bytes 135200 | tf_op jit(solution)/shard_map/ppermute | solution.py:743
  30.0 41.0 %step.1 = (f32[3,256]{1,0:T(4,128)}, f32[48,256]{1,0:T(8,128)}, f32[10,264,128]{2,1,0:T(8,128)}, f32[10,264,128]{2,1,0:T(8,128)}) custom-call(s32[8,256]{1,0:T(8,128)} %get-tuple-element.35.tile_cell_ref, s32[24,128]{1,0:T(8,128)} %get-tuple-element.36.tile_start_ref, f32[8,1024]{1,0:T(8,128)} %get-tuple-element.37.meta_ref, s32[4,256]{1,0:T(4,128)} %fusion.8.cells_ref, ...), custom_call_target="tpu_custom_call" | custom-call | tf_op jit(solution)/shard_map/step/pallas_call | solution.py:783
  71.2 3.2 %collective-permute-done.15 = f32[10,264,128]{2,1,0:T(8,128)S(1)} collective-permute-done((f32[10,264,128]{2,1,0:T(8,128)}, f32[10,264,128]{2,1,0:T(8,128)S(1)}, u32[]{:S(2)}, u32[]{:S(2)}) %collective-permute-start.15) | collective-permute-done | bytes 1351712 | tf_op jit(solution)/shard_map/ppermute | solution.py:743
  74.3 1.6 %fusion = (f32[264,128]{1,0:T(8,128)S(1)}, f32[264,128]{1,0:T(8,128)S(1)}, f32[264,128]{1,0:T(8,128)S(1)}, f32[264,128]{1,0:T(8,128)S(1)}, f32[264,128]{1,0:T(8,...) fusion(f32[10,264,128]{2,1,0:T(8,128)S(1)} %collective-permute-, ...), kind=kLoop, calls=%fused_computation.1 | loop fusion | flops 168960 | bytes 4460544 | tf_op jit(solution)/shard_map/add | solution.py:826
  76.5 1.5 %collective-permute-start.21 = (f32[264,128]{1,0:T(8,128)S(1)}, f32[264,128]{1,0:T(8,128)S(1)}, u32[]{:S(2)}, u32[]{:S(2)}) collective-permute-start(f32[264,128]{1,0:T(8,128)S(1)} %get-tuple-element.69), channel_id=1, source_target_pairs={{0,2},{1,3},{2,0},{3,1},{4,6},{5,7},{6,4},{7,5},{8,10},{9,11},{10,... | collective-permute-start | bytes 405512 | tf_op jit(solution)/shard_map/ppermute | solution.py:743
  78.5 1.5 %collective-permute-start.17 = (f32[264,128]{1,0:T(8,128)S(1)}, f32[264,128]{1,0:T(8,128)S(1)}, u32[]{:S(2)}, u32[]{:S(2)}) collective-permute-start(f32[264,128]{1,0:T(8,128)S(1)} %get-tuple-element.71), channel_id=1, source_target_pairs={{0,2},{1,3},{2,0},{3,1},{4,6},{5,7},{6,4},{7,5},{8,10},{9,11},{10,... | collective-permute-start | bytes 405512 | tf_op jit(solution)/shard_map/ppermute | solution.py:743
  80.5 1.9 %collective-permute-done.23 = f32[264,128]{1,0:T(8,128)S(1)} collective-permute-done((f32[264,128]{1,0:T(8,128)S(1)}, f32[264,128]{1,0:T(8,128)S(1)}, u32[]{:S(2)}, u32[]{:S(2)}) %collective-permute-start.23) | collective-permute-done | bytes 135200 | tf_op jit(solution)/shard_map/ppermute | solution.py:743
  82.4 1.6 %collective-permute-start.24 = (f32[256,128]{1,0:T(8,128)S(1)}, f32[256,128]{1,0:T(8,128)S(1)}, u32[]{:S(2)}, u32[]{:S(2)}) collective-permute-start(f32[256,128]{1,0:T(8,128)S(1)} %slice_add_fusion.5), channel_id=1, source_target_pairs={{0,4},{4,0},{8,12},{12,8},{1,5},{5,1},{9,13},{13,9},{2,6},{6,2},{1... | collective-permute-start | bytes 393224 | tf_op jit(solution)/shard_map/ppermute | solution.py:743
  84.0 1.3 %collective-permute-done.21 = f32[264,128]{1,0:T(8,128)S(1)} collective-permute-done((f32[264,128]{1,0:T(8,128)S(1)}, f32[264,128]{1,0:T(8,128)S(1)}, u32[]{:S(2)}, u32[]{:S(2)}) %collective-permute-start.21) | collective-permute-done | bytes 135200 | tf_op jit(solution)/shard_map/ppermute | solution.py:743
  85.3 2.6 %collective-permute-start.22 = (f32[264,128]{1,0:T(8,128)S(1)}, f32[264,128]{1,0:T(8,128)S(1)}, u32[]{:S(2)}, u32[]{:S(2)}) collective-permute-start(f32[264,128]{1,0:T(8,128)S(1)} %add_add_fusion.1), channel_id=1, source_target_pairs={{0,12},{4,8},{8,4},{12,0},{1,13},{5,9},{9,5},{13,1},{2,14},{6,10},... | collective-permute-start | bytes 405512 | tf_op jit(solution)/shard_map/ppermute | solution.py:743
  88.2 1.6 %collective-permute-start.20 = (f32[264,128]{1,0:T(8,128)S(1)}, f32[264,128]{1,0:T(8,128)S(1)}, u32[]{:S(2)}, u32[]{:S(2)}) collective-permute-start(f32[264,128]{1,0:T(8,128)S(1)} %add_add_fusion.2), channel_id=1, source_target_pairs={{0,4},{4,0},{8,12},{12,8},{1,5},{5,1},{9,13},{13,9},{2,6},{6,2},{1... | collective-permute-start | bytes 405512 | tf_op jit(solution)/shard_map/ppermute | solution.py:743
  89.8 1.3 %collective-permute-done.17 = f32[264,128]{1,0:T(8,128)S(1)} collective-permute-done((f32[264,128]{1,0:T(8,128)S(1)}, f32[264,128]{1,0:T(8,128)S(1)}, u32[]{:S(2)}, u32[]{:S(2)}) %collective-permute-start.17) | collective-permute-done | bytes 135200 | tf_op jit(solution)/shard_map/ppermute | solution.py:743
  91.1 3.1 %collective-permute-start.18 = (f32[264,128]{1,0:T(8,128)S(1)}, f32[264,128]{1,0:T(8,128)S(1)}, u32[]{:S(2)}, u32[]{:S(2)}) collective-permute-start(f32[264,128]{1,0:T(8,128)S(1)} %add_add_fusion.3), channel_id=1, source_target_pairs={{0,8},{4,12},{8,0},{12,4},{1,9},{5,13},{9,1},{13,5},{2,10},{6,14},... | collective-permute-start | bytes 405512 | tf_op jit(solution)/shard_map/ppermute | solution.py:743
  94.2 2.1 %collective-permute-start.25 = (f32[256,128]{1,0:T(8,128)S(1)}, f32[256,128]{1,0:T(8,128)S(1)}, u32[]{:S(2)}, u32[]{:S(2)}) collective-permute-start(f32[256,128]{1,0:T(8,128)S(1)} %add.114), channel_id=1, source_target_pairs={{0,8},{4,12},{8,0},{12,4},{1,9},{5,13},{9,1},{13,5},{2,10},{6,14},... | collective-permute-start | bytes 393224 | tf_op jit(solution)/shard_map/ppermute | solution.py:743
  96.3 7.2 %collective-permute-done.18 = f32[264,128]{1,0:T(8,128)S(1)} collective-permute-done((f32[264,128]{1,0:T(8,128)S(1)}, f32[264,128]{1,0:T(8,128)S(1)}, u32[]{:S(2)}, u32[]{:S(2)}) %collective-permute-start.18) | collective-permute-done | bytes 135200 | tf_op jit(solution)/shard_map/ppermute | solution.py:743
  (75 shorter events, 10.5 us)
Async XLA Ops:
  2.3 14.0 %collective-permute-start.7 = (f32[264,128]{1,0:T(8,128)}, f32[264,128]{1,0:T(8,128)S(1)}, u32[]{:S(2)}, u32[]{:S(2)}) collective-permute-start(f32[264,128]{1,0:T(8,128)} %get-tuple-element.41.refs_0_), channel_id=1, source_target_pairs={{0,1},{1,0},{2,3},{3,2},{4,5},{5,4},{6,7},{7,6},{8,9},{9,8},{10,11... | collective-permute-start | bytes 405512 | tf_op jit(solution)/shard_map/ppermute | solution.py:743
  2.8 13.0 %collective-permute-start.3 = (f32[264,128]{1,0:T(8,128)}, f32[264,128]{1,0:T(8,128)S(1)}, u32[]{:S(2)}, u32[]{:S(2)}) collective-permute-start(f32[264,128]{1,0:T(8,128)} %get-tuple-element.41.refs_0_), channel_id=1, source_target_pairs={{0,2},{1,3},{2,0},{3,1},{4,6},{5,7},{6,4},{7,5},{8,10},{9,11},{10,... | collective-permute-start | bytes 405512 | tf_op jit(solution)/shard_map/ppermute | solution.py:743
  5.3 9.7 %collective-permute-start.1 = (f32[264,128]{1,0:T(8,128)}, f32[264,128]{1,0:T(8,128)S(1)}, u32[]{:S(2)}, u32[]{:S(2)}) collective-permute-start(f32[264,128]{1,0:T(8,128)} %get-tuple-element.41.refs_0_), channel_id=1, source_target_pairs={{0,8},{4,12},{8,0},{12,4},{1,9},{5,13},{9,1},{13,5},{2,10},{6,14},... | collective-permute-start | bytes 405512 | tf_op jit(solution)/shard_map/ppermute | solution.py:743
  13.4 6.7 %collective-permute-start = (f32[264,128]{1,0:T(8,128)}, f32[264,128]{1,0:T(8,128)S(1)}, u32[]{:S(2)}, u32[]{:S(2)}) collective-permute-start(f32[264,128]{1,0:T(8,128)} %get-tuple-element.42), channel_id=1, source_target_pairs={{0,4},{4,0},{8,12},{12,8},{1,5},{5,1},{9,13},{13,9},{2,6},{6,2},{1... | collective-permute-start | bytes 405512 | tf_op jit(solution)/shard_map/ppermute | solution.py:743
  15.0 7.0 %collective-permute-start.2 = (f32[264,128]{1,0:T(8,128)S(1)}, f32[264,128]{1,0:T(8,128)S(1)}, u32[]{:S(2)}, u32[]{:S(2)}) collective-permute-start(f32[264,128]{1,0:T(8,128)S(1)} %collective-permute-done.1.refs_2_), channel_id=1, source_target_pairs={{0,4},{4,0},{8,12},{12,8},{1,5},{5,1},{9,13},{13,9},{2,6},{6,2},{1... | collective-permute-start | bytes 405512 | tf_op jit(solution)/shard_map/ppermute | solution.py:743
  15.8 6.7 %collective-permute-start.11 = (f32[264,128]{1,0:T(8,128)S(1)}, f32[264,128]{1,0:T(8,128)S(1)}, u32[]{:S(2)}, u32[]{:S(2)}) collective-permute-start(f32[264,128]{1,0:T(8,128)S(1)} %collective-permute-done.3.refs_4_), channel_id=1, source_target_pairs={{0,1},{1,0},{2,3},{3,2},{4,5},{5,4},{6,7},{7,6},{8,9},{9,8},{10,11... | collective-permute-start | bytes 405512 | tf_op jit(solution)/shard_map/ppermute | solution.py:743
  15.8 6.7 %collective-permute-start.9 = (f32[264,128]{1,0:T(8,128)S(1)}, f32[264,128]{1,0:T(8,128)S(1)}, u32[]{:S(2)}, u32[]{:S(2)}) collective-permute-start(f32[264,128]{1,0:T(8,128)S(1)} %collective-permute-done.1.refs_2_), channel_id=1, source_target_pairs={{0,1},{1,0},{2,3},{3,2},{4,5},{5,4},{6,7},{7,6},{8,9},{9,8},{10,11... | collective-permute-start | bytes 405512 | tf_op jit(solution)/shard_map/ppermute | solution.py:743
  16.3 6.7 %collective-permute-start.5 = (f32[264,128]{1,0:T(8,128)S(1)}, f32[264,128]{1,0:T(8,128)S(1)}, u32[]{:S(2)}, u32[]{:S(2)}) collective-permute-start(f32[264,128]{1,0:T(8,128)S(1)} %collective-permute-done.1.refs_2_), channel_id=1, source_target_pairs={{0,2},{1,3},{2,0},{3,1},{4,6},{5,7},{6,4},{7,5},{8,10},{9,11},{10,... | collective-permute-start | bytes 405512 | tf_op jit(solution)/shard_map/ppermute | solution.py:743
  20.1 6.5 %collective-permute-start.4 = (f32[264,128]{1,0:T(8,128)S(1)}, f32[264,128]{1,0:T(8,128)S(1)}, u32[]{:S(2)}, u32[]{:S(2)}) collective-permute-start(f32[264,128]{1,0:T(8,128)S(1)} %collective-permute-done.refs_1_), channel_id=1, source_target_pairs={{0,2},{1,3},{2,0},{3,1},{4,6},{5,7},{6,4},{7,5},{8,10},{9,11},{10,... | collective-permute-start | bytes 405512 | tf_op jit(solution)/shard_map/ppermute | solution.py:743
  22.0 6.0 %collective-permute-start.6 = (f32[264,128]{1,0:T(8,128)S(1)}, f32[264,128]{1,0:T(8,128)S(1)}, u32[]{:S(2)}, u32[]{:S(2)}) collective-permute-start(f32[264,128]{1,0:T(8,128)S(1)} %collective-permute-done.2.refs_3_), channel_id=1, source_target_pairs={{0,2},{1,3},{2,0},{3,1},{4,6},{5,7},{6,4},{7,5},{8,10},{9,11},{10,... | collective-permute-start | bytes 405512 | tf_op jit(solution)/shard_map/ppermute | solution.py:743
  22.5 5.5 %collective-permute-start.8 = (f32[264,128]{1,0:T(8,128)S(1)}, f32[264,128]{1,0:T(8,128)S(1)}, u32[]{:S(2)}, u32[]{:S(2)}) collective-permute-start(f32[264,128]{1,0:T(8,128)S(1)} %collective-permute-done.refs_1_), channel_id=1, source_target_pairs={{0,1},{1,0},{2,3},{3,2},{4,5},{5,4},{6,7},{7,6},{8,9},{9,8},{10,11... | collective-permute-start | bytes 405512 | tf_op jit(solution)/shard_map/ppermute | solution.py:743
  22.5 5.5 %collective-permute-start.10 = (f32[264,128]{1,0:T(8,128)S(1)}, f32[264,128]{1,0:T(8,128)S(1)}, u32[]{:S(2)}, u32[]{:S(2)}) collective-permute-start(f32[264,128]{1,0:T(8,128)S(1)} %collective-permute-done.2.refs_3_), channel_id=1, source_target_pairs={{0,1},{1,0},{2,3},{3,2},{4,5},{5,4},{6,7},{7,6},{8,9},{9,8},{10,11... | collective-permute-start | bytes 405512 | tf_op jit(solution)/shard_map/ppermute | solution.py:743
  23.0 5.0 %collective-permute-start.13 = (f32[264,128]{1,0:T(8,128)S(1)}, f32[264,128]{1,0:T(8,128)S(1)}, u32[]{:S(2)}, u32[]{:S(2)}) collective-permute-start(f32[264,128]{1,0:T(8,128)S(1)} %collective-permute-done.5.refs_6_), channel_id=1, source_target_pairs={{0,1},{1,0},{2,3},{3,2},{4,5},{5,4},{6,7},{7,6},{8,9},{9,8},{10,11... | collective-permute-start | bytes 405512 | tf_op jit(solution)/shard_map/ppermute | solution.py:743
  71.0 3.4 %collective-permute-start.15 = (f32[10,264,128]{2,1,0:T(8,128)}, f32[10,264,128]{2,1,0:T(8,128)S(1)}, u32[]{:S(2)}, u32[]{:S(2)}) collective-permute-start(f32[10,264,128]{2,1,0:T(8,128)} %get-tuple-element.45), channel_id=1, source_target_pairs={{0,1},{1,0},{2,3},{3,2},{4,5},{5,4},{6,7},{7,6},{8,9},{9,8},{10,11... | collective-permute-start | bytes 4055048 | tf_op jit(solution)/shard_map/ppermute | solution.py:743
  75.9 6.5 %collective-permute-start.23 = (f32[264,128]{1,0:T(8,128)S(1)}, f32[264,128]{1,0:T(8,128)S(1)}, u32[]{:S(2)}, u32[]{:S(2)}) collective-permute-start(f32[264,128]{1,0:T(8,128)S(1)} %get-tuple-element.68), channel_id=1, source_target_pairs={{0,2},{1,3},{2,0},{3,1},{4,6},{5,7},{6,4},{7,5},{8,10},{9,11},{10,... | collective-permute-start | bytes 405512 | tf_op jit(solution)/shard_map/ppermute | solution.py:743
  76.5 8.8 %collective-permute-start.21 = (f32[264,128]{1,0:T(8,128)S(1)}, f32[264,128]{1,0:T(8,128)S(1)}, u32[]{:S(2)}, u32[]{:S(2)}) collective-permute-start(f32[264,128]{1,0:T(8,128)S(1)} %get-tuple-element.69), channel_id=1, source_target_pairs={{0,2},{1,3},{2,0},{3,1},{4,6},{5,7},{6,4},{7,5},{8,10},{9,11},{10,... | collective-permute-start | bytes 405512 | tf_op jit(solution)/shard_map/ppermute | solution.py:743
  78.0 10.2 %collective-permute-start.19 = (f32[264,128]{1,0:T(8,128)S(1)}, f32[264,128]{1,0:T(8,128)S(1)}, u32[]{:S(2)}, u32[]{:S(2)}) collective-permute-start(f32[264,128]{1,0:T(8,128)S(1)} %get-tuple-element.70), channel_id=1, source_target_pairs={{0,2},{1,3},{2,0},{3,1},{4,6},{5,7},{6,4},{7,5},{8,10},{9,11},{10,... | collective-permute-start | bytes 405512 | tf_op jit(solution)/shard_map/ppermute | solution.py:743
  78.5 12.6 %collective-permute-start.17 = (f32[264,128]{1,0:T(8,128)S(1)}, f32[264,128]{1,0:T(8,128)S(1)}, u32[]{:S(2)}, u32[]{:S(2)}) collective-permute-start(f32[264,128]{1,0:T(8,128)S(1)} %get-tuple-element.71), channel_id=1, source_target_pairs={{0,2},{1,3},{2,0},{3,1},{4,6},{5,7},{6,4},{7,5},{8,10},{9,11},{10,... | collective-permute-start | bytes 405512 | tf_op jit(solution)/shard_map/ppermute | solution.py:743
  80.0 14.2 %collective-permute-start.16 = (f32[264,128]{1,0:T(8,128)S(1)}, f32[264,128]{1,0:T(8,128)S(1)}, u32[]{:S(2)}, u32[]{:S(2)}) collective-permute-start(f32[264,128]{1,0:T(8,128)S(1)} %get-tuple-element.72), channel_id=1, source_target_pairs={{0,2},{1,3},{2,0},{3,1},{4,6},{5,7},{6,4},{7,5},{8,10},{9,11},{10,... | collective-permute-start | bytes 405512 | tf_op jit(solution)/shard_map/ppermute | solution.py:743
  82.4 11.8 %collective-permute-start.24 = (f32[256,128]{1,0:T(8,128)S(1)}, f32[256,128]{1,0:T(8,128)S(1)}, u32[]{:S(2)}, u32[]{:S(2)}) collective-permute-start(f32[256,128]{1,0:T(8,128)S(1)} %slice_add_fusion.5), channel_id=1, source_target_pairs={{0,4},{4,0},{8,12},{12,8},{1,5},{5,1},{9,13},{13,9},{2,6},{6,2},{1... | collective-permute-start | bytes 393224 | tf_op jit(solution)/shard_map/ppermute | solution.py:743
  85.3 11.0 %collective-permute-start.22 = (f32[264,128]{1,0:T(8,128)S(1)}, f32[264,128]{1,0:T(8,128)S(1)}, u32[]{:S(2)}, u32[]{:S(2)}) collective-permute-start(f32[264,128]{1,0:T(8,128)S(1)} %add_add_fusion.1), channel_id=1, source_target_pairs={{0,12},{4,8},{8,4},{12,0},{1,13},{5,9},{9,5},{13,1},{2,14},{6,10},... | collective-permute-start | bytes 405512 | tf_op jit(solution)/shard_map/ppermute | solution.py:743
  88.2 8.1 %collective-permute-start.20 = (f32[264,128]{1,0:T(8,128)S(1)}, f32[264,128]{1,0:T(8,128)S(1)}, u32[]{:S(2)}, u32[]{:S(2)}) collective-permute-start(f32[264,128]{1,0:T(8,128)S(1)} %add_add_fusion.2), channel_id=1, source_target_pairs={{0,4},{4,0},{8,12},{12,8},{1,5},{5,1},{9,13},{13,9},{2,6},{6,2},{1... | collective-permute-start | bytes 405512 | tf_op jit(solution)/shard_map/ppermute | solution.py:743
  91.1 12.4 %collective-permute-start.18 = (f32[264,128]{1,0:T(8,128)S(1)}, f32[264,128]{1,0:T(8,128)S(1)}, u32[]{:S(2)}, u32[]{:S(2)}) collective-permute-start(f32[264,128]{1,0:T(8,128)S(1)} %add_add_fusion.3), channel_id=1, source_target_pairs={{0,8},{4,12},{8,0},{12,4},{1,9},{5,13},{9,1},{13,5},{2,10},{6,14},... | collective-permute-start | bytes 405512 | tf_op jit(solution)/shard_map/ppermute | solution.py:743
  94.2 11.1 %collective-permute-start.25 = (f32[256,128]{1,0:T(8,128)S(1)}, f32[256,128]{1,0:T(8,128)S(1)}, u32[]{:S(2)}, u32[]{:S(2)}) collective-permute-start(f32[256,128]{1,0:T(8,128)S(1)} %add.114), channel_id=1, source_target_pairs={{0,8},{4,12},{8,0},{12,4},{1,9},{5,13},{9,1},{13,5},{2,10},{6,14},... | collective-permute-start | bytes 393224 | tf_op jit(solution)/shard_map/ppermute | solution.py:743
  (17 other events, 91.3 us)

commit v4 on v3

--- a/solution.py
+++ b/solution.py
@@ -273,6 +273,14 @@
 HEAD_ROW = 256
 APP_ROW = 260
 VMEM_LIMIT = 56 * 1024 * 1024
+SIN = (
+    6.283185005187988,
+    -41.341590881347656,
+    81.59994506835938,
+    -76.61447143554688,
+    41.3428840637207,
+    -12.471243858337402,
+)
 COS = (
     0.9999992251396179,
     -19.738981246948242,
@@ -306,8 +314,10 @@
 
 
 def pick_nn(x, select):
-    high, mid, low = split3(x)
-    return (dot_nn(low, select) + dot_nn(mid, select)) + dot_nn(high, select)
+    rows = x.shape[0]
+    parts = jnp.concatenate([part.astype(F32) for part in split3(x)], axis=0)
+    parts = dot_nn(parts.astype(BF16), select)
+    return (parts[2 * rows :] + parts[rows : 2 * rows]) + parts[:rows]
 
 
 def pick_nt(select, x):
@@ -382,6 +392,7 @@
     jitter_ref,
     frequency_ref,
     own_ref,
+    other_ref,
     meta_ref,
     spacing_ref,
     tile_cell_ref,
@@ -390,7 +401,7 @@
     factor_ref,
     passed_ref,
 ):
-    del own_ref, passed_ref
+    del own_ref, other_ref, passed_ref
     tiles = spacing_ref.shape[0]
     lanes = TILE * samples
     crossings, rays = cells_ref.shape
@@ -459,17 +470,15 @@
     spacing_ref[...] = ending - depths
     for c in range(3):
         put_channel(position_ref, c, channel[c] + depths * channel[3 + c])
-    put_channel(position_ref, 3, jnp.ones((tiles, lanes), F32))
-    for c in range(4, 8):
+    for c in range(3, 8):
         put_channel(position_ref, c, jnp.zeros((tiles, lanes), F32))
     turns = frequency_ref[...] * 0.15915494309189535
-    turns = jnp.concatenate([turns, turns], axis=1)
-    features = turns.shape[1]
-    quarter = jnp.where(iota((1, features), 1) < features // 2, -0.25, 0.0)
-    block = jnp.concatenate([turns, quarter, jnp.zeros((4, features), F32)], axis=0)
+    count = turns.shape[1]
+    block = jnp.concatenate([turns, jnp.zeros((5, count), F32)], axis=0)
+    block = jnp.concatenate([block, jnp.zeros((8, 128 - count), F32)], axis=1)
     high, mid, low = [part.astype(F32) for part in split3(block)]
-    stack = [high, high, high, mid, mid, low, jnp.zeros((features - 48, features), F32)]
-    factor_ref[...] = jnp.concatenate(stack, axis=0).T[:, 0:48].astype(BF16)
+    stack = [high, high, high, mid, mid, low, jnp.zeros((128 - 48, 128), F32)]
+    factor_ref[...] = jnp.concatenate(stack, axis=0).T[0:count, 0:48].astype(BF16)
 
 
 def encode(position_ref, factor, encoded_ref, some):
@@ -482,10 +491,12 @@
     for t, phase in zip(some, phases):
         phase = phase - jnp.round(phase)
         square = phase * phase
-        value = square * COS[5] + COS[4]
+        sine, cosine = square * SIN[5] + SIN[4], square * COS[5] + COS[4]
         for c in (3, 2, 1, 0):
-            value = value * square + COS[c]
-        encoded_ref[t] = value.astype(BF16)
+            sine, cosine = sine * square + SIN[c], cosine * square + COS[c]
+        half = phase.shape[0]
+        encoded_ref[t, 0:half, :] = (sine * phase).astype(BF16)
+        encoded_ref[t, half:, :] = cosine.astype(BF16)
 
 
 def step_kernel(
@@ -689,28 +700,30 @@
             sums_ref[v, 0:128, :] += first
         return carry
 
-    lax.fori_loop(0, trips, backward, 0)
     num_cell = cells // 4
     copies = []
-    for district in range(4):
-        members = sums_ref.at[pl.ds(district * num_cell, num_cell)]
-        total = sums_ref[district * num_cell]
-        for s in range(1, num_cell):
-            total = total + sums_ref[district * num_cell + s]
-        sums_ref[cells + district] = total
-        out_ref = (keep_ref, send_ref)[district // 2]
-        at = (district % 2) * (num_cell + 1)
-        for n, (source, sink) in enumerate(
-            [
+
+    def emit(half):
+        for district in (2 * half, 2 * half + 1):
+            members = sums_ref.at[pl.ds(district * num_cell, num_cell)]
+            total = sums_ref[district * num_cell]
+            for s in range(1, num_cell):
+                total = total + sums_ref[district * num_cell + s]
+            sums_ref[cells + district] = total
+            out_ref = (keep_ref, send_ref)[half]
+            at = (district % 2) * (num_cell + 1)
+            for source, sink in (
                 (members, out_ref.at[pl.ds(at, num_cell)]),
                 (sums_ref.at[cells + district], out_ref.at[at + num_cell]),
-            ]
-        ):
-            copies.append(
-                pltpu.make_async_copy(source, sink, semaphore.at[district * 2 + n])
-            )
-    for copy in copies:
-        copy.start()
+            ):
+                copies.append(pltpu.make_async_copy(source, sink, semaphore.at[len(copies)]))
+                copies[-1].start()
+
+    middle = (tile_start_ref[cells // 2, 0] + UNROLL - 1) // UNROLL
+    lax.fori_loop(0, middle, backward, 0)
+    emit(0)
+    lax.fori_loop(middle, trips, backward, 0)
+    emit(1)
     for copy in copies:
         copy.wait()
 
@@ -749,6 +762,7 @@
     anywhere = pl.BlockSpec(memory_space=pl.ANY)
     params = pltpu.CompilerParams(vmem_limit_bytes=VMEM_LIMIT)
 
+    crossed_own = flip(own, 2)
     away = (crossing % num_district) ^ me_district
     steps = (crossing // num_district) ^ me_cell
     virtual = (((away & 1) * 2 + (away >> 1)) * num_cell + steps).T
@@ -756,7 +770,7 @@
     default = pl.BlockSpec()
     meta, spacing, tile_cell, tile_start, position, factor, passed = pl.pallas_call(
         functools.partial(deal_kernel, cells, samples),
-        in_specs=[default] * 5 + [anywhere],
+        in_specs=[default] * 5 + [anywhere, anywhere],
         out_specs=[default] * 6 + [anywhere],
         input_output_aliases={5: 6},
         out_shape=[
@@ -765,18 +779,18 @@
             jax.ShapeDtypeStruct((8, 256), jnp.int32),
             jax.ShapeDtypeStruct((cells + 8, 128), jnp.int32),
             jax.ShapeDtypeStruct((halves, tiles * 8, 128), F32),
-            jax.ShapeDtypeStruct((128, 48), BF16),
+            jax.ShapeDtypeStruct((frequencies.shape[1], 48), BF16),
             jax.ShapeDtypeStruct((ROWS, 128), F32),
         ],
         compiler_params=params,
         cost_estimate=pl.CostEstimate(flops=6 << 30, bytes_accessed=4 << 20, transcendentals=0),
         name="deal",
-    )(virtual, ray_geometry, segment_length.T, jitter, frequencies, again)
+    )(virtual, ray_geometry, segment_length.T, jitter, frequencies, again, crossed_own)
     near = [own]
     for s in range(1, num_cell):
-        near.append(flip(near[s & (s - 1)] if s > 1 else passed, s & -s, "cell"))
-    flipped = [flip(piece, 2) for piece in near]
-    weights = near + flipped + [flip(piece, 1) for piece in near + flipped]
+        near.append(flip(near[s & (s - 1)], s & -s, "cell"))
+    flipped = [crossed_own] + [flip(piece, 2) for piece in near[1:]]
+    weights = near + flipped + [flip(piece, 1) for piece in [passed] + near[1:] + flipped]
 
 
     half = 2 * (num_cell + 1)
@@ -820,21 +834,24 @@
     )
 
     crossed = flip(send, 1)
-    order = [num_cell, num_cell // 2]
-    order += [s for s in range(1, num_cell) if s != num_cell // 2] + [0]
+    order = [3, 2, num_cell, 1, 0]
     far = num_cell + 1
     pieces = {s: flip(keep[far + s] + crossed[far + s], 2) for s in order}
     for s in order:
         near_part, cross_part, other = lax.optimization_barrier((keep[s], crossed[s], pieces[s]))
         pieces[s] = near_part + cross_part + other
     prior = pieces[num_cell][0:HEAD_ROW]
+    bit = num_cell // 2
+    while bit > 0:
+        prior = prior + flip(prior, bit, "cell")
+        bit //= 2
+    prior = (prior / num_cell).reshape(2, 128, 128)
     bit = 1
     while bit < num_cell:
-        prior = prior + flip(prior, bit, "cell")
+        for s in reversed(range(bit, num_cell, 2 * bit)):
+            pieces[s - bit] = pieces[s - bit] + flip(pieces[s], bit, "cell")
         bit *= 2
-    prior = (prior / num_cell).reshape(2, 128, 128)
-    arrived = [flip(pieces[s], s, "cell") for s in order[1:-1]]
-    own_sum = pieces[0] + sum(arrived)
+    own_sum = pieces[0]
     return (
         rendered,
         own_sum[0:HEAD_ROW].reshape(1, 2, 128, 128),

time: 106 us -> 101 us (0.953)
  waiting for transfers between devices: 25.8 us -> 21.5 us
  Pallas kernels: 46.9 us -> 44.6 us
  starting transfers between devices: 26.3 us -> 27.7 us
    ppermute x26, waiting for transfers between devices: 25.8 us -> 21.5 us  [flip(): lax.ppermute(x, axis, [(i, i ^ bits) for i in range(lax.axis_size(axis))])]
    pallas_call x1, Pallas kernels: 41 us -> 38.7 us  [resident(): pl.pallas_call(functools.partial(step_kernel, cells, samples), in_specs=[...]
    ppermute x26, starting transfers between devices: 26.3 us -> 27.7 us  [flip(): lax.ppermute(x, axis, [(i, i ^ bits) for i in range(lax.axis_size(axis))])]
  transfers between devices with their start and end apart: 26 -> 26, of which waited for: 11 -> 12; matrix products, arithmetic and copies ran while one was open for 3% -> 2% of each run, Pallas kernels for 4% -> 4%
where the time goes in v4:
time: 101 us
  Pallas kernels  44.6 us (44%)
  starting transfers between devices  27.7 us (27%)
  waiting for transfers between devices  21.5 us (21%)
  other arithmetic  3.69 us (4%)
  local copies, waits for them, and re-layouts  2.45 us (2%)
    pallas_call x1, Pallas kernels, resident(): pl.pallas_call(functools.partial(step_kernel, cells, samples), in_specs=[...  38.7 us
    ppermute x26, starting transfers between devices, flip(): lax.ppermute(x, axis, [(i, i ^ bits) for i in range(lax.axis_size(axis))])  27.7 us
    ppermute x26, waiting for transfers between devices, flip(): lax.ppermute(x, axis, [(i, i ^ bits) for i in range(lax.axis_size(axis))])  21.5 us
    pallas_call x1, Pallas kernels, resident(): pl.pallas_call(functools.partial(deal_kernel, cells, samples), in_specs=[...  4.22 us
  transfers between devices with their start and end apart: 26, of which 12 were waited for; matrix products, arithmetic and copies ran while one was open for 2% of the time, Pallas kernels for 4%

profile of v4, /device:TPU:0, one launch (start us, length us, event | category | flops | bytes accessed | tf_op | source)
XLA Modules:
  0.0 100.8 jit_solution(16316506828574705528)
XLA Ops:
  0.6 1.7 %pack.1 = (f32[264,128]{1,0:T(8,128)}, f32[264,128]{1,0:T(8,128)}) custom-call(bf16[1,2,128,128]{3,2,1,0:T(8,128)(2,1)} %layers_ref.1, bf16[1,2,128,128]{3,2,1,0:T(8,128)(2,1)} %prior_ref.1, bf16[1,4,128]{2,1,0:T(4,128)(2,1)} %head_ref.1, f32[3,1,48]{2,1,0:T(1,128)} %bitcast.45), custom_call_target="tpu_custom_call" | custom-call | tf_op jit(solution)/shard_map/pack/pallas_call | solution.py:758
  2.3 4.0 %collective-permute-start.2 = (f32[264,128]{1,0:T(8,128)}, f32[264,128]{1,0:T(8,128)S(1)}, u32[]{:S(2)}, u32[]{:S(2)}) collective-permute-start(f32[264,128]{1,0:T(8,128)} %get-tuple-element.35.refs_0_), channel_id=1, source_target_pairs={{0,8},{4,12},{8,0},{12,4},{1,9},{5,13},{9,1},{13,5},{2,10},{6,14},... | collective-permute-start | bytes 405512 | tf_op jit(solution)/shard_map/ppermute | solution.py:756
  6.4 1.6 %collective-permute-start.1 = (f32[264,128]{1,0:T(8,128)}, f32[264,128]{1,0:T(8,128)S(1)}, u32[]{:S(2)}, u32[]{:S(2)}) collective-permute-start(f32[264,128]{1,0:T(8,128)} %get-tuple-element.35.refs_0_), channel_id=1, source_target_pairs={{0,4},{4,0},{8,12},{12,8},{1,5},{5,1},{9,13},{13,9},{2,6},{6,2},{1... | collective-permute-start | bytes 405512 | tf_op jit(solution)/shard_map/ppermute | solution.py:756
  7.9 1.5 %collective-permute-start = (f32[264,128]{1,0:T(8,128)}, f32[264,128]{1,0:T(8,128)S(1)}, u32[]{:S(2)}, u32[]{:S(2)}) collective-permute-start(f32[264,128]{1,0:T(8,128)} %get-tuple-element.35.refs_0_), channel_id=1, source_target_pairs={{0,2},{1,3},{2,0},{3,1},{4,6},{5,7},{6,4},{7,5},{8,10},{9,11},{10,... | collective-permute-start | bytes 405512 | tf_op jit(solution)/shard_map/ppermute | solution.py:756
  9.4 3.7 %collective-permute-done.2.refs_2_ = f32[264,128]{1,0:T(8,128)S(1)} collective-permute-done((f32[264,128]{1,0:T(8,128)}, f32[264,128]{1,0:T(8,128)S(1)}, u32[]{:S(2)}, u32[]{:S(2)}) %collective-permute-start.2) | collective-permute-done | bytes 135200 | tf_op jit(solution)/shard_map/ppermute | solution.py:756
  13.9 1.3 %fusion.8.cells_ref = s32[4,256]{1,0:T(4,128)} fusion(s32[256,4]{0,1:T(4,128)} %param.16, s32[]{:T(128)S(6)} %axis_index.25, s32[]{:T(128)S(6)} %axis_index.22), kind=kLoop, calls=%fused_computation.35 | loop fusion | flops 27648 | bytes 8200 | tf_op jit(solution)/shard_map/transpose | solution.py:768
  15.2 1.5 %collective-permute-start.5 = (f32[264,128]{1,0:T(8,128)S(1)}, f32[264,128]{1,0:T(8,128)S(1)}, u32[]{:S(2)}, u32[]{:S(2)}) collective-permute-start(f32[264,128]{1,0:T(8,128)S(1)} %collective-permute-done.2.refs_2_), channel_id=1, source_target_pairs={{0,2},{1,3},{2,0},{3,1},{4,6},{5,7},{6,4},{7,5},{8,10},{9,11},{10,... | collective-permute-start | bytes 405512 | tf_op jit(solution)/shard_map/ppermute | solution.py:756
  17.5 1.7 %collective-permute-done.3.refs_3_ = f32[264,128]{1,0:T(8,128)S(1)} collective-permute-done((f32[264,128]{1,0:T(8,128)S(1)}, f32[264,128]{1,0:T(8,128)S(1)}, u32[]{:S(2)}, u32[]{:S(2)}) %collective-permute-start.3) | collective-permute-done | bytes 135200 | tf_op jit(solution)/shard_map/ppermute | solution.py:756
  19.2 1.5 %collective-permute-start.6 = (f32[264,128]{1,0:T(8,128)S(1)}, f32[264,128]{1,0:T(8,128)S(1)}, u32[]{:S(2)}, u32[]{:S(2)}) collective-permute-start(f32[264,128]{1,0:T(8,128)S(1)} %collective-permute-done.3.refs_3_), channel_id=1, source_target_pairs={{0,2},{1,3},{2,0},{3,1},{4,6},{5,7},{6,4},{7,5},{8,10},{9,11},{10,... | collective-permute-start | bytes 405512 | tf_op jit(solution)/shard_map/ppermute | solution.py:756
  20.7 4.2 %deal.1 = (f32[8,1024]{1,0:T(8,128)}, f32[144,256]{1,0:T(8,128)}, s32[8,256]{1,0:T(8,128)}, s32[24,128]{1,0:T(8,128)}, f32[2,1152,128]{2,1,0:T(8,128)}, /*index=5*/bf16[64,48]{1,0:T(8,128)(2,1)}, f32[264,128]{1,0:T(8,128)}) custom-call(s32[4,256]{1,0:T(4,128)} %fusion.8.cells_ref, f32[6,256]{1,0:T(8,128)} %geometry_ref.1, ...), custom_call_target="tpu_custom_call", output_to_operand_aliasing={{6}: (5, {})} | custom-call | flops 6442450944 | bytes 4194304 | tf_op jit(solution)/shard_map/deal/pallas_call | solution.py:771
  28.7 38.7 %step.1 = (f32[3,256]{1,0:T(4,128)}, f32[48,256]{1,0:T(8,128)}, f32[10,264,128]{2,1,0:T(8,128)}, f32[10,264,128]{2,1,0:T(8,128)}) custom-call(s32[8,256]{1,0:T(8,128)} %get-tuple-element.36.tile_cell_ref, s32[24,128]{1,0:T(8,128)} %get-tuple-element.37.tile_start_ref, f32[8,1024]{1,0:T(8,128)} %get-tuple-element.38.meta_ref, s32[4,256]{1,0:T(4,128)} %fusion.8.cells_ref, ...), custom_call_target="tpu_custom_call" | custom-call | tf_op jit(solution)/shard_map/step/pallas_call | solution.py:797
  67.5 3.2 %collective-permute-done.15 = f32[10,264,128]{2,1,0:T(8,128)S(1)} collective-permute-done((f32[10,264,128]{2,1,0:T(8,128)}, f32[10,264,128]{2,1,0:T(8,128)S(1)}, u32[]{:S(2)}, u32[]{:S(2)}) %collective-permute-start.15) | collective-permute-done | bytes 1351712 | tf_op jit(solution)/shard_map/ppermute | solution.py:756
  70.7 1.6 %fusion = (f32[264,128]{1,0:T(8,128)S(1)}, f32[264,128]{1,0:T(8,128)S(1)}, f32[264,128]{1,0:T(8,128)S(1)}, f32[264,128]{1,0:T(8,128)S(1)}, f32[264,128]{1,0:T(8,...) fusion(f32[10,264,128]{2,1,0:T(8,128)S(1)} %collective-permute-, ...), kind=kLoop, calls=%fused_computation.1 | loop fusion | flops 168960 | bytes 4460544 | tf_op jit(solution)/shard_map/add | solution.py:839
  72.3 1.5 %collective-permute-start.23 = (f32[264,128]{1,0:T(8,128)S(1)}, f32[264,128]{1,0:T(8,128)S(1)}, u32[]{:S(2)}, u32[]{:S(2)}) collective-permute-start(f32[264,128]{1,0:T(8,128)S(1)} %get-tuple-element.68), channel_id=1, source_target_pairs={{0,2},{1,3},{2,0},{3,1},{4,6},{5,7},{6,4},{7,5},{8,10},{9,11},{10,... | collective-permute-start | bytes 405512 | tf_op jit(solution)/shard_map/ppermute | solution.py:756
  74.4 1.5 %collective-permute-start.19 = (f32[264,128]{1,0:T(8,128)S(1)}, f32[264,128]{1,0:T(8,128)S(1)}, u32[]{:S(2)}, u32[]{:S(2)}) collective-permute-start(f32[264,128]{1,0:T(8,128)S(1)} %get-tuple-element.70), channel_id=1, source_target_pairs={{0,2},{1,3},{2,0},{3,1},{4,6},{5,7},{6,4},{7,5},{8,10},{9,11},{10,... | collective-permute-start | bytes 405512 | tf_op jit(solution)/shard_map/ppermute | solution.py:756
  76.4 1.5 %collective-permute-start.16 = (f32[264,128]{1,0:T(8,128)S(1)}, f32[264,128]{1,0:T(8,128)S(1)}, u32[]{:S(2)}, u32[]{:S(2)}) collective-permute-start(f32[264,128]{1,0:T(8,128)S(1)} %get-tuple-element.72), channel_id=1, source_target_pairs={{0,2},{1,3},{2,0},{3,1},{4,6},{5,7},{6,4},{7,5},{8,10},{9,11},{10,... | collective-permute-start | bytes 405512 | tf_op jit(solution)/shard_map/ppermute | solution.py:756
  77.9 0.9 collective-permute-done.23
  78.8 3.3 %collective-permute-start.24 = (f32[256,128]{1,0:T(8,128)S(1)}, f32[256,128]{1,0:T(8,128)S(1)}, u32[]{:S(2)}, u32[]{:S(2)}) collective-permute-start(f32[256,128]{1,0:T(8,128)S(1)} %slice_add_fusion.5), channel_id=1, source_target_pairs={{0,8},{4,12},{8,0},{12,4},{1,9},{5,13},{9,1},{13,5},{2,10},{6,14},... | collective-permute-start | bytes 393224 | tf_op jit(solution)/shard_map/ppermute | solution.py:756
  83.0 1.5 %collective-permute-done.19 = f32[264,128]{1,0:T(8,128)S(1)} collective-permute-done((f32[264,128]{1,0:T(8,128)S(1)}, f32[264,128]{1,0:T(8,128)S(1)}, u32[]{:S(2)}, u32[]{:S(2)}) %collective-permute-start.19) | collective-permute-done | bytes 135200 | tf_op jit(solution)/shard_map/ppermute | solution.py:756
  84.6 2.9 %collective-permute-done.17 = f32[264,128]{1,0:T(8,128)S(1)} collective-permute-done((f32[264,128]{1,0:T(8,128)S(1)}, f32[264,128]{1,0:T(8,128)S(1)}, u32[]{:S(2)}, u32[]{:S(2)}) %collective-permute-start.17) | collective-permute-done | bytes 135200 | tf_op jit(solution)/shard_map/ppermute | solution.py:756
  87.5 1.3 %collective-permute-start.18 = (f32[264,128]{1,0:T(8,128)S(1)}, f32[264,128]{1,0:T(8,128)S(1)}, u32[]{:S(2)}, u32[]{:S(2)}) collective-permute-start(f32[264,128]{1,0:T(8,128)S(1)} %add_add_fusion.3), channel_id=1, source_target_pairs={{0,4},{4,0},{8,12},{12,8},{1,5},{5,1},{9,13},{13,9},{2,6},{6,2},{1... | collective-permute-start | bytes 405512 | tf_op jit(solution)/shard_map/ppermute | solution.py:756
  89.6 1.4 %collective-permute-start.25 = (f32[256,128]{1,0:T(8,128)S(1)}, f32[256,128]{1,0:T(8,128)S(1)}, u32[]{:S(2)}, u32[]{:S(2)}) collective-permute-start(f32[256,128]{1,0:T(8,128)S(1)} %add.114), channel_id=1, source_target_pairs={{0,4},{4,0},{8,12},{12,8},{1,5},{5,1},{9,13},{13,9},{2,6},{6,2},{1... | collective-permute-start | bytes 393224 | tf_op jit(solution)/shard_map/ppermute | solution.py:756
  91.0 2.3 %collective-permute-start.22 = (f32[264,128]{1,0:T(8,128)S(1)}, f32[264,128]{1,0:T(8,128)S(1)}, u32[]{:S(2)}, u32[]{:S(2)}) collective-permute-start(f32[264,128]{1,0:T(8,128)S(1)} %add_add_fusion.1), channel_id=1, source_target_pairs={{0,8},{4,12},{8,0},{12,4},{1,9},{5,13},{9,1},{13,5},{2,10},{6,14},... | collective-permute-start | bytes 405512 | tf_op jit(solution)/shard_map/ppermute | solution.py:756
  93.3 5.0 %collective-permute-done.25 = f32[256,128]{1,0:T(8,128)S(1)} collective-permute-done((f32[256,128]{1,0:T(8,128)S(1)}, f32[256,128]{1,0:T(8,128)S(1)}, u32[]{:S(2)}, u32[]{:S(2)}) %collective-permute-start.25) | collective-permute-done | bytes 131104 | tf_op jit(solution)/shard_map/ppermute | solution.py:756
  (75 shorter events, 10.8 us)
Async XLA Ops:
  2.3 10.8 %collective-permute-start.2 = (f32[264,128]{1,0:T(8,128)}, f32[264,128]{1,0:T(8,128)S(1)}, u32[]{:S(2)}, u32[]{:S(2)}) collective-permute-start(f32[264,128]{1,0:T(8,128)} %get-tuple-element.35.refs_0_), channel_id=1, source_target_pairs={{0,8},{4,12},{8,0},{12,4},{1,9},{5,13},{9,1},{13,5},{2,10},{6,14},... | collective-permute-start | bytes 405512 | tf_op jit(solution)/shard_map/ppermute | solution.py:756
  6.4 10.3 %collective-permute-start.1 = (f32[264,128]{1,0:T(8,128)}, f32[264,128]{1,0:T(8,128)S(1)}, u32[]{:S(2)}, u32[]{:S(2)}) collective-permute-start(f32[264,128]{1,0:T(8,128)} %get-tuple-element.35.refs_0_), channel_id=1, source_target_pairs={{0,4},{4,0},{8,12},{12,8},{1,5},{5,1},{9,13},{13,9},{2,6},{6,2},{1... | collective-permute-start | bytes 405512 | tf_op jit(solution)/shard_map/ppermute | solution.py:756
  7.9 8.8 %collective-permute-start = (f32[264,128]{1,0:T(8,128)}, f32[264,128]{1,0:T(8,128)S(1)}, u32[]{:S(2)}, u32[]{:S(2)}) collective-permute-start(f32[264,128]{1,0:T(8,128)} %get-tuple-element.35.refs_0_), channel_id=1, source_target_pairs={{0,2},{1,3},{2,0},{3,1},{4,6},{5,7},{6,4},{7,5},{8,10},{9,11},{10,... | collective-permute-start | bytes 405512 | tf_op jit(solution)/shard_map/ppermute | solution.py:756
  13.2 4.2 %collective-permute-start.9 = (f32[264,128]{1,0:T(8,128)S(1)}, f32[264,128]{1,0:T(8,128)S(1)}, u32[]{:S(2)}, u32[]{:S(2)}) collective-permute-start(f32[264,128]{1,0:T(8,128)S(1)} %collective-permute-done.2.refs_2_), channel_id=1, source_target_pairs={{0,1},{1,0},{2,3},{3,2},{4,5},{5,4},{6,7},{7,6},{8,9},{9,8},{10,11... | collective-permute-start | bytes 405512 | tf_op jit(solution)/shard_map/ppermute | solution.py:756
  13.2 6.0 %collective-permute-start.3 = (f32[264,128]{1,0:T(8,128)S(1)}, f32[264,128]{1,0:T(8,128)S(1)}, u32[]{:S(2)}, u32[]{:S(2)}) collective-permute-start(f32[264,128]{1,0:T(8,128)S(1)} %collective-permute-done.2.refs_2_), channel_id=1, source_target_pairs={{0,4},{4,0},{8,12},{12,8},{1,5},{5,1},{9,13},{13,9},{2,6},{6,2},{1... | collective-permute-start | bytes 405512 | tf_op jit(solution)/shard_map/ppermute | solution.py:756
  15.2 9.8 %collective-permute-start.5 = (f32[264,128]{1,0:T(8,128)S(1)}, f32[264,128]{1,0:T(8,128)S(1)}, u32[]{:S(2)}, u32[]{:S(2)}) collective-permute-start(f32[264,128]{1,0:T(8,128)S(1)} %collective-permute-done.2.refs_2_), channel_id=1, source_target_pairs={{0,2},{1,3},{2,0},{3,1},{4,6},{5,7},{6,4},{7,5},{8,10},{9,11},{10,... | collective-permute-start | bytes 405512 | tf_op jit(solution)/shard_map/ppermute | solution.py:756
  16.7 8.4 %collective-permute-start.8 = (f32[264,128]{1,0:T(8,128)S(1)}, f32[264,128]{1,0:T(8,128)S(1)}, u32[]{:S(2)}, u32[]{:S(2)}) collective-permute-start(f32[264,128]{1,0:T(8,128)S(1)} %collective-permute-done.1.refs_1_), channel_id=1, source_target_pairs={{0,1},{1,0},{2,3},{3,2},{4,5},{5,4},{6,7},{7,6},{8,9},{9,8},{10,11... | collective-permute-start | bytes 405512 | tf_op jit(solution)/shard_map/ppermute | solution.py:756
  16.7 8.9 %collective-permute-start.4 = (f32[264,128]{1,0:T(8,128)S(1)}, f32[264,128]{1,0:T(8,128)S(1)}, u32[]{:S(2)}, u32[]{:S(2)}) collective-permute-start(f32[264,128]{1,0:T(8,128)S(1)} %collective-permute-done.1.refs_1_), channel_id=1, source_target_pairs={{0,2},{1,3},{2,0},{3,1},{4,6},{5,7},{6,4},{7,5},{8,10},{9,11},{10,... | collective-permute-start | bytes 405512 | tf_op jit(solution)/shard_map/ppermute | solution.py:756
  17.3 8.4 %collective-permute-start.11 = (f32[264,128]{1,0:T(8,128)S(1)}, f32[264,128]{1,0:T(8,128)S(1)}, u32[]{:S(2)}, u32[]{:S(2)}) collective-permute-start(f32[264,128]{1,0:T(8,128)S(1)} %collective-permute-done.other_ref.refs_4_), channel_id=1, source_target_pairs={{0,1},{1,0},{2,3},{3,2},{4,5},{5,4},{6,7},{7,6},{8,9},{9,8},{10,11... | collective-permute-start | bytes 405512 | tf_op jit(solution)/shard_map/ppermute | solution.py:756
  19.2 7.5 %collective-permute-start.6 = (f32[264,128]{1,0:T(8,128)S(1)}, f32[264,128]{1,0:T(8,128)S(1)}, u32[]{:S(2)}, u32[]{:S(2)}) collective-permute-start(f32[264,128]{1,0:T(8,128)S(1)} %collective-permute-done.3.refs_3_), channel_id=1, source_target_pairs={{0,2},{1,3},{2,0},{3,1},{4,6},{5,7},{6,4},{7,5},{8,10},{9,11},{10,... | collective-permute-start | bytes 405512 | tf_op jit(solution)/shard_map/ppermute | solution.py:756
  25.0 1.7 %collective-permute-start.7 = (f32[264,128]{1,0:T(8,128)}, f32[264,128]{1,0:T(8,128)S(1)}, u32[]{:S(2)}, u32[]{:S(2)}) collective-permute-start(f32[264,128]{1,0:T(8,128)} %get-tuple-element.42), channel_id=1, source_target_pairs={{0,1},{1,0},{2,3},{3,2},{4,5},{5,4},{6,7},{7,6},{8,9},{9,8},{10,11... | collective-permute-start | bytes 405512 | tf_op jit(solution)/shard_map/ppermute | solution.py:756
  25.1 1.9 %collective-permute-start.10 = (f32[264,128]{1,0:T(8,128)S(1)}, f32[264,128]{1,0:T(8,128)S(1)}, u32[]{:S(2)}, u32[]{:S(2)}) collective-permute-start(f32[264,128]{1,0:T(8,128)S(1)} %collective-permute-done.3.refs_3_), channel_id=1, source_target_pairs={{0,1},{1,0},{2,3},{3,2},{4,5},{5,4},{6,7},{7,6},{8,9},{9,8},{10,11... | collective-permute-start | bytes 405512 | tf_op jit(solution)/shard_map/ppermute | solution.py:756
  25.7 1.4 %collective-permute-start.12 = (f32[264,128]{1,0:T(8,128)S(1)}, f32[264,128]{1,0:T(8,128)S(1)}, u32[]{:S(2)}, u32[]{:S(2)}) collective-permute-start(f32[264,128]{1,0:T(8,128)S(1)} %collective-permute-done.4.refs_5_), channel_id=1, source_target_pairs={{0,1},{1,0},{2,3},{3,2},{4,5},{5,4},{6,7},{7,6},{8,9},{9,8},{10,11... | collective-permute-start | bytes 405512 | tf_op jit(solution)/shard_map/ppermute | solution.py:756
  67.3 3.4 %collective-permute-start.15 = (f32[10,264,128]{2,1,0:T(8,128)}, f32[10,264,128]{2,1,0:T(8,128)S(1)}, u32[]{:S(2)}, u32[]{:S(2)}) collective-permute-start(f32[10,264,128]{2,1,0:T(8,128)} %get-tuple-element.45), channel_id=1, source_target_pairs={{0,1},{1,0},{2,3},{3,2},{4,5},{5,4},{6,7},{7,6},{8,9},{9,8},{10,11... | collective-permute-start | bytes 4055048 | tf_op jit(solution)/shard_map/ppermute | solution.py:756
  72.3 6.5 %collective-permute-start.23 = (f32[264,128]{1,0:T(8,128)S(1)}, f32[264,128]{1,0:T(8,128)S(1)}, u32[]{:S(2)}, u32[]{:S(2)}) collective-permute-start(f32[264,128]{1,0:T(8,128)S(1)} %get-tuple-element.68), channel_id=1, source_target_pairs={{0,2},{1,3},{2,0},{3,1},{4,6},{5,7},{6,4},{7,5},{8,10},{9,11},{10,... | collective-permute-start | bytes 405512 | tf_op jit(solution)/shard_map/ppermute | solution.py:756
  73.8 8.3 %collective-permute-start.20 = (f32[264,128]{1,0:T(8,128)S(1)}, f32[264,128]{1,0:T(8,128)S(1)}, u32[]{:S(2)}, u32[]{:S(2)}) collective-permute-start(f32[264,128]{1,0:T(8,128)S(1)} %get-tuple-element.69), channel_id=1, source_target_pairs={{0,2},{1,3},{2,0},{3,1},{4,6},{5,7},{6,4},{7,5},{8,10},{9,11},{10,... | collective-permute-start | bytes 405512 | tf_op jit(solution)/shard_map/ppermute | solution.py:756
  74.4 10.2 %collective-permute-start.19 = (f32[264,128]{1,0:T(8,128)S(1)}, f32[264,128]{1,0:T(8,128)S(1)}, u32[]{:S(2)}, u32[]{:S(2)}) collective-permute-start(f32[264,128]{1,0:T(8,128)S(1)} %get-tuple-element.70), channel_id=1, source_target_pairs={{0,2},{1,3},{2,0},{3,1},{4,6},{5,7},{6,4},{7,5},{8,10},{9,11},{10,... | collective-permute-start | bytes 405512 | tf_op jit(solution)/shard_map/ppermute | solution.py:756
  75.8 11.6 %collective-permute-start.17 = (f32[264,128]{1,0:T(8,128)S(1)}, f32[264,128]{1,0:T(8,128)S(1)}, u32[]{:S(2)}, u32[]{:S(2)}) collective-permute-start(f32[264,128]{1,0:T(8,128)S(1)} %get-tuple-element.71), channel_id=1, source_target_pairs={{0,2},{1,3},{2,0},{3,1},{4,6},{5,7},{6,4},{7,5},{8,10},{9,11},{10,... | collective-permute-start | bytes 405512 | tf_op jit(solution)/shard_map/ppermute | solution.py:756
  76.4 13.2 %collective-permute-start.16 = (f32[264,128]{1,0:T(8,128)S(1)}, f32[264,128]{1,0:T(8,128)S(1)}, u32[]{:S(2)}, u32[]{:S(2)}) collective-permute-start(f32[264,128]{1,0:T(8,128)S(1)} %get-tuple-element.72), channel_id=1, source_target_pairs={{0,2},{1,3},{2,0},{3,1},{4,6},{5,7},{6,4},{7,5},{8,10},{9,11},{10,... | collective-permute-start | bytes 405512 | tf_op jit(solution)/shard_map/ppermute | solution.py:756
  78.8 10.8 %collective-permute-start.24 = (f32[256,128]{1,0:T(8,128)S(1)}, f32[256,128]{1,0:T(8,128)S(1)}, u32[]{:S(2)}, u32[]{:S(2)}) collective-permute-start(f32[256,128]{1,0:T(8,128)S(1)} %slice_add_fusion.5), channel_id=1, source_target_pairs={{0,8},{4,12},{8,0},{12,4},{1,9},{5,13},{9,1},{13,5},{2,10},{6,14},... | collective-permute-start | bytes 393224 | tf_op jit(solution)/shard_map/ppermute | solution.py:756
  82.1 8.8 %collective-permute-start.21 = (f32[264,128]{1,0:T(8,128)S(1)}, f32[264,128]{1,0:T(8,128)S(1)}, u32[]{:S(2)}, u32[]{:S(2)}) collective-permute-start(f32[264,128]{1,0:T(8,128)S(1)} %add_add_fusion), channel_id=1, source_target_pairs={{0,4},{4,0},{8,12},{12,8},{1,5},{5,1},{9,13},{13,9},{2,6},{6,2},{1... | collective-permute-start | bytes 405512 | tf_op jit(solution)/shard_map/ppermute | solution.py:756
  87.5 11.5 %collective-permute-start.18 = (f32[264,128]{1,0:T(8,128)S(1)}, f32[264,128]{1,0:T(8,128)S(1)}, u32[]{:S(2)}, u32[]{:S(2)}) collective-permute-start(f32[264,128]{1,0:T(8,128)S(1)} %add_add_fusion.3), channel_id=1, source_target_pairs={{0,4},{4,0},{8,12},{12,8},{1,5},{5,1},{9,13},{13,9},{2,6},{6,2},{1... | collective-permute-start | bytes 405512 | tf_op jit(solution)/shard_map/ppermute | solution.py:756
  89.6 8.7 %collective-permute-start.25 = (f32[256,128]{1,0:T(8,128)S(1)}, f32[256,128]{1,0:T(8,128)S(1)}, u32[]{:S(2)}, u32[]{:S(2)}) collective-permute-start(f32[256,128]{1,0:T(8,128)S(1)} %add.114), channel_id=1, source_target_pairs={{0,4},{4,0},{8,12},{12,8},{1,5},{5,1},{9,13},{13,9},{2,6},{6,2},{1... | collective-permute-start | bytes 393224 | tf_op jit(solution)/shard_map/ppermute | solution.py:756
  91.0 8.0 %collective-permute-start.22 = (f32[264,128]{1,0:T(8,128)S(1)}, f32[264,128]{1,0:T(8,128)S(1)}, u32[]{:S(2)}, u32[]{:S(2)}) collective-permute-start(f32[264,128]{1,0:T(8,128)S(1)} %add_add_fusion.1), channel_id=1, source_target_pairs={{0,8},{4,12},{8,0},{12,4},{1,9},{5,13},{9,1},{13,5},{2,10},{6,14},... | collective-permute-start | bytes 405512 | tf_op jit(solution)/shard_map/ppermute | solution.py:756
  (17 other events, 57.7 us)

commit v5 on v4

--- a/solution.py
+++ b/solution.py
@@ -272,7 +272,7 @@
 ROWS = 264
 HEAD_ROW = 256
 APP_ROW = 260
-VMEM_LIMIT = 56 * 1024 * 1024
+VMEM_LIMIT = 48 * 1024 * 1024
 SIN = (
     6.283185005187988,
     -41.341590881347656,
@@ -517,8 +517,10 @@
     (
         rendered_ref,
         codes_grad_ref,
-        keep_ref,
-        send_ref,
+        keep_near_ref,
+        keep_far_ref,
+        send_near_ref,
+        send_far_ref,
         encoded_ref,
         first_ref,
         second_ref,
@@ -704,17 +706,16 @@
     copies = []
 
     def emit(half):
-        for district in (2 * half, 2 * half + 1):
+        for district in (2 * half + 1, 2 * half):
             members = sums_ref.at[pl.ds(district * num_cell, num_cell)]
             total = sums_ref[district * num_cell]
             for s in range(1, num_cell):
                 total = total + sums_ref[district * num_cell + s]
             sums_ref[cells + district] = total
-            out_ref = (keep_ref, send_ref)[half]
-            at = (district % 2) * (num_cell + 1)
+            out_ref = (keep_near_ref, keep_far_ref, send_near_ref, send_far_ref)[district]
             for source, sink in (
-                (members, out_ref.at[pl.ds(at, num_cell)]),
-                (sums_ref.at[cells + district], out_ref.at[at + num_cell]),
+                (members, out_ref.at[pl.ds(0, num_cell)]),
+                (sums_ref.at[cells + district], out_ref.at[num_cell]),
             ):
                 copies.append(pltpu.make_async_copy(source, sink, semaphore.at[len(copies)]))
                 copies[-1].start()
@@ -763,8 +764,8 @@
     params = pltpu.CompilerParams(vmem_limit_bytes=VMEM_LIMIT)
 
     crossed_own = flip(own, 2)
-    away = (crossing % num_district) ^ me_district
-    steps = (crossing // num_district) ^ me_cell
+    away = (crossing & 3) ^ me_district
+    steps = (crossing >> 2) ^ me_cell
     virtual = (((away & 1) * 2 + (away >> 1)) * num_cell + steps).T
     halves = lanes // 128
     default = pl.BlockSpec()
@@ -793,16 +794,14 @@
     weights = near + flipped + [flip(piece, 1) for piece in [passed] + near[1:] + flipped]
 
 
-    half = 2 * (num_cell + 1)
-    rendered, codes_grad, keep, send = pl.pallas_call(
+    rendered, codes_grad, keep, keep_far, send, send_far = pl.pallas_call(
         functools.partial(step_kernel, cells, samples),
         in_specs=[smem, smem] + [vmem] * (7 + cells),
-        out_specs=[vmem, vmem, anywhere, anywhere],
+        out_specs=[vmem, vmem, anywhere, vmem, anywhere, anywhere],
         out_shape=[
             jax.ShapeDtypeStruct((3, rays), F32),
             jax.ShapeDtypeStruct((width, rays), F32),
-            jax.ShapeDtypeStruct((half, ROWS, 128), F32),
-            jax.ShapeDtypeStruct((half, ROWS, 128), F32),
+            *[jax.ShapeDtypeStruct((num_cell + 1, ROWS, 128), F32)] * 4,
         ],
         scratch_shapes=[
             pltpu.VMEM((tiles, 128, lanes), BF16),
@@ -833,10 +832,9 @@
         *weights,
     )
 
-    crossed = flip(send, 1)
+    cross_far, crossed = flip(send_far, 1), flip(send, 1)
     order = [3, 2, num_cell, 1, 0]
-    far = num_cell + 1
-    pieces = {s: flip(keep[far + s] + crossed[far + s], 2) for s in order}
+    pieces = {s: flip(keep_far[s] + cross_far[s], 2) for s in order}
     for s in order:
         near_part, cross_part, other = lax.optimization_barrier((keep[s], crossed[s], pieces[s]))
         pieces[s] = near_part + cross_part + other

time: 101 us -> 98.5 us (0.975)
  local copies, waits for them, and re-layouts: 2.45 us -> 5.91 us
  Pallas kernels: 44.6 us -> 41.9 us
  other arithmetic: 3.69 us -> 1.6 us
  starting transfers between devices: 27.7 us -> 26.3 us
    unnamed x31 -> x17, local copies, waits for them, and re-layouts: 1.19 us -> 4.58 us
    pallas_call x1, Pallas kernels: 4.22 us -> 2.17 us  [resident(): pl.pallas_call(functools.partial(deal_kernel, cells, samples), in_specs=[...]
    add x1, other arithmetic: 1.55 us -> 0.07 us  [resident(): pieces = {s: flip(keep_far[s] + cross_far[s], 2) for s in order}]
    ppermute x26 -> x27, starting transfers between devices: 27.7 us -> 26.3 us  [flip(): lax.ppermute(x, axis, [(i, i ^ bits) for i in range(lax.axis_size(axis))])]
    ppermute x26 -> x27, waiting for transfers between devices: 21.5 us -> 21.7 us  [flip(): lax.ppermute(x, axis, [(i, i ^ bits) for i in range(lax.axis_size(axis))])]
  transfers between devices with their start and end apart: 26 -> 27, of which waited for: 12 -> 13; matrix products, arithmetic and copies ran while one was open for 2% -> 2% of each run, Pallas kernels for 4% -> 2%
where the time goes in v5:
time: 98.5 us; the launch traced here: 98.2 us
  Pallas kernels  41.9 us (43%)
  starting transfers between devices  26.3 us (27%)
  waiting for transfers between devices  21.7 us (22%)
  local copies, waits for them, and re-layouts  5.91 us (6%)
  other arithmetic  1.6 us (2%)
    pallas_call x1, Pallas kernels, resident(): pl.pallas_call(functools.partial(step_kernel, cells, samples), in_specs=[...  38 us
    ppermute x27, starting transfers between devices, flip(): lax.ppermute(x, axis, [(i, i ^ bits) for i in range(lax.axis_size(axis))])  26.3 us
    ppermute x27, waiting for transfers between devices, flip(): lax.ppermute(x, axis, [(i, i ^ bits) for i in range(lax.axis_size(axis))])  21.7 us
    unnamed x17, local copies, waits for them, and re-layouts  4.58 us
    pallas_call x1, Pallas kernels, resident(): pl.pallas_call(functools.partial(deal_kernel, cells, samples), in_specs=[...  2.17 us
  transfers between devices with their start and end apart: 27, of which 13 were waited for; matrix products, arithmetic and copies ran while one was open for 2% of the time, Pallas kernels for 2%

profile of v5, /device:TPU:0, one launch (start us, length us, event | category | flops | bytes accessed | tf_op | source)
XLA Modules:
  0.0 98.2 jit_solution(17391125928195099408)
XLA Ops:
  0.6 1.7 %pack.1 = (f32[264,128]{1,0:T(8,128)}, f32[264,128]{1,0:T(8,128)}) custom-call(bf16[1,2,128,128]{3,2,1,0:T(8,128)(2,1)} %layers_ref.1, bf16[1,2,128,128]{3,2,1,0:T(8,128)(2,1)} %prior_ref.1, bf16[1,4,128]{2,1,0:T(4,128)(2,1)} %head_ref.1, f32[3,1,48]{2,1,0:T(1,128)} %bitcast.46), custom_call_target="tpu_custom_call" | custom-call | tf_op jit(solution)/shard_map/pack/pallas_call | solution.py:759
  2.3 4.0 %collective-permute-start.2 = (f32[264,128]{1,0:T(8,128)}, f32[264,128]{1,0:T(8,128)S(1)}, u32[]{:S(2)}, u32[]{:S(2)}) collective-permute-start(f32[264,128]{1,0:T(8,128)} %get-tuple-element.37.refs_0_), channel_id=1, source_target_pairs={{0,8},{4,12},{8,0},{12,4},{1,9},{5,13},{9,1},{13,5},{2,10},{6,14},... | collective-permute-start | bytes 405512 | tf_op jit(solution)/shard_map/ppermute | solution.py:757
  6.4 1.6 %collective-permute-start.1 = (f32[264,128]{1,0:T(8,128)}, f32[264,128]{1,0:T(8,128)S(1)}, u32[]{:S(2)}, u32[]{:S(2)}) collective-permute-start(f32[264,128]{1,0:T(8,128)} %get-tuple-element.37.refs_0_), channel_id=1, source_target_pairs={{0,4},{4,0},{8,12},{12,8},{1,5},{5,1},{9,13},{13,9},{2,6},{6,2},{1... | collective-permute-start | bytes 405512 | tf_op jit(solution)/shard_map/ppermute | solution.py:757
  7.9 1.5 %collective-permute-start = (f32[264,128]{1,0:T(8,128)}, f32[264,128]{1,0:T(8,128)S(1)}, u32[]{:S(2)}, u32[]{:S(2)}) collective-permute-start(f32[264,128]{1,0:T(8,128)} %get-tuple-element.37.refs_0_), channel_id=1, source_target_pairs={{0,2},{1,3},{2,0},{3,1},{4,6},{5,7},{6,4},{7,5},{8,10},{9,11},{10,... | collective-permute-start | bytes 405512 | tf_op jit(solution)/shard_map/ppermute | solution.py:757
  9.4 3.7 %collective-permute-done.2.refs_2_ = f32[264,128]{1,0:T(8,128)S(1)} collective-permute-done((f32[264,128]{1,0:T(8,128)}, f32[264,128]{1,0:T(8,128)S(1)}, u32[]{:S(2)}, u32[]{:S(2)}) %collective-permute-start.2) | collective-permute-done | bytes 135200 | tf_op jit(solution)/shard_map/ppermute | solution.py:757
  14.6 1.5 %collective-permute-start.5 = (f32[264,128]{1,0:T(8,128)S(1)}, f32[264,128]{1,0:T(8,128)S(1)}, u32[]{:S(2)}, u32[]{:S(2)}) collective-permute-start(f32[264,128]{1,0:T(8,128)S(1)} %collective-permute-done.2.refs_2_), channel_id=1, source_target_pairs={{0,2},{1,3},{2,0},{3,1},{4,6},{5,7},{6,4},{7,5},{8,10},{9,11},{10,... | collective-permute-start | bytes 405512 | tf_op jit(solution)/shard_map/ppermute | solution.py:757
  16.9 2.3 %collective-permute-done.3.refs_3_ = f32[264,128]{1,0:T(8,128)S(1)} collective-permute-done((f32[264,128]{1,0:T(8,128)S(1)}, f32[264,128]{1,0:T(8,128)S(1)}, u32[]{:S(2)}, u32[]{:S(2)}) %collective-permute-start.3) | collective-permute-done | bytes 135200 | tf_op jit(solution)/shard_map/ppermute | solution.py:757
  19.2 1.5 %collective-permute-start.6 = (f32[264,128]{1,0:T(8,128)S(1)}, f32[264,128]{1,0:T(8,128)S(1)}, u32[]{:S(2)}, u32[]{:S(2)}) collective-permute-start(f32[264,128]{1,0:T(8,128)S(1)} %collective-permute-done.3.refs_3_), channel_id=1, source_target_pairs={{0,2},{1,3},{2,0},{3,1},{4,6},{5,7},{6,4},{7,5},{8,10},{9,11},{10,... | collective-permute-start | bytes 405512 | tf_op jit(solution)/shard_map/ppermute | solution.py:757
  20.7 0.9 copy-done.4
  23.7 2.2 %deal.1 = (f32[8,1024]{1,0:T(8,128)S(1)}, f32[144,256]{1,0:T(8,128)S(1)}, s32[8,256]{1,0:T(8,128)S(1)}, s32[24,128]{1,0:T(8,128)S(1)}, f32[2,1152,128]{2,1,0:T(8...) custom-call(s32[4,256]{1,0:T(4,128)S(1)} %add_bitcast_fusion.cells_ref, ...), custom_call_target="tpu_custom_call", output_to_operand_aliasing={{6}: (5, {})} | custom-call | flops 6442450944 | bytes 4194304 | tf_op jit(solution)/shard_map/deal/pallas_call | solution.py:772
  25.9 1.0 %copy-done = f32[2,1152,128]{2,1,0:T(8,128)} copy-done((f32[2,1152,128]{2,1,0:T(8,128)}, f32[2,1152,128]{2,1,0:T(8,128)S(1)}, u32[]{:S(2)}) %copy-start) | copy-done | bytes 1179672
  29.3 38.0 %step.1 = (f32[3,256]{1,0:T(4,128)}, f32[48,256]{1,0:T(8,128)}, f32[5,264,128]{2,1,0:T(8,128)S(1)}, f32[5,264,128]{2,1,0:T(8,128)S(1)}, f32[5,264,128]{2,1,0:T(8,128)S(1)}, /*index=5*/f32[5,264,128]{2,1,0:T(8,128)S(1)}) custom-call(s32[8,256]{1,0:T(8,128)S(1)} %get-tuple-element.38.tile_cell_ref, s32[24,128]{1,0:T(8,128)S(1)} %get-tuple-element.39.tile_start_ref, ...), custom_call_target="tpu_custom_call" | custom-call | tf_op jit(solution)/shard_map/step/pallas_call | solution.py:797
  68.0 1.6 %collective-permute-done.16 = f32[5,264,128]{2,1,0:T(8,128)S(1)} collective-permute-done((f32[5,264,128]{2,1,0:T(8,128)S(1)}, f32[5,264,128]{2,1,0:T(8,128)S(1)}, u32[]{:S(2)}, u32[]{:S(2)}) %collective-permute-start.16) | collective-permute-done | bytes 675872 | tf_op jit(solution)/shard_map/ppermute | solution.py:757
  70.2 1.5 %collective-permute-start.21 = (f32[264,128]{1,0:T(8,128)S(1)}, f32[264,128]{1,0:T(8,128)S(1)}, u32[]{:S(2)}, u32[]{:S(2)}) collective-permute-start(f32[264,128]{1,0:T(8,128)S(1)} %get-tuple-element.73), channel_id=1, source_target_pairs={{0,2},{1,3},{2,0},{3,1},{4,6},{5,7},{6,4},{7,5},{8,10},{9,11},{10,... | collective-permute-start | bytes 405512 | tf_op jit(solution)/shard_map/ppermute | solution.py:757
  72.2 1.5 %collective-permute-start.18 = (f32[264,128]{1,0:T(8,128)S(1)}, f32[264,128]{1,0:T(8,128)S(1)}, u32[]{:S(2)}, u32[]{:S(2)}) collective-permute-start(f32[264,128]{1,0:T(8,128)S(1)} %get-tuple-element.75), channel_id=1, source_target_pairs={{0,2},{1,3},{2,0},{3,1},{4,6},{5,7},{6,4},{7,5},{8,10},{9,11},{10,... | collective-permute-start | bytes 405512 | tf_op jit(solution)/shard_map/ppermute | solution.py:757
  74.3 1.8 %collective-permute-done.24 = f32[264,128]{1,0:T(8,128)S(1)} collective-permute-done((f32[264,128]{1,0:T(8,128)S(1)}, f32[264,128]{1,0:T(8,128)S(1)}, u32[]{:S(2)}, u32[]{:S(2)}) %collective-permute-start.24) | collective-permute-done | bytes 135200 | tf_op jit(solution)/shard_map/ppermute | solution.py:757
  76.1 2.3 %collective-permute-start.25 = (f32[256,128]{1,0:T(8,128)S(1)}, f32[256,128]{1,0:T(8,128)S(1)}, u32[]{:S(2)}, u32[]{:S(2)}) collective-permute-start(f32[256,128]{1,0:T(8,128)S(1)} %slice_add_fusion.5), channel_id=1, source_target_pairs={{0,8},{4,12},{8,0},{12,4},{1,9},{5,13},{9,1},{13,5},{2,10},{6,14},... | collective-permute-start | bytes 393224 | tf_op jit(solution)/shard_map/ppermute | solution.py:757
  79.0 1.2 %collective-permute-start.22 = (f32[264,128]{1,0:T(8,128)S(1)}, f32[264,128]{1,0:T(8,128)S(1)}, u32[]{:S(2)}, u32[]{:S(2)}) collective-permute-start(f32[264,128]{1,0:T(8,128)S(1)} %add_add_fusion), channel_id=1, source_target_pairs={{0,4},{4,0},{8,12},{12,8},{1,5},{5,1},{9,13},{13,9},{2,6},{6,2},{1... | collective-permute-start | bytes 405512 | tf_op jit(solution)/shard_map/ppermute | solution.py:757
  80.2 1.7 %collective-permute-done.20 = f32[264,128]{1,0:T(8,128)S(1)} collective-permute-done((f32[264,128]{1,0:T(8,128)S(1)}, f32[264,128]{1,0:T(8,128)S(1)}, u32[]{:S(2)}, u32[]{:S(2)}) %collective-permute-start.20) | collective-permute-done | bytes 135200 | tf_op jit(solution)/shard_map/ppermute | solution.py:757
  81.9 2.9 %collective-permute-done.18 = f32[264,128]{1,0:T(8,128)S(1)} collective-permute-done((f32[264,128]{1,0:T(8,128)S(1)}, f32[264,128]{1,0:T(8,128)S(1)}, u32[]{:S(2)}, u32[]{:S(2)}) %collective-permute-start.18) | collective-permute-done | bytes 135200 | tf_op jit(solution)/shard_map/ppermute | solution.py:757
  84.8 0.8 collective-permute-start.19
  85.6 1.4 %collective-permute-done.17 = f32[264,128]{1,0:T(8,128)S(1)} collective-permute-done((f32[264,128]{1,0:T(8,128)S(1)}, f32[264,128]{1,0:T(8,128)S(1)}, u32[]{:S(2)}, u32[]{:S(2)}) %collective-permute-start.17) | collective-permute-done | bytes 135200 | tf_op jit(solution)/shard_map/ppermute | solution.py:757
  87.8 3.3 %collective-permute-start.23 = (f32[264,128]{1,0:T(8,128)S(1)}, f32[264,128]{1,0:T(8,128)S(1)}, u32[]{:S(2)}, u32[]{:S(2)}) collective-permute-start(f32[264,128]{1,0:T(8,128)S(1)} %add_add_fusion.1), channel_id=1, source_target_pairs={{0,8},{4,12},{8,0},{12,4},{1,9},{5,13},{9,1},{13,5},{2,10},{6,14},... | collective-permute-start | bytes 405512 | tf_op jit(solution)/shard_map/ppermute | solution.py:757
  91.1 4.5 %collective-permute-done.26 = f32[256,128]{1,0:T(8,128)S(1)} collective-permute-done((f32[256,128]{1,0:T(8,128)S(1)}, f32[256,128]{1,0:T(8,128)S(1)}, u32[]{:S(2)}, u32[]{:S(2)}) %collective-permute-start.26) | collective-permute-done | bytes 131104 | tf_op jit(solution)/shard_map/ppermute | solution.py:757
  (64 shorter events, 13.0 us)
Async XLA Ops:
  2.3 10.8 %collective-permute-start.2 = (f32[264,128]{1,0:T(8,128)}, f32[264,128]{1,0:T(8,128)S(1)}, u32[]{:S(2)}, u32[]{:S(2)}) collective-permute-start(f32[264,128]{1,0:T(8,128)} %get-tuple-element.37.refs_0_), channel_id=1, source_target_pairs={{0,8},{4,12},{8,0},{12,4},{1,9},{5,13},{9,1},{13,5},{2,10},{6,14},... | collective-permute-start | bytes 405512 | tf_op jit(solution)/shard_map/ppermute | solution.py:757
  6.4 9.7 %collective-permute-start.1 = (f32[264,128]{1,0:T(8,128)}, f32[264,128]{1,0:T(8,128)S(1)}, u32[]{:S(2)}, u32[]{:S(2)}) collective-permute-start(f32[264,128]{1,0:T(8,128)} %get-tuple-element.37.refs_0_), channel_id=1, source_target_pairs={{0,4},{4,0},{8,12},{12,8},{1,5},{5,1},{9,13},{13,9},{2,6},{6,2},{1... | collective-permute-start | bytes 405512 | tf_op jit(solution)/shard_map/ppermute | solution.py:757
  7.9 8.2 %collective-permute-start = (f32[264,128]{1,0:T(8,128)}, f32[264,128]{1,0:T(8,128)S(1)}, u32[]{:S(2)}, u32[]{:S(2)}) collective-permute-start(f32[264,128]{1,0:T(8,128)} %get-tuple-element.37.refs_0_), channel_id=1, source_target_pairs={{0,2},{1,3},{2,0},{3,1},{4,6},{5,7},{6,4},{7,5},{8,10},{9,11},{10,... | collective-permute-start | bytes 405512 | tf_op jit(solution)/shard_map/ppermute | solution.py:757
  13.2 3.5 %collective-permute-start.9 = (f32[264,128]{1,0:T(8,128)S(1)}, f32[264,128]{1,0:T(8,128)S(1)}, u32[]{:S(2)}, u32[]{:S(2)}) collective-permute-start(f32[264,128]{1,0:T(8,128)S(1)} %collective-permute-done.2.refs_2_), channel_id=1, source_target_pairs={{0,1},{1,0},{2,3},{3,2},{4,5},{5,4},{6,7},{7,6},{8,9},{9,8},{10,11... | collective-permute-start | bytes 405512 | tf_op jit(solution)/shard_map/ppermute | solution.py:757
  13.2 6.0 %collective-permute-start.3 = (f32[264,128]{1,0:T(8,128)S(1)}, f32[264,128]{1,0:T(8,128)S(1)}, u32[]{:S(2)}, u32[]{:S(2)}) collective-permute-start(f32[264,128]{1,0:T(8,128)S(1)} %collective-permute-done.2.refs_2_), channel_id=1, source_target_pairs={{0,4},{4,0},{8,12},{12,8},{1,5},{5,1},{9,13},{13,9},{2,6},{6,2},{1... | collective-permute-start | bytes 405512 | tf_op jit(solution)/shard_map/ppermute | solution.py:757
  14.6 12.3 %collective-permute-start.5 = (f32[264,128]{1,0:T(8,128)S(1)}, f32[264,128]{1,0:T(8,128)S(1)}, u32[]{:S(2)}, u32[]{:S(2)}) collective-permute-start(f32[264,128]{1,0:T(8,128)S(1)} %collective-permute-done.2.refs_2_), channel_id=1, source_target_pairs={{0,2},{1,3},{2,0},{3,1},{4,6},{5,7},{6,4},{7,5},{8,10},{9,11},{10,... | collective-permute-start | bytes 405512 | tf_op jit(solution)/shard_map/ppermute | solution.py:757
  16.1 10.8 %collective-permute-start.8 = (f32[264,128]{1,0:T(8,128)S(1)}, f32[264,128]{1,0:T(8,128)S(1)}, u32[]{:S(2)}, u32[]{:S(2)}) collective-permute-start(f32[264,128]{1,0:T(8,128)S(1)} %collective-permute-done.1.refs_1_), channel_id=1, source_target_pairs={{0,1},{1,0},{2,3},{3,2},{4,5},{5,4},{6,7},{7,6},{8,9},{9,8},{10,11... | collective-permute-start | bytes 405512 | tf_op jit(solution)/shard_map/ppermute | solution.py:757
  16.1 11.3 %collective-permute-start.4 = (f32[264,128]{1,0:T(8,128)S(1)}, f32[264,128]{1,0:T(8,128)S(1)}, u32[]{:S(2)}, u32[]{:S(2)}) collective-permute-start(f32[264,128]{1,0:T(8,128)S(1)} %collective-permute-done.1.refs_1_), channel_id=1, source_target_pairs={{0,2},{1,3},{2,0},{3,1},{4,6},{5,7},{6,4},{7,5},{8,10},{9,11},{10,... | collective-permute-start | bytes 405512 | tf_op jit(solution)/shard_map/ppermute | solution.py:757
  16.7 10.8 %collective-permute-start.11 = (f32[264,128]{1,0:T(8,128)S(1)}, f32[264,128]{1,0:T(8,128)S(1)}, u32[]{:S(2)}, u32[]{:S(2)}) collective-permute-start(f32[264,128]{1,0:T(8,128)S(1)} %collective-permute-done.other_ref.refs_4_), channel_id=1, source_target_pairs={{0,1},{1,0},{2,3},{3,2},{4,5},{5,4},{6,7},{7,6},{8,9},{9,8},{10,11... | collective-permute-start | bytes 405512 | tf_op jit(solution)/shard_map/ppermute | solution.py:757
  19.2 8.8 %collective-permute-start.6 = (f32[264,128]{1,0:T(8,128)S(1)}, f32[264,128]{1,0:T(8,128)S(1)}, u32[]{:S(2)}, u32[]{:S(2)}) collective-permute-start(f32[264,128]{1,0:T(8,128)S(1)} %collective-permute-done.3.refs_3_), channel_id=1, source_target_pairs={{0,2},{1,3},{2,0},{3,1},{4,6},{5,7},{6,4},{7,5},{8,10},{9,11},{10,... | collective-permute-start | bytes 405512 | tf_op jit(solution)/shard_map/ppermute | solution.py:757
  26.9 1.6 %collective-permute-start.7 = (f32[264,128]{1,0:T(8,128)}, f32[264,128]{1,0:T(8,128)S(1)}, u32[]{:S(2)}, u32[]{:S(2)}) collective-permute-start(f32[264,128]{1,0:T(8,128)} %get-tuple-element.44), channel_id=1, source_target_pairs={{0,1},{1,0},{2,3},{3,2},{4,5},{5,4},{6,7},{7,6},{8,9},{9,8},{10,11... | collective-permute-start | bytes 405512 | tf_op jit(solution)/shard_map/ppermute | solution.py:757
  26.9 1.9 %collective-permute-start.10 = (f32[264,128]{1,0:T(8,128)S(1)}, f32[264,128]{1,0:T(8,128)S(1)}, u32[]{:S(2)}, u32[]{:S(2)}) collective-permute-start(f32[264,128]{1,0:T(8,128)S(1)} %collective-permute-done.3.refs_3_), channel_id=1, source_target_pairs={{0,1},{1,0},{2,3},{3,2},{4,5},{5,4},{6,7},{7,6},{8,9},{9,8},{10,11... | collective-permute-start | bytes 405512 | tf_op jit(solution)/shard_map/ppermute | solution.py:757
  67.4 2.2 %collective-permute-start.16 = (f32[5,264,128]{2,1,0:T(8,128)S(1)}, f32[5,264,128]{2,1,0:T(8,128)S(1)}, u32[]{:S(2)}, u32[]{:S(2)}) collective-permute-start(f32[5,264,128]{2,1,0:T(8,128)S(1)} %get-tuple-element.49), channel_id=1, source_target_pairs={{0,1},{1,0},{2,3},{3,2},{4,5},{5,4},{6,7},{7,6},{8,9},{9,8},{10,11... | collective-permute-start | bytes 2027528 | tf_op jit(solution)/shard_map/ppermute | solution.py:757
  67.6 6.1 %collective-permute-start.15 = (f32[5,264,128]{2,1,0:T(8,128)S(1)}, f32[5,264,128]{2,1,0:T(8,128)S(1)}, u32[]{:S(2)}, u32[]{:S(2)}) collective-permute-start(f32[5,264,128]{2,1,0:T(8,128)S(1)} %get-tuple-element.47), channel_id=1, source_target_pairs={{0,1},{1,0},{2,3},{3,2},{4,5},{5,4},{6,7},{7,6},{8,9},{9,8},{10,11... | collective-permute-start | bytes 2027528 | tf_op jit(solution)/shard_map/ppermute | solution.py:757
  69.6 6.5 %collective-permute-start.24 = (f32[264,128]{1,0:T(8,128)S(1)}, f32[264,128]{1,0:T(8,128)S(1)}, u32[]{:S(2)}, u32[]{:S(2)}) collective-permute-start(f32[264,128]{1,0:T(8,128)S(1)} %get-tuple-element.72), channel_id=1, source_target_pairs={{0,2},{1,3},{2,0},{3,1},{4,6},{5,7},{6,4},{7,5},{8,10},{9,11},{10,... | collective-permute-start | bytes 405512 | tf_op jit(solution)/shard_map/ppermute | solution.py:757
  70.2 8.8 %collective-permute-start.21 = (f32[264,128]{1,0:T(8,128)S(1)}, f32[264,128]{1,0:T(8,128)S(1)}, u32[]{:S(2)}, u32[]{:S(2)}) collective-permute-start(f32[264,128]{1,0:T(8,128)S(1)} %get-tuple-element.73), channel_id=1, source_target_pairs={{0,2},{1,3},{2,0},{3,1},{4,6},{5,7},{6,4},{7,5},{8,10},{9,11},{10,... | collective-permute-start | bytes 405512 | tf_op jit(solution)/shard_map/ppermute | solution.py:757
  71.7 10.2 %collective-permute-start.20 = (f32[264,128]{1,0:T(8,128)S(1)}, f32[264,128]{1,0:T(8,128)S(1)}, u32[]{:S(2)}, u32[]{:S(2)}) collective-permute-start(f32[264,128]{1,0:T(8,128)S(1)} %get-tuple-element.74), channel_id=1, source_target_pairs={{0,2},{1,3},{2,0},{3,1},{4,6},{5,7},{6,4},{7,5},{8,10},{9,11},{10,... | collective-permute-start | bytes 405512 | tf_op jit(solution)/shard_map/ppermute | solution.py:757
  72.2 12.6 %collective-permute-start.18 = (f32[264,128]{1,0:T(8,128)S(1)}, f32[264,128]{1,0:T(8,128)S(1)}, u32[]{:S(2)}, u32[]{:S(2)}) collective-permute-start(f32[264,128]{1,0:T(8,128)S(1)} %get-tuple-element.75), channel_id=1, source_target_pairs={{0,2},{1,3},{2,0},{3,1},{4,6},{5,7},{6,4},{7,5},{8,10},{9,11},{10,... | collective-permute-start | bytes 405512 | tf_op jit(solution)/shard_map/ppermute | solution.py:757
  73.7 13.2 %collective-permute-start.17 = (f32[264,128]{1,0:T(8,128)S(1)}, f32[264,128]{1,0:T(8,128)S(1)}, u32[]{:S(2)}, u32[]{:S(2)}) collective-permute-start(f32[264,128]{1,0:T(8,128)S(1)} %get-tuple-element.76), channel_id=1, source_target_pairs={{0,2},{1,3},{2,0},{3,1},{4,6},{5,7},{6,4},{7,5},{8,10},{9,11},{10,... | collective-permute-start | bytes 405512 | tf_op jit(solution)/shard_map/ppermute | solution.py:757
  76.1 10.9 %collective-permute-start.25 = (f32[256,128]{1,0:T(8,128)S(1)}, f32[256,128]{1,0:T(8,128)S(1)}, u32[]{:S(2)}, u32[]{:S(2)}) collective-permute-start(f32[256,128]{1,0:T(8,128)S(1)} %slice_add_fusion.5), channel_id=1, source_target_pairs={{0,8},{4,12},{8,0},{12,4},{1,9},{5,13},{9,1},{13,5},{2,10},{6,14},... | collective-permute-start | bytes 393224 | tf_op jit(solution)/shard_map/ppermute | solution.py:757
  79.0 8.7 %collective-permute-start.22 = (f32[264,128]{1,0:T(8,128)S(1)}, f32[264,128]{1,0:T(8,128)S(1)}, u32[]{:S(2)}, u32[]{:S(2)}) collective-permute-start(f32[264,128]{1,0:T(8,128)S(1)} %add_add_fusion), channel_id=1, source_target_pairs={{0,4},{4,0},{8,12},{12,8},{1,5},{5,1},{9,13},{13,9},{2,6},{6,2},{1... | collective-permute-start | bytes 405512 | tf_op jit(solution)/shard_map/ppermute | solution.py:757
  84.8 11.5 %collective-permute-start.19 = (f32[264,128]{1,0:T(8,128)S(1)}, f32[264,128]{1,0:T(8,128)S(1)}, u32[]{:S(2)}, u32[]{:S(2)}) collective-permute-start(f32[264,128]{1,0:T(8,128)S(1)} %add_add_fusion.3), channel_id=1, source_target_pairs={{0,4},{4,0},{8,12},{12,8},{1,5},{5,1},{9,13},{13,9},{2,6},{6,2},{1... | collective-permute-start | bytes 405512 | tf_op jit(solution)/shard_map/ppermute | solution.py:757
  87.0 8.6 %collective-permute-start.26 = (f32[256,128]{1,0:T(8,128)S(1)}, f32[256,128]{1,0:T(8,128)S(1)}, u32[]{:S(2)}, u32[]{:S(2)}) collective-permute-start(f32[256,128]{1,0:T(8,128)S(1)} %add.106), channel_id=1, source_target_pairs={{0,4},{4,0},{8,12},{12,8},{1,5},{5,1},{9,13},{13,9},{2,6},{6,2},{1... | collective-permute-start | bytes 393224 | tf_op jit(solution)/shard_map/ppermute | solution.py:757
  87.8 8.5 %collective-permute-start.23 = (f32[264,128]{1,0:T(8,128)S(1)}, f32[264,128]{1,0:T(8,128)S(1)}, u32[]{:S(2)}, u32[]{:S(2)}) collective-permute-start(f32[264,128]{1,0:T(8,128)S(1)} %add_add_fusion.1), channel_id=1, source_target_pairs={{0,8},{4,12},{8,0},{12,4},{1,9},{5,13},{9,1},{13,5},{2,10},{6,14},... | collective-permute-start | bytes 405512 | tf_op jit(solution)/shard_map/ppermute | solution.py:757
  (11 other events, 25.1 us)

commit v6 on v5

--- a/solution.py
+++ b/solution.py
@@ -845,17 +845,19 @@
         bit //= 2
     prior = (prior / num_cell).reshape(2, 128, 128)
     bit = 1
-    while bit < num_cell:
+    while 2 * bit < num_cell:
         for s in reversed(range(bit, num_cell, 2 * bit)):
             pieces[s - bit] = pieces[s - bit] + flip(pieces[s], bit, "cell")
         bit *= 2
-    own_sum = pieces[0]
+    last = flip(pieces[bit], bit, "cell")
+    layers = pieces[0][0:HEAD_ROW] + last[0:HEAD_ROW]
+    tail = pieces[0][HEAD_ROW:] + last[HEAD_ROW:]
     return (
         rendered,
-        own_sum[0:HEAD_ROW].reshape(1, 2, 128, 128),
+        layers.reshape(1, 2, 128, 128),
         prior[None],
-        own_sum[None, HEAD_ROW : HEAD_ROW + 4],
-        own_sum[None, APP_ROW : APP_ROW + 3, 0:width],
+        tail[None, 0:4],
+        tail[None, APP_ROW - HEAD_ROW : APP_ROW - HEAD_ROW + 3, 0:width],
         codes_grad.T,
     )
 

time: 98.5 us -> 98.5 us (level)
  no operation moved by 1% of the time
where the time goes in v6:
time: 98.5 us; the launch traced here: 98.1 us
  Pallas kernels  41.9 us (43%)
  starting transfers between devices  26.2 us (27%)
  waiting for transfers between devices  21.7 us (22%)
  local copies, waits for them, and re-layouts  5.25 us (5%)
  other arithmetic  2.3 us (2%)
    pallas_call x1, Pallas kernels, resident(): pl.pallas_call(functools.partial(step_kernel, cells, samples), in_specs=[...  38 us
    ppermute x27, starting transfers between devices, flip(): lax.ppermute(x, axis, [(i, i ^ bits) for i in range(lax.axis_size(axis))])  26.2 us
    ppermute x27, waiting for transfers between devices, flip(): lax.ppermute(x, axis, [(i, i ^ bits) for i in range(lax.axis_size(axis))])  21.7 us
    unnamed x17, local copies, waits for them, and re-layouts  4.58 us
    pallas_call x1, Pallas kernels, resident(): pl.pallas_call(functools.partial(deal_kernel, cells, samples), in_specs=[...  2.17 us
  transfers between devices with their start and end apart: 27, of which 13 were waited for; matrix products, arithmetic and copies ran while one was open for 2% of the time, Pallas kernels for 2%

profile of v6, /device:TPU:0, one launch (start us, length us, event | category | flops | bytes accessed | tf_op | source)
XLA Modules:
  0.0 98.1 jit_solution(5226938025350056864)
XLA Ops:
  0.6 1.7 %pack.1 = (f32[264,128]{1,0:T(8,128)}, f32[264,128]{1,0:T(8,128)}) custom-call(bf16[1,2,128,128]{3,2,1,0:T(8,128)(2,1)} %layers_ref.1, bf16[1,2,128,128]{3,2,1,0:T(8,128)(2,1)} %prior_ref.1, bf16[1,4,128]{2,1,0:T(4,128)(2,1)} %head_ref.1, f32[3,1,48]{2,1,0:T(1,128)} %bitcast.46), custom_call_target="tpu_custom_call" | custom-call | tf_op jit(solution)/shard_map/pack/pallas_call | solution.py:759
  2.3 4.0 %collective-permute-start.2 = (f32[264,128]{1,0:T(8,128)}, f32[264,128]{1,0:T(8,128)S(1)}, u32[]{:S(2)}, u32[]{:S(2)}) collective-permute-start(f32[264,128]{1,0:T(8,128)} %get-tuple-element.37.refs_0_), channel_id=1, source_target_pairs={{0,8},{4,12},{8,0},{12,4},{1,9},{5,13},{9,1},{13,5},{2,10},{6,14},... | collective-permute-start | bytes 405512 | tf_op jit(solution)/shard_map/ppermute | solution.py:757
  6.4 1.6 %collective-permute-start.1 = (f32[264,128]{1,0:T(8,128)}, f32[264,128]{1,0:T(8,128)S(1)}, u32[]{:S(2)}, u32[]{:S(2)}) collective-permute-start(f32[264,128]{1,0:T(8,128)} %get-tuple-element.37.refs_0_), channel_id=1, source_target_pairs={{0,4},{4,0},{8,12},{12,8},{1,5},{5,1},{9,13},{13,9},{2,6},{6,2},{1... | collective-permute-start | bytes 405512 | tf_op jit(solution)/shard_map/ppermute | solution.py:757
  7.9 1.5 %collective-permute-start = (f32[264,128]{1,0:T(8,128)}, f32[264,128]{1,0:T(8,128)S(1)}, u32[]{:S(2)}, u32[]{:S(2)}) collective-permute-start(f32[264,128]{1,0:T(8,128)} %get-tuple-element.37.refs_0_), channel_id=1, source_target_pairs={{0,2},{1,3},{2,0},{3,1},{4,6},{5,7},{6,4},{7,5},{8,10},{9,11},{10,... | collective-permute-start | bytes 405512 | tf_op jit(solution)/shard_map/ppermute | solution.py:757
  9.4 3.7 %collective-permute-done.2.refs_2_ = f32[264,128]{1,0:T(8,128)S(1)} collective-permute-done((f32[264,128]{1,0:T(8,128)}, f32[264,128]{1,0:T(8,128)S(1)}, u32[]{:S(2)}, u32[]{:S(2)}) %collective-permute-start.2) | collective-permute-done | bytes 135200 | tf_op jit(solution)/shard_map/ppermute | solution.py:757
  14.6 1.5 %collective-permute-start.5 = (f32[264,128]{1,0:T(8,128)S(1)}, f32[264,128]{1,0:T(8,128)S(1)}, u32[]{:S(2)}, u32[]{:S(2)}) collective-permute-start(f32[264,128]{1,0:T(8,128)S(1)} %collective-permute-done.2.refs_2_), channel_id=1, source_target_pairs={{0,2},{1,3},{2,0},{3,1},{4,6},{5,7},{6,4},{7,5},{8,10},{9,11},{10,... | collective-permute-start | bytes 405512 | tf_op jit(solution)/shard_map/ppermute | solution.py:757
  16.9 2.3 %collective-permute-done.3.refs_3_ = f32[264,128]{1,0:T(8,128)S(1)} collective-permute-done((f32[264,128]{1,0:T(8,128)S(1)}, f32[264,128]{1,0:T(8,128)S(1)}, u32[]{:S(2)}, u32[]{:S(2)}) %collective-permute-start.3) | collective-permute-done | bytes 135200 | tf_op jit(solution)/shard_map/ppermute | solution.py:757
  19.2 1.5 %collective-permute-start.6 = (f32[264,128]{1,0:T(8,128)S(1)}, f32[264,128]{1,0:T(8,128)S(1)}, u32[]{:S(2)}, u32[]{:S(2)}) collective-permute-start(f32[264,128]{1,0:T(8,128)S(1)} %collective-permute-done.3.refs_3_), channel_id=1, source_target_pairs={{0,2},{1,3},{2,0},{3,1},{4,6},{5,7},{6,4},{7,5},{8,10},{9,11},{10,... | collective-permute-start | bytes 405512 | tf_op jit(solution)/shard_map/ppermute | solution.py:757
  20.7 0.9 copy-done.4
  23.7 2.2 %deal.1 = (f32[8,1024]{1,0:T(8,128)S(1)}, f32[144,256]{1,0:T(8,128)S(1)}, s32[8,256]{1,0:T(8,128)S(1)}, s32[24,128]{1,0:T(8,128)S(1)}, f32[2,1152,128]{2,1,0:T(8...) custom-call(s32[4,256]{1,0:T(4,128)S(1)} %add_bitcast_fusion.cells_ref, ...), custom_call_target="tpu_custom_call", output_to_operand_aliasing={{6}: (5, {})} | custom-call | flops 6442450944 | bytes 4194304 | tf_op jit(solution)/shard_map/deal/pallas_call | solution.py:772
  25.9 1.0 %copy-done = f32[2,1152,128]{2,1,0:T(8,128)} copy-done((f32[2,1152,128]{2,1,0:T(8,128)}, f32[2,1152,128]{2,1,0:T(8,128)S(1)}, u32[]{:S(2)}) %copy-start) | copy-done | bytes 1179672
  29.3 38.0 %step.1 = (f32[3,256]{1,0:T(4,128)}, f32[48,256]{1,0:T(8,128)}, f32[5,264,128]{2,1,0:T(8,128)S(1)}, f32[5,264,128]{2,1,0:T(8,128)S(1)}, f32[5,264,128]{2,1,0:T(8,128)S(1)}, /*index=5*/f32[5,264,128]{2,1,0:T(8,128)S(1)}) custom-call(s32[8,256]{1,0:T(8,128)S(1)} %get-tuple-element.38.tile_cell_ref, s32[24,128]{1,0:T(8,128)S(1)} %get-tuple-element.39.tile_start_ref, ...), custom_call_target="tpu_custom_call" | custom-call | tf_op jit(solution)/shard_map/step/pallas_call | solution.py:797
  68.0 1.6 %collective-permute-done.16 = f32[5,264,128]{2,1,0:T(8,128)S(1)} collective-permute-done((f32[5,264,128]{2,1,0:T(8,128)S(1)}, f32[5,264,128]{2,1,0:T(8,128)S(1)}, u32[]{:S(2)}, u32[]{:S(2)}) %collective-permute-start.16) | collective-permute-done | bytes 675872 | tf_op jit(solution)/shard_map/ppermute | solution.py:757
  70.2 1.5 %collective-permute-start.21 = (f32[264,128]{1,0:T(8,128)S(1)}, f32[264,128]{1,0:T(8,128)S(1)}, u32[]{:S(2)}, u32[]{:S(2)}) collective-permute-start(f32[264,128]{1,0:T(8,128)S(1)} %get-tuple-element.73), channel_id=1, source_target_pairs={{0,2},{1,3},{2,0},{3,1},{4,6},{5,7},{6,4},{7,5},{8,10},{9,11},{10,... | collective-permute-start | bytes 405512 | tf_op jit(solution)/shard_map/ppermute | solution.py:757
  72.2 1.5 %collective-permute-start.18 = (f32[264,128]{1,0:T(8,128)S(1)}, f32[264,128]{1,0:T(8,128)S(1)}, u32[]{:S(2)}, u32[]{:S(2)}) collective-permute-start(f32[264,128]{1,0:T(8,128)S(1)} %get-tuple-element.75), channel_id=1, source_target_pairs={{0,2},{1,3},{2,0},{3,1},{4,6},{5,7},{6,4},{7,5},{8,10},{9,11},{10,... | collective-permute-start | bytes 405512 | tf_op jit(solution)/shard_map/ppermute | solution.py:757
  74.3 1.8 %collective-permute-done.24 = f32[264,128]{1,0:T(8,128)S(1)} collective-permute-done((f32[264,128]{1,0:T(8,128)S(1)}, f32[264,128]{1,0:T(8,128)S(1)}, u32[]{:S(2)}, u32[]{:S(2)}) %collective-permute-start.24) | collective-permute-done | bytes 135200 | tf_op jit(solution)/shard_map/ppermute | solution.py:757
  76.1 2.3 %collective-permute-start.25 = (f32[256,128]{1,0:T(8,128)S(1)}, f32[256,128]{1,0:T(8,128)S(1)}, u32[]{:S(2)}, u32[]{:S(2)}) collective-permute-start(f32[256,128]{1,0:T(8,128)S(1)} %slice_add_fusion.5), channel_id=1, source_target_pairs={{0,8},{4,12},{8,0},{12,4},{1,9},{5,13},{9,1},{13,5},{2,10},{6,14},... | collective-permute-start | bytes 393224 | tf_op jit(solution)/shard_map/ppermute | solution.py:757
  79.0 1.2 %collective-permute-start.22 = (f32[264,128]{1,0:T(8,128)S(1)}, f32[264,128]{1,0:T(8,128)S(1)}, u32[]{:S(2)}, u32[]{:S(2)}) collective-permute-start(f32[264,128]{1,0:T(8,128)S(1)} %add_add_fusion), channel_id=1, source_target_pairs={{0,4},{4,0},{8,12},{12,8},{1,5},{5,1},{9,13},{13,9},{2,6},{6,2},{1... | collective-permute-start | bytes 405512 | tf_op jit(solution)/shard_map/ppermute | solution.py:757
  80.3 1.6 %collective-permute-done.20 = f32[264,128]{1,0:T(8,128)S(1)} collective-permute-done((f32[264,128]{1,0:T(8,128)S(1)}, f32[264,128]{1,0:T(8,128)S(1)}, u32[]{:S(2)}, u32[]{:S(2)}) %collective-permute-start.20) | collective-permute-done | bytes 135200 | tf_op jit(solution)/shard_map/ppermute | solution.py:757
  81.9 2.9 %collective-permute-done.18 = f32[264,128]{1,0:T(8,128)S(1)} collective-permute-done((f32[264,128]{1,0:T(8,128)S(1)}, f32[264,128]{1,0:T(8,128)S(1)}, u32[]{:S(2)}, u32[]{:S(2)}) %collective-permute-start.18) | collective-permute-done | bytes 135200 | tf_op jit(solution)/shard_map/ppermute | solution.py:757
  85.6 1.4 %collective-permute-done.17 = f32[264,128]{1,0:T(8,128)S(1)} collective-permute-done((f32[264,128]{1,0:T(8,128)S(1)}, f32[264,128]{1,0:T(8,128)S(1)}, u32[]{:S(2)}, u32[]{:S(2)}) %collective-permute-start.17) | collective-permute-done | bytes 135200 | tf_op jit(solution)/shard_map/ppermute | solution.py:757
  87.0 0.8 collective-permute-start.26
  87.8 3.3 %collective-permute-start.23 = (f32[264,128]{1,0:T(8,128)S(1)}, f32[264,128]{1,0:T(8,128)S(1)}, u32[]{:S(2)}, u32[]{:S(2)}) collective-permute-start(f32[264,128]{1,0:T(8,128)S(1)} %add_add_fusion.1), channel_id=1, source_target_pairs={{0,8},{4,12},{8,0},{12,4},{1,9},{5,13},{9,1},{13,5},{2,10},{6,14},... | collective-permute-start | bytes 405512 | tf_op jit(solution)/shard_map/ppermute | solution.py:757
  91.1 4.5 %collective-permute-done.26 = f32[256,128]{1,0:T(8,128)S(1)} collective-permute-done((f32[256,128]{1,0:T(8,128)S(1)}, f32[256,128]{1,0:T(8,128)S(1)}, u32[]{:S(2)}, u32[]{:S(2)}) %collective-permute-start.26) | collective-permute-done | bytes 131104 | tf_op jit(solution)/shard_map/ppermute | solution.py:757
  (65 shorter events, 13.0 us)
Async XLA Ops:
  2.3 10.8 %collective-permute-start.2 = (f32[264,128]{1,0:T(8,128)}, f32[264,128]{1,0:T(8,128)S(1)}, u32[]{:S(2)}, u32[]{:S(2)}) collective-permute-start(f32[264,128]{1,0:T(8,128)} %get-tuple-element.37.refs_0_), channel_id=1, source_target_pairs={{0,8},{4,12},{8,0},{12,4},{1,9},{5,13},{9,1},{13,5},{2,10},{6,14},... | collective-permute-start | bytes 405512 | tf_op jit(solution)/shard_map/ppermute | solution.py:757
  6.4 9.7 %collective-permute-start.1 = (f32[264,128]{1,0:T(8,128)}, f32[264,128]{1,0:T(8,128)S(1)}, u32[]{:S(2)}, u32[]{:S(2)}) collective-permute-start(f32[264,128]{1,0:T(8,128)} %get-tuple-element.37.refs_0_), channel_id=1, source_target_pairs={{0,4},{4,0},{8,12},{12,8},{1,5},{5,1},{9,13},{13,9},{2,6},{6,2},{1... | collective-permute-start | bytes 405512 | tf_op jit(solution)/shard_map/ppermute | solution.py:757
  7.9 8.2 %collective-permute-start = (f32[264,128]{1,0:T(8,128)}, f32[264,128]{1,0:T(8,128)S(1)}, u32[]{:S(2)}, u32[]{:S(2)}) collective-permute-start(f32[264,128]{1,0:T(8,128)} %get-tuple-element.37.refs_0_), channel_id=1, source_target_pairs={{0,2},{1,3},{2,0},{3,1},{4,6},{5,7},{6,4},{7,5},{8,10},{9,11},{10,... | collective-permute-start | bytes 405512 | tf_op jit(solution)/shard_map/ppermute | solution.py:757
  13.2 3.5 %collective-permute-start.9 = (f32[264,128]{1,0:T(8,128)S(1)}, f32[264,128]{1,0:T(8,128)S(1)}, u32[]{:S(2)}, u32[]{:S(2)}) collective-permute-start(f32[264,128]{1,0:T(8,128)S(1)} %collective-permute-done.2.refs_2_), channel_id=1, source_target_pairs={{0,1},{1,0},{2,3},{3,2},{4,5},{5,4},{6,7},{7,6},{8,9},{9,8},{10,11... | collective-permute-start | bytes 405512 | tf_op jit(solution)/shard_map/ppermute | solution.py:757
  13.2 6.0 %collective-permute-start.3 = (f32[264,128]{1,0:T(8,128)S(1)}, f32[264,128]{1,0:T(8,128)S(1)}, u32[]{:S(2)}, u32[]{:S(2)}) collective-permute-start(f32[264,128]{1,0:T(8,128)S(1)} %collective-permute-done.2.refs_2_), channel_id=1, source_target_pairs={{0,4},{4,0},{8,12},{12,8},{1,5},{5,1},{9,13},{13,9},{2,6},{6,2},{1... | collective-permute-start | bytes 405512 | tf_op jit(solution)/shard_map/ppermute | solution.py:757
  14.6 12.3 %collective-permute-start.5 = (f32[264,128]{1,0:T(8,128)S(1)}, f32[264,128]{1,0:T(8,128)S(1)}, u32[]{:S(2)}, u32[]{:S(2)}) collective-permute-start(f32[264,128]{1,0:T(8,128)S(1)} %collective-permute-done.2.refs_2_), channel_id=1, source_target_pairs={{0,2},{1,3},{2,0},{3,1},{4,6},{5,7},{6,4},{7,5},{8,10},{9,11},{10,... | collective-permute-start | bytes 405512 | tf_op jit(solution)/shard_map/ppermute | solution.py:757
  16.1 10.8 %collective-permute-start.8 = (f32[264,128]{1,0:T(8,128)S(1)}, f32[264,128]{1,0:T(8,128)S(1)}, u32[]{:S(2)}, u32[]{:S(2)}) collective-permute-start(f32[264,128]{1,0:T(8,128)S(1)} %collective-permute-done.1.refs_1_), channel_id=1, source_target_pairs={{0,1},{1,0},{2,3},{3,2},{4,5},{5,4},{6,7},{7,6},{8,9},{9,8},{10,11... | collective-permute-start | bytes 405512 | tf_op jit(solution)/shard_map/ppermute | solution.py:757
  16.1 11.3 %collective-permute-start.4 = (f32[264,128]{1,0:T(8,128)S(1)}, f32[264,128]{1,0:T(8,128)S(1)}, u32[]{:S(2)}, u32[]{:S(2)}) collective-permute-start(f32[264,128]{1,0:T(8,128)S(1)} %collective-permute-done.1.refs_1_), channel_id=1, source_target_pairs={{0,2},{1,3},{2,0},{3,1},{4,6},{5,7},{6,4},{7,5},{8,10},{9,11},{10,... | collective-permute-start | bytes 405512 | tf_op jit(solution)/shard_map/ppermute | solution.py:757
  16.7 10.8 %collective-permute-start.11 = (f32[264,128]{1,0:T(8,128)S(1)}, f32[264,128]{1,0:T(8,128)S(1)}, u32[]{:S(2)}, u32[]{:S(2)}) collective-permute-start(f32[264,128]{1,0:T(8,128)S(1)} %collective-permute-done.other_ref.refs_4_), channel_id=1, source_target_pairs={{0,1},{1,0},{2,3},{3,2},{4,5},{5,4},{6,7},{7,6},{8,9},{9,8},{10,11... | collective-permute-start | bytes 405512 | tf_op jit(solution)/shard_map/ppermute | solution.py:757
  19.2 8.8 %collective-permute-start.6 = (f32[264,128]{1,0:T(8,128)S(1)}, f32[264,128]{1,0:T(8,128)S(1)}, u32[]{:S(2)}, u32[]{:S(2)}) collective-permute-start(f32[264,128]{1,0:T(8,128)S(1)} %collective-permute-done.3.refs_3_), channel_id=1, source_target_pairs={{0,2},{1,3},{2,0},{3,1},{4,6},{5,7},{6,4},{7,5},{8,10},{9,11},{10,... | collective-permute-start | bytes 405512 | tf_op jit(solution)/shard_map/ppermute | solution.py:757
  26.9 1.6 %collective-permute-start.7 = (f32[264,128]{1,0:T(8,128)}, f32[264,128]{1,0:T(8,128)S(1)}, u32[]{:S(2)}, u32[]{:S(2)}) collective-permute-start(f32[264,128]{1,0:T(8,128)} %get-tuple-element.44), channel_id=1, source_target_pairs={{0,1},{1,0},{2,3},{3,2},{4,5},{5,4},{6,7},{7,6},{8,9},{9,8},{10,11... | collective-permute-start | bytes 405512 | tf_op jit(solution)/shard_map/ppermute | solution.py:757
  26.9 1.9 %collective-permute-start.10 = (f32[264,128]{1,0:T(8,128)S(1)}, f32[264,128]{1,0:T(8,128)S(1)}, u32[]{:S(2)}, u32[]{:S(2)}) collective-permute-start(f32[264,128]{1,0:T(8,128)S(1)} %collective-permute-done.3.refs_3_), channel_id=1, source_target_pairs={{0,1},{1,0},{2,3},{3,2},{4,5},{5,4},{6,7},{7,6},{8,9},{9,8},{10,11... | collective-permute-start | bytes 405512 | tf_op jit(solution)/shard_map/ppermute | solution.py:757
  67.4 2.2 %collective-permute-start.16 = (f32[5,264,128]{2,1,0:T(8,128)S(1)}, f32[5,264,128]{2,1,0:T(8,128)S(1)}, u32[]{:S(2)}, u32[]{:S(2)}) collective-permute-start(f32[5,264,128]{2,1,0:T(8,128)S(1)} %get-tuple-element.49), channel_id=1, source_target_pairs={{0,1},{1,0},{2,3},{3,2},{4,5},{5,4},{6,7},{7,6},{8,9},{9,8},{10,11... | collective-permute-start | bytes 2027528 | tf_op jit(solution)/shard_map/ppermute | solution.py:757
  67.6 6.1 %collective-permute-start.15 = (f32[5,264,128]{2,1,0:T(8,128)S(1)}, f32[5,264,128]{2,1,0:T(8,128)S(1)}, u32[]{:S(2)}, u32[]{:S(2)}) collective-permute-start(f32[5,264,128]{2,1,0:T(8,128)S(1)} %get-tuple-element.47), channel_id=1, source_target_pairs={{0,1},{1,0},{2,3},{3,2},{4,5},{5,4},{6,7},{7,6},{8,9},{9,8},{10,11... | collective-permute-start | bytes 2027528 | tf_op jit(solution)/shard_map/ppermute | solution.py:757
  69.6 6.5 %collective-permute-start.24 = (f32[264,128]{1,0:T(8,128)S(1)}, f32[264,128]{1,0:T(8,128)S(1)}, u32[]{:S(2)}, u32[]{:S(2)}) collective-permute-start(f32[264,128]{1,0:T(8,128)S(1)} %get-tuple-element.72), channel_id=1, source_target_pairs={{0,2},{1,3},{2,0},{3,1},{4,6},{5,7},{6,4},{7,5},{8,10},{9,11},{10,... | collective-permute-start | bytes 405512 | tf_op jit(solution)/shard_map/ppermute | solution.py:757
  70.2 8.8 %collective-permute-start.21 = (f32[264,128]{1,0:T(8,128)S(1)}, f32[264,128]{1,0:T(8,128)S(1)}, u32[]{:S(2)}, u32[]{:S(2)}) collective-permute-start(f32[264,128]{1,0:T(8,128)S(1)} %get-tuple-element.73), channel_id=1, source_target_pairs={{0,2},{1,3},{2,0},{3,1},{4,6},{5,7},{6,4},{7,5},{8,10},{9,11},{10,... | collective-permute-start | bytes 405512 | tf_op jit(solution)/shard_map/ppermute | solution.py:757
  71.7 10.2 %collective-permute-start.20 = (f32[264,128]{1,0:T(8,128)S(1)}, f32[264,128]{1,0:T(8,128)S(1)}, u32[]{:S(2)}, u32[]{:S(2)}) collective-permute-start(f32[264,128]{1,0:T(8,128)S(1)} %get-tuple-element.74), channel_id=1, source_target_pairs={{0,2},{1,3},{2,0},{3,1},{4,6},{5,7},{6,4},{7,5},{8,10},{9,11},{10,... | collective-permute-start | bytes 405512 | tf_op jit(solution)/shard_map/ppermute | solution.py:757
  72.2 12.6 %collective-permute-start.18 = (f32[264,128]{1,0:T(8,128)S(1)}, f32[264,128]{1,0:T(8,128)S(1)}, u32[]{:S(2)}, u32[]{:S(2)}) collective-permute-start(f32[264,128]{1,0:T(8,128)S(1)} %get-tuple-element.75), channel_id=1, source_target_pairs={{0,2},{1,3},{2,0},{3,1},{4,6},{5,7},{6,4},{7,5},{8,10},{9,11},{10,... | collective-permute-start | bytes 405512 | tf_op jit(solution)/shard_map/ppermute | solution.py:757
  73.7 13.2 %collective-permute-start.17 = (f32[264,128]{1,0:T(8,128)S(1)}, f32[264,128]{1,0:T(8,128)S(1)}, u32[]{:S(2)}, u32[]{:S(2)}) collective-permute-start(f32[264,128]{1,0:T(8,128)S(1)} %get-tuple-element.76), channel_id=1, source_target_pairs={{0,2},{1,3},{2,0},{3,1},{4,6},{5,7},{6,4},{7,5},{8,10},{9,11},{10,... | collective-permute-start | bytes 405512 | tf_op jit(solution)/shard_map/ppermute | solution.py:757
  76.1 10.8 %collective-permute-start.25 = (f32[256,128]{1,0:T(8,128)S(1)}, f32[256,128]{1,0:T(8,128)S(1)}, u32[]{:S(2)}, u32[]{:S(2)}) collective-permute-start(f32[256,128]{1,0:T(8,128)S(1)} %slice_add_fusion.5), channel_id=1, source_target_pairs={{0,8},{4,12},{8,0},{12,4},{1,9},{5,13},{9,1},{13,5},{2,10},{6,14},... | collective-permute-start | bytes 393224 | tf_op jit(solution)/shard_map/ppermute | solution.py:757
  79.0 8.7 %collective-permute-start.22 = (f32[264,128]{1,0:T(8,128)S(1)}, f32[264,128]{1,0:T(8,128)S(1)}, u32[]{:S(2)}, u32[]{:S(2)}) collective-permute-start(f32[264,128]{1,0:T(8,128)S(1)} %add_add_fusion), channel_id=1, source_target_pairs={{0,4},{4,0},{8,12},{12,8},{1,5},{5,1},{9,13},{13,9},{2,6},{6,2},{1... | collective-permute-start | bytes 405512 | tf_op jit(solution)/shard_map/ppermute | solution.py:757
  84.8 6.3 %collective-permute-start.19 = (f32[264,128]{1,0:T(8,128)S(1)}, f32[264,128]{1,0:T(8,128)S(1)}, u32[]{:S(2)}, u32[]{:S(2)}) collective-permute-start(f32[264,128]{1,0:T(8,128)S(1)} %add_add_fusion.2), channel_id=1, source_target_pairs={{0,4},{4,0},{8,12},{12,8},{1,5},{5,1},{9,13},{13,9},{2,6},{6,2},{1... | collective-permute-start | bytes 405512 | tf_op jit(solution)/shard_map/ppermute | solution.py:757
  87.0 8.6 %collective-permute-start.26 = (f32[256,128]{1,0:T(8,128)S(1)}, f32[256,128]{1,0:T(8,128)S(1)}, u32[]{:S(2)}, u32[]{:S(2)}) collective-permute-start(f32[256,128]{1,0:T(8,128)S(1)} %add.109), channel_id=1, source_target_pairs={{0,4},{4,0},{8,12},{12,8},{1,5},{5,1},{9,13},{13,9},{2,6},{6,2},{1... | collective-permute-start | bytes 393224 | tf_op jit(solution)/shard_map/ppermute | solution.py:757
  87.8 8.5 %collective-permute-start.23 = (f32[264,128]{1,0:T(8,128)S(1)}, f32[264,128]{1,0:T(8,128)S(1)}, u32[]{:S(2)}, u32[]{:S(2)}) collective-permute-start(f32[264,128]{1,0:T(8,128)S(1)} %add_add_fusion.1), channel_id=1, source_target_pairs={{0,8},{4,12},{8,0},{12,4},{1,9},{5,13},{9,1},{13,5},{2,10},{6,14},... | collective-permute-start | bytes 405512 | tf_op jit(solution)/shard_map/ppermute | solution.py:757
  (11 other events, 25.1 us)
